TPU v7x, 128 devices: a whole 4x4x4 slice. The times are simulated.
128 devices in a mesh: tile: 2 (over x_hi), kern: 4 (over x_lo, core), noise: 16 (over y, z).
Axes of the slice: x: 4 (x_hi: 2, x_lo: 2; x = x_hi * 2 + x_lo), y: 4, z: 4, core: 2. Of those that a mesh axis runs over, the one named last changes fastest.
Arguments:
- mask_values: float32 [2048, 4096], P(('kern', 'noise'), 'tile'), may hold values from 0 to 1
- kernels: float32 [24, 2, 128, 128], P('kern'), may hold values from -6 to 6
- weights: float32 [24], P('kern'), may hold values from 0.02 to 0.5
- target: bfloat16 [2048, 4096], P(('kern', 'noise'), 'tile'), may hold values from 0 to 1
- dose_noise: bfloat16 [32, 2048, 4096], P('noise', 'kern', 'tile'), may hold values from -4 to 4
Outputs:
- mask_grad: float32 [2048, 4096], P(('kern', 'noise'), 'tile')
All inputs are finite; a program needn't handle non-finite values.
Results may differ from a plain program's by a relative error of at most 0.0019.
Values may be sent and summed in bfloat16 or wider, within the bound.
No kernel may reach another device: no remote copies, remote signals or barrier semaphores. Data moves between devices by JAX's collectives and lax.ppermute only.
A program may use at most 192 MiB of HBM per device.

v0:
```python
import jax
import jax.numpy as jnp
from jax import lax
from jax.sharding import PartitionSpec as P

HALO = 16


two_pi = 6.283185307179586
slope = 2.0
thresh = 2.0
dose_sigma = 0.25
penalty = 4.0


def padded_2(block, sides, width):
    for axis, dim in sides:
        count = lax.axis_size(axis)
        forward = [(i, i + 1) for i in range(count - 1)]
        backward = [(target, source) for source, target in forward]
        low = lax.ppermute(
            lax.slice_in_dim(block, block.shape[dim] - width, None, axis=dim), axis, forward
        )
        high = lax.ppermute(lax.slice_in_dim(block, 0, width, axis=dim), axis, backward)
        block = jnp.concatenate([low, block, high], axis=dim)
    return block


def matmul(left, right):
    return jnp.dot(left, right, precision=lax.Precision.HIGHEST, preferred_element_type=jnp.float32)


def wave_tables(row_ids, freq_count, period):
    centred = jnp.arange(freq_count, dtype=jnp.int32) - freq_count // 2
    wrapped = centred[:, None] * row_ids[None, :] % period
    angles = wrapped.astype(jnp.float32) * (two_pi / period)
    return (jnp.cos(angles), jnp.sin(angles))


def spectrum(transmit, row_cos, row_sin, col_cos, col_sin):
    period = transmit.shape[1]
    by_cos = matmul(transmit, col_cos.T)
    by_sin = matmul(transmit, col_sin.T)
    real_part = (matmul(row_cos, by_cos) - matmul(row_sin, by_sin)) / period
    imag_part = -(matmul(row_cos, by_sin) + matmul(row_sin, by_cos)) / period
    return jnp.stack([real_part, imag_part])


def kernel_intensity(spectral, kernel, weight, row_cos, row_sin, col_cos, col_sin):
    freq_count = spectral.shape[1]
    near_real = kernel[0] * spectral[0] - kernel[1] * spectral[1]
    near_imag = kernel[0] * spectral[1] + kernel[1] * spectral[0]
    left_real = matmul(row_cos.T, near_real) - matmul(row_sin.T, near_imag)
    left_imag = matmul(row_cos.T, near_imag) + matmul(row_sin.T, near_real)
    field_real = (matmul(left_real, col_cos) - matmul(left_imag, col_sin)) / freq_count
    field_imag = (matmul(left_real, col_sin) + matmul(left_imag, col_cos)) / freq_count
    return weight * (field_real * field_real + field_imag * field_imag)


def band_matrix(out_count, halo_width):
    offsets = jnp.arange(2 * halo_width + 1, dtype=jnp.int32) - halo_width
    deviation = halo_width / 2.0
    taps_sum = jnp.sum(jnp.exp(-offsets.astype(jnp.float32) ** 2 / (2.0 * deviation * deviation)))
    shift_ids = (
        jnp.arange(out_count + 2 * halo_width, dtype=jnp.int32)[None, :]
        - jnp.arange(out_count, dtype=jnp.int32)[:, None]
        - halo_width
    )
    values = jnp.exp(-shift_ids.astype(jnp.float32) ** 2 / (2.0 * deviation * deviation)) / taps_sum
    return jnp.where(jnp.abs(shift_ids) <= halo_width, values, 0.0)


def sample_terms(acid_rows, noise_rows):
    dose_factor = 1.0 + dose_sigma * noise_rows.astype(jnp.float32)
    response = jax.nn.sigmoid(slope * (acid_rows[None] * dose_factor - thresh))
    response_slope = slope * response * (1.0 - response) * dose_factor
    return (response, response_slope)


def body(mask_values, kernels, weights, target, dose_noise):
    block_rows, period = mask_values.shape
    freq_count = kernels.shape[2]
    kern_count = lax.axis_size("kern")
    noise_count = lax.axis_size("noise")
    kern_pos = lax.axis_index("kern")
    noise_pos = lax.axis_index("noise")
    sample_count = dose_noise.shape[0] * noise_count
    local_ids = jnp.arange(block_rows, dtype=jnp.int32)
    block_ids = (kern_pos * noise_count + noise_pos) * block_rows + local_ids
    group_ids = jnp.arange(kern_count, dtype=jnp.int32)[:, None] * noise_count + noise_pos
    slab_ids = (group_ids * block_rows + local_ids[None, :]).reshape(-1)
    col_cos, col_sin = wave_tables(jnp.arange(period, dtype=jnp.int32), freq_count, period)
    block_cos, block_sin = wave_tables(block_ids, freq_count, period)
    slab_cos, slab_sin = wave_tables(slab_ids, freq_count, period)

    def block_spectrum(values):
        return spectrum(values, block_cos, block_sin, col_cos, col_sin)

    transmit = 2.0 * mask_values - 1.0
    partial_spec, pull_mask = jax.vjp(block_spectrum, transmit)
    spectral = lax.psum(partial_spec, ("kern", "noise"))

    def slab_intensity(spectral_in):
        running = jnp.zeros((slab_ids.shape[0], period), jnp.float32)
        for which_kern in range(kernels.shape[0]):
            running = running + kernel_intensity(
                spectral_in,
                kernels[which_kern],
                weights[which_kern],
                slab_cos,
                slab_sin,
                col_cos,
                col_sin,
            )
        return running

    slab_part, pull_spec = jax.vjp(slab_intensity, spectral)
    intensity = lax.psum_scatter(slab_part, "kern", scatter_dimension=0, tiled=True)
    row_band = band_matrix(block_rows, HALO)
    col_band = band_matrix(period, HALO).T

    def diffuse(source):
        padded = padded_2(source, (("tile", 1), (("kern", "noise"), 0)), HALO)
        return matmul(matmul(row_band, padded), col_band)

    acid_block = diffuse(intensity)
    target_field = target.astype(jnp.float32)
    acid_rows = lax.all_gather(acid_block, "noise", axis=0, tiled=True)
    response, response_slope = sample_terms(acid_rows, dose_noise)
    mean_resp = lax.psum(jnp.sum(response, 0), "noise") / sample_count
    upper_sum = jnp.sum(
        response_slope * ((1.0 + penalty) * response - penalty * mean_resp[None]), 0
    )
    lower_sum = jnp.sum(response_slope, 0)
    upper_sum, lower_sum = (
        lax.psum_scatter(upper_sum, "noise", scatter_dimension=0, tiled=True),
        lax.psum_scatter(lower_sum, "noise", scatter_dimension=0, tiled=True),
    )
    acid_grad = 2.0 / sample_count * (upper_sum - target_field * lower_sum)
    intensity_grad = diffuse(acid_grad)
    slab_grad = lax.all_gather(
        intensity_grad.astype(jnp.bfloat16), "kern", axis=0, tiled=True
    ).astype(intensity_grad.dtype)
    spec_grad = lax.psum(pull_spec(slab_grad)[0], ("kern", "noise"))
    return 2.0 * pull_mask(spec_grad)[0]


def solution(mesh):
    return jax.shard_map(
        body,
        mesh=mesh,
        in_specs=(
            P(("kern", "noise"), "tile"),
            P("kern", None, None, None),
            P("kern"),
            P(("kern", "noise"), "tile"),
            P("noise", "kern", "tile"),
        ),
        out_specs=P(("kern", "noise"), "tile"),
        check_vma=False,
    )
```

profile of v0, /device:TPU:1, one launch (start us, length us, event | category | flops | bytes accessed | tf_op | source)
XLA Modules:
  0.0 1762.7 jit_solution(18392071325109907044)
XLA Ops:
  6.6 5.9 fusion.221
  12.5 4.9 fusion.187
  21.5 477.7 %all-reduce.28.cloned.1.call-done = f32[2,128,128]{2,1,0:T(8,128)} async-done(((f32[2,128,128]{2,1,0:T(8,128)}), f32[2,128,128]{2,1,0:T(8,128)}) %all-reduce.28.cloned.1.call-update) | async-done | bytes 131088 | tf_op jit(solution)/shard_map/psum | solution.py:101
  502.8 4.9 fusion.169
  507.7 4.9 fusion.219
  514.6 4.9 fusion.216
  519.5 4.9 fusion.184
  526.3 4.9 fusion.213
  537.8 5.3 fusion.210
  543.1 4.9 fusion.178
  549.7 5.1 fusion.207
  561.4 5.1 fusion.204
  574.9 5.3 fusion.12
  580.2 4.9 fusion.13
  585.2 5.0 fusion.10
  590.2 4.9 fusion.11
  595.1 4.9 fusion.8
  600.0 5.1 fusion.9
  605.1 4.9 fusion.6
  610.0 5.3 fusion.7
  615.4 4.9 fusion.4
  620.2 5.1 fusion.5
  625.4 4.9 fusion.3
  630.4 10.9 multiply_add_fusion.1
  641.3 25.1 %reduce-scatter.4.cloned.1.call-done = f32[32,2048]{1,0:T(8,128)} async-done(((f32[128,2048]{1,0:T(8,128)}), f32[32,2048]{1,0:T(8,128)}) %reduce-scatter.4.cloned.1.call-update) | async-done | bytes 262160 | tf_op jit(solution)/shard_map/reduce_scatter | solution.py:118
  668.5 5.5 collective-permute-start
  679.2 7.1 collective-permute-start.3
  689.1 24.6 %fusion.1 = f32[32,2048]{1,0:T(8,128)} fusion(f32[32,2080]{1,0:T(8,128)S(1)} %fusion.58, f32[]{:T(128)} %exponential_reduce_fusion), kind=kOutput, calls=%fused_computation.3 | convolution fusion | flops 1678376960 | bytes 528388 | tf_op jit(solution)/shard_map/dot_general | solution.py:30
  714.2 55.0 %all-gather.2.cloned.1.call-done = f32[512,2048]{1,0:T(8,128)} async-done(((f32[32,2048]{1,0:T(8,128)}), f32[512,2048]{1,0:T(8,128)}) %all-gather.2.cloned.1.call-update) | async-done | bytes 4194320 | tf_op jit(solution)/shard_map/all_gather | solution.py:128
  769.2 7.8 fusion.857
  777.1 103.0 %all-reduce.30.cloned.1.call-done = f32[512,2048]{1,0:T(8,128)} async-done(((f32[512,2048]{1,0:T(8,128)}), f32[512,2048]{1,0:T(8,128)}) %all-reduce.30.cloned.1.call-update) | async-done | bytes 4194320 | tf_op jit(solution)/shard_map/psum | solution.py:130
  884.8 9.8 fusion.2
  895.3 75.6 %reduce-scatter.8.cloned.1.call-done = f32[32,2048]{1,0:T(8,128)} async-done(((f32[512,2048]{1,0:T(8,128)}), f32[32,2048]{1,0:T(8,128)}) %reduce-scatter.8.cloned.1.call-update) | async-done | bytes 262160 | tf_op jit(solution)/shard_map/reduce_scatter | solution.py:137
  970.9 80.6 %reduce-scatter.6.cloned.1.call-done = f32[32,2048]{1,0:T(8,128)} async-done(((f32[512,2048]{1,0:T(8,128)}), f32[32,2048]{1,0:T(8,128)}) %reduce-scatter.6.cloned.1.call-update) | async-done | bytes 262160 | tf_op jit(solution)/shard_map/reduce_scatter | solution.py:136
  1054.0 5.5 collective-permute-start.4
  1063.4 6.7 collective-permute-start.7
  1073.1 24.0 %fusion.16 = bf16[32,2048]{1,0:T(8,128)(2,1)S(1)} fusion(f32[32,2080]{1,0:T(8,128)S(1)} %fusion.64, f32[]{:T(128)} %exponential_reduce_fusion), kind=kOutput, calls=%fused_computation.41 | convolution fusion | flops 1678442496 | bytes 397316 | tf_op jit(solution)/shard_map/dot_general | solution.py:30
  1097.1 11.4 all_gather.7
  1108.5 5.6 fusion.102
  1114.2 5.7 fusion.104
  1119.9 5.9 convolution_add_fusion.10
  1126.8 5.7 fusion.96
  1132.5 6.1 fusion.98
  1138.7 5.8 convolution_add_fusion.14
  1145.5 5.9 fusion.90
  1151.4 5.8 fusion.92
  1157.2 6.0 convolution_add_fusion.18
  1164.3 5.7 fusion.84
  1170.0 5.7 fusion.86
  1175.8 6.2 convolution_add_fusion.22
  1183.0 5.8 fusion.78
  1188.8 5.9 fusion.80
  1194.7 5.9 convolution_add_fusion.26
  1201.6 5.9 fusion.72
  1207.5 5.7 fusion.74
  1213.2 6.1 convolution_add_fusion.30
  1220.3 5.6 convolution_add_fusion.9
  1226.9 5.8 convolution_add_fusion.13
  1233.8 5.7 convolution_add_fusion.17
  1240.5 6.1 convolution_add_fusion.21
  1247.7 5.7 convolution_add_fusion.25
  1254.5 5.9 convolution_add_fusion.29
  1264.4 477.5 %all-reduce.32.cloned.1.call-done = f32[2,128,128]{2,1,0:T(8,128)} async-done(((f32[2,128,128]{2,1,0:T(8,128)}), f32[2,128,128]{2,1,0:T(8,128)}) %all-reduce.32.cloned.1.call-update) | async-done | bytes 131088 | tf_op jit(solution)/shard_map/psum | solution.py:144
  1750.5 5.2 fusion.15
  (166 shorter events, 83.8 us)
Async XLA Ops:
  6.5 5.9 copy-start.25
  6.5 492.7 %all-reduce.28.cloned.1.call-start = ((), (), s32[]{:S(2)}) async-start(), calls=%async_computation.3 | async-start | bytes 262144 | tf_op jit(solution)/shard_map/psum | solution.py:101
  6.5 14.3 copy-start.24
  6.5 492.7 %copy-start.2 = (f32[6,2,128,128]{3,2,1,0:T(8,128)S(1)}, f32[6,2,128,128]{3,2,1,0:T(8,128)}, u32[]{:S(2)}) copy-start(f32[6,2,128,128]{3,2,1,0:T(8,128)} %param.6) | copy-start | bytes 2359300
  17.4 3.3 copy-start.27
  20.1 646.3 %reduce-scatter.4.cloned.1.call-start = ((), (), s32[]{:S(2)}) async-start(), calls=%async_computation.4 | async-start | bytes 1310720 | tf_op jit(solution)/shard_map/reduce_scatter | solution.py:118
  502.8 9.8 copy-start.3
  580.2 50.1 %copy-start.21 = (f32[128,2048]{1,0:T(8,128)}, f32[128,2048]{1,0:T(8,128)S(1)}, u32[]{:S(2)}) copy-start(f32[128,2048]{1,0:T(8,128)S(1)} %fusion.12) | copy-start | bytes 3145732
  585.2 45.1 %copy-start.10 = (f32[128,2048]{1,0:T(8,128)}, f32[128,2048]{1,0:T(8,128)S(1)}, u32[]{:S(2)}) copy-start(f32[128,2048]{1,0:T(8,128)S(1)} %fusion.13) | copy-start | bytes 3145732
  590.2 40.1 %copy-start.19 = (f32[128,2048]{1,0:T(8,128)}, f32[128,2048]{1,0:T(8,128)S(1)}, u32[]{:S(2)}) copy-start(f32[128,2048]{1,0:T(8,128)S(1)} %fusion.10) | copy-start | bytes 3145732
  595.1 35.2 %copy-start.8 = (f32[128,2048]{1,0:T(8,128)}, f32[128,2048]{1,0:T(8,128)S(1)}, u32[]{:S(2)}) copy-start(f32[128,2048]{1,0:T(8,128)S(1)} %fusion.11) | copy-start | bytes 3145732
  600.0 30.3 %copy-start.17 = (f32[128,2048]{1,0:T(8,128)}, f32[128,2048]{1,0:T(8,128)S(1)}, u32[]{:S(2)}) copy-start(f32[128,2048]{1,0:T(8,128)S(1)} %fusion.8) | copy-start | bytes 3145732
  605.1 25.2 %copy-start.6 = (f32[128,2048]{1,0:T(8,128)}, f32[128,2048]{1,0:T(8,128)S(1)}, u32[]{:S(2)}) copy-start(f32[128,2048]{1,0:T(8,128)S(1)} %fusion.9) | copy-start | bytes 3145732
  610.0 20.3 %copy-start.15 = (f32[128,2048]{1,0:T(8,128)}, f32[128,2048]{1,0:T(8,128)S(1)}, u32[]{:S(2)}) copy-start(f32[128,2048]{1,0:T(8,128)S(1)} %fusion.6) | copy-start | bytes 3145732
  615.3 15.0 copy-start.4
  620.2 10.1 copy-start.12
  641.3 128.0 %all-gather.2.cloned.1.call-start = ((), (), s32[]{:S(2)}) async-start(), calls=%async_computation.5 | async-start | bytes 4456448 | tf_op jit(solution)/shard_map/all_gather | solution.py:128
  667.2 6.8 collective-permute-start.1
  668.5 6.3 collective-permute-start
  676.0 10.9 collective-permute-start.2
  679.2 8.9 collective-permute-start.3
  713.7 166.4 %all-reduce.30.cloned.1.call-start = ((), (), s32[]{:S(2)}) async-start(), calls=%async_computation.6 | async-start | bytes 8388608 | tf_op jit(solution)/shard_map/psum | solution.py:130
  777.0 193.8 %reduce-scatter.8.cloned.1.call-start = ((), (), s32[]{:S(2)}) async-start(), calls=%async_computation.8 | async-start | bytes 4456448 | tf_op jit(solution)/shard_map/reduce_scatter | solution.py:137
  880.1 3.4 copy-start
  880.1 4.7 copy-start.1
  894.6 156.9 %copy-start.23 = (bf16[32,2048]{1,0:T(8,128)(2,1)S(1)}, bf16[32,2048]{1,0:T(8,128)(2,1)}, u32[]{:S(2)}) copy-start(bf16[32,2048]{1,0:T(8,128)(2,1)} %param.8) | copy-start | bytes 393220
  894.7 156.9 %reduce-scatter.6.cloned.1.call-start = ((), (), s32[]{:S(2)}) async-start(), calls=%async_computation.7 | async-start | bytes 4456448 | tf_op jit(solution)/shard_map/reduce_scatter | solution.py:136
  895.2 846.7 %all-reduce.32.cloned.1.call-start = ((), (), s32[]{:S(2)}) async-start(), calls=%async_computation.9 | async-start | bytes 262144 | tf_op jit(solution)/shard_map/psum | solution.py:144
  1052.7 6.8 collective-permute-start.5
  1054.0 6.3 collective-permute-start.4
  1060.5 10.3 collective-permute-start.6
  1063.4 8.7 collective-permute-start.7
  1073.1 35.4 %copy-start.22 = (f32[128,2048]{1,0:T(8,128)S(1)}, f32[128,2048]{1,0:T(8,128)}, u32[]{:S(2)}) copy-start(f32[128,2048]{1,0:T(8,128)} %copy-done.21) | copy-start | bytes 3145732
  1114.2 5.7 copy-start.11
  1119.9 7.0 copy-start.20
  1132.5 6.2 copy-start.9
  1138.7 6.8 copy-start.18
  1151.4 5.8 copy-start.7
  1157.2 7.1 copy-start.16
  1170.0 5.8 copy-start.5
  1175.8 7.2 copy-start.13
  1194.7 6.9 copy-start.14
  1254.4 487.5 %copy-start.28 = (s32[32]{0:T(128)S(1)}, s32[32]{0:T(128)}, u32[]{:S(2)}) copy-start(s32[32]{0:T(128)} %copy-done.27) | copy-start | bytes 388
  1741.9 7.4 copy-start.26
Sparse Core Ops, SparseCore 0:
  20.2 478.9 all-reduce.27
  641.4 24.9 reduce-scatter.3
  713.8 55.3 all-gather.1
  777.2 102.8 all-reduce.29
  894.8 76.0 reduce-scatter.7
  974.4 77.0 reduce-scatter.5
  1264.5 477.3 all-reduce.31
where the time goes:
time: 1780 us; the launch traced here: 1760 us
  waiting for transfers between devices  1300 us (73%)
  matrix products  371 us (21%)
  starting transfers between devices  34.4 us (2%)
  other arithmetic  25.5 us (1%)
    psum x1, waiting for transfers between devices, body(): spectral = lax.psum(partial_spec, ('kern', 'noise'))  478 us
    psum x1, waiting for transfers between devices, body(): spec_grad = lax.psum(pull_spec(slab_grad)[0], ('kern', 'noise'))  478 us
    dot_general x112, matrix products, matmul(): jnp.dot(left, right, precision=lax.Precision.HIGHEST, preferred_element_t...  371 us
    psum x1, waiting for transfers between devices, body(): mean_resp = lax.psum(jnp.sum(response, 0), 'noise') / sample_count  103 us
    reduce_scatter x1, waiting for transfers between devices, body(): lax.psum_scatter(upper_sum, 'noise', scatter_dimension=0, tiled=True)  80.6 us
    reduce_scatter x1, waiting for transfers between devices, body(): lax.psum_scatter(lower_sum, 'noise', scatter_dimension=0, tiled=True)  75.6 us
    all_gather x1, waiting for transfers between devices, body(): acid_rows = lax.all_gather(acid_block, 'noise', axis=0, tiled=True)  55 us
  transfers between devices with their start and end apart: 15, of which 12 were waited for; matrix products, arithmetic and copies ran while one was open for 0% of the time, Pallas kernels for 0%

commit v1 on v0

v1 whole, which is shorter than its diff:
```python
import math

import jax
import jax.numpy as jnp
import numpy as np
from jax import lax
from jax.experimental import pallas as pl
from jax.experimental.pallas import tpu as pltpu
from jax.sharding import PartitionSpec as P

HALO = 16
FREQ = 128
COARSE = 256
PERIOD = 2048
ROWS = 32
REACH = ROWS + 2 * HALO
EDGE = 128
GROUP = 6
KERNELS = 24
SAMPLES = 32
VMEM_BYTES = 48 * 1024 * 1024
BF = jnp.bfloat16
F32 = jnp.float32


def np_split(table):
    table = np.asarray(table, np.float32)
    high = table.astype(jnp.bfloat16)
    low = (table - high.astype(np.float32)).astype(jnp.bfloat16)
    return high, low


def np_waves(ids):
    centred = np.arange(FREQ) - FREQ // 2
    angles = 2.0 * np.pi * ((centred[:, None] * ids[None, :]) % PERIOD) / PERIOD
    return np.cos(angles), np.sin(angles)


def tables():
    cos, sin = np_waves(np.arange(PERIOD))
    waves = np.concatenate([cos, sin], 0).T
    reach = np.zeros((PERIOD + 2 * HALO, 4 * FREQ))
    reach[HALO:-HALO] = np.concatenate([cos, -sin, sin, cos], 0).T
    ccos, csin = np_waves(np.arange(COARSE) * (PERIOD // COARSE))
    grid = np.block([[ccos, csin], [-csin, ccos]]) / FREQ
    offsets = np.arange(-HALO, HALO + 1)
    taps = np.exp(-(offsets.astype(np.float64) ** 2) / (2.0 * (HALO / 2.0) ** 2))
    taps = taps / taps.sum()
    row_blur = np.zeros((ROWS, REACH))
    for row in range(ROWS):
        row_blur[row, row : row + 2 * HALO + 1] = taps
    shift = np.arange(PERIOD)[:, None] - (PERIOD // COARSE) * np.arange(COARSE)[None, :]
    freqs = np.arange(1, FREQ)
    line = (1.0 + 2.0 * np.cos(2.0 * np.pi * np.outer(np.arange(PERIOD), freqs) / PERIOD).sum(1)) / COARSE
    interp = line[shift % PERIOD]
    padded = np.zeros((PERIOD + 2 * HALO, COARSE))
    padded[HALO:-HALO] = interp
    own = np.zeros((PERIOD, COARSE))
    for index, tap in enumerate(taps):
        own += tap * padded[index : index + PERIOD]
    cross = np.zeros((2, COARSE, 2 * EDGE))
    for column in range(HALO):
        for index, offset in enumerate(offsets):
            if column + offset < 0:
                cross[1, :, column] += taps[index] * interp[PERIOD + column + offset]
            place = PERIOD - 1 - column + offset
            if place >= PERIOD:
                cross[0, :, 2 * EDGE - 1 - column] += taps[index] * interp[place - PERIOD]
    return waves, reach, grid, row_blur, own.T, cross


WAVES, REACH_WAVES, GRID, ROW_BLUR, OWN, CROSS = tables()
WAVES_HI, WAVES_LO = np_split(WAVES)
GRID_HI, GRID_LO = np_split(GRID)
OWN_HI, OWN_LO = np_split(OWN)
CROSS_HI, CROSS_LO = np_split(CROSS)


def split(value):
    high = value.astype(BF)
    return high, (value - high.astype(F32)).astype(BF)


NN = (((1,), (0,)), ((), ()))
NT = (((1,), (1,)), ((), ()))
TN = (((0,), (0,)), ((), ()))


def dot3(left, right, dims=NN):
    lh, ll = left
    rh, rl = right

    def one(a, b):
        return lax.dot_general(a, b, dims, preferred_element_type=F32)

    return one(lh, rh) + (one(lh, rl) + one(ll, rh))


def call(body, out_shape, args, **kw):
    return pl.pallas_call(
        body,
        out_shape=out_shape,
        compiler_params=pltpu.CompilerParams(vmem_limit_bytes=VMEM_BYTES),
        **kw,
    )(*args)


def spectrum_body(mask_ref, wh_ref, wl_ref, block_ref, out_ref):
    transmit = 2.0 * mask_ref[...] - 1.0
    by_col = dot3(split(transmit), (wh_ref[...], wl_ref[...]))
    both = dot3(split(block_ref[...]), split(by_col), TN)
    out_ref[:FREQ] = (both[:FREQ, :FREQ] - both[FREQ:, FREQ:]) * (1.0 / PERIOD)
    out_ref[FREQ:] = (both[:FREQ, FREQ:] + both[FREQ:, :FREQ]) * (-1.0 / PERIOD)


def field_body(spec_ref, kern_ref, reach_ref, gh_ref, gl_ref, blur_ref, field_ref, rows_ref, total_ref):
    step = pl.program_id(0)
    spec_re = spec_ref[:FREQ]
    spec_im = spec_ref[FREQ:]
    wave = split(jnp.concatenate([reach_ref[:, : 2 * FREQ], reach_ref[:, 2 * FREQ :]], 0))
    lefts = []
    for pair in range(GROUP // 2):
        near_re, near_im = [], []
        for index in (2 * pair, 2 * pair + 1):
            kern_re, kern_im = kern_ref[index, 0], kern_ref[index, 1]
            near_re.append(kern_re * spec_re - kern_im * spec_im)
            near_im.append(kern_re * spec_im + kern_im * spec_re)
        near = jnp.concatenate([jnp.concatenate(near_re, 1), jnp.concatenate(near_im, 1)], 0)
        left = dot3(wave, split(near))
        for half in range(2):
            cols = left[:, half * FREQ : (half + 1) * FREQ]
            lefts.append(jnp.concatenate([cols[:REACH], cols[REACH:]], 1))
    field = dot3(split(jnp.concatenate(lefts, 0)), (gh_ref[...], gl_ref[...]))
    field_ref[...] = field
    power = field * field
    power = power[:, :COARSE] + power[:, COARSE:]
    total = power[:REACH]
    for index in range(1, GROUP):
        total = total + power[index * REACH : (index + 1) * REACH]

    @pl.when(step == 0)
    def _():
        total_ref[...] = total

    @pl.when(step > 0)
    def _():
        total_ref[...] += total

    @pl.when(step == pl.num_programs(0) - 1)
    def _():
        rows_ref[...] = dot3(split(blur_ref[...]), split(total_ref[...]))


def own_body(rows_ref, oh_ref, ol_ref, out_ref):
    out_ref[...] = dot3(split(rows_ref[...]), (oh_ref[...], ol_ref[...]))


CHUNK = 512
LANES = 256


def dose_body(own_ref, other_ref, ch_ref, cl_ref, target_ref, noise_ref, grad_ref, send_ref, edge_ref, acid_ref):
    step = pl.program_id(0)
    last = pl.num_programs(0) - 1
    acid_ref[...] = own_ref[...]

    @pl.when(step == 0)
    def _():
        edge_ref[...] = dot3(split(other_ref[...]), (ch_ref[...], cl_ref[...]))
        acid_ref[:, :EDGE] += edge_ref[:, :EDGE]

    @pl.when(step == last)
    def _():
        acid_ref[:, CHUNK - EDGE :] += edge_ref[:, EDGE:]

    for row in range(0, ROWS, 16):
        for col in range(0, CHUNK, LANES):
            place = (slice(row, row + 16), slice(col, col + LANES))
            acid = acid_ref[place]
            quarter = 0.25 * acid
            base = acid - 2.0

            def sample(index, carry):
                sum_u, sum_q, sum_qu = carry
                noise = noise_ref[(index,) + place].astype(F32)
                u = jnp.tanh(quarter * noise + base)
                q = (1.0 - u * u) * (1.0 + 0.25 * noise)
                return sum_u + u, sum_q + q, sum_qu + q * u

            zero = jnp.zeros((16, LANES), F32)
            sum_u, sum_q, sum_qu = lax.fori_loop(0, SAMPLES, sample, (zero, zero, zero), unroll=8)
            target = target_ref[place].astype(F32)
            inner = 0.25 - sum_u * (1.0 / SAMPLES) - 0.5 * target
            grad_ref[place] = (1.0 / 16.0) * (sum_q * inner + 1.25 * sum_qu)

    @pl.when(step == 0)
    def _():
        edge_ref[:, :EDGE] = grad_ref[:, :EDGE]

    @pl.when(step == last)
    def _():
        edge_ref[:, EDGE:] = grad_ref[:, CHUNK - EDGE :]
        send_ref[...] = dot3(split(edge_ref[...]), (ch_ref[...], cl_ref[...]), NT)


def back_own_body(grad_ref, oh_ref, ol_ref, out_ref):
    out_ref[...] = dot3(split(grad_ref[...]), (oh_ref[...], ol_ref[...]), NT)


def back_body(own_ref, other_ref, field_ref, kern_ref, reach_ref, gh_ref, gl_ref, blur_ref, out_ref, grad_ref):
    step = pl.program_id(0)

    @pl.when(step == 0)
    def _():
        rows = own_ref[...] + other_ref[...]
        part = 2.0 * dot3(split(blur_ref[...]), split(rows), TN)
        grad_ref[:, :COARSE] = part
        grad_ref[:, COARSE:] = part
        out_ref[...] = jnp.zeros_like(out_ref)

    grad = grad_ref[...]
    pulled = jnp.concatenate(
        [field_ref[index * REACH : (index + 1) * REACH] * grad for index in range(GROUP)], 0
    )
    lefts = dot3(split(pulled), (gh_ref[...], gl_ref[...]), NT)
    wave = split(jnp.concatenate([reach_ref[:, : 2 * FREQ], reach_ref[:, 2 * FREQ :]], 0))
    sum_re = out_ref[:FREQ]
    sum_im = out_ref[FREQ:]
    for pair in range(GROUP // 2):
        stack = []
        for index in (2 * pair, 2 * pair + 1):
            left = lefts[index * REACH : (index + 1) * REACH]
            stack.append(jnp.concatenate([left[:, :FREQ], left[:, FREQ:]], 0))
        near = dot3(wave, split(jnp.concatenate(stack, 1)), TN)
        for half in range(2):
            index = 2 * pair + half
            near_re = near[:FREQ, half * FREQ : (half + 1) * FREQ]
            near_im = near[FREQ:, half * FREQ : (half + 1) * FREQ]
            kern_re, kern_im = kern_ref[index, 0], kern_ref[index, 1]
            sum_re = sum_re + (kern_re * near_re + kern_im * near_im)
            sum_im = sum_im + (kern_re * near_im - kern_im * near_re)
    out_ref[:FREQ] = sum_re
    out_ref[FREQ:] = sum_im


def final_body(spec_ref, block_ref, wh_ref, wl_ref, out_ref):
    grad_re = spec_ref[:FREQ]
    grad_im = spec_ref[FREQ:]
    mix = jnp.concatenate(
        [jnp.concatenate([grad_re, -grad_im], 1), jnp.concatenate([-grad_im, -grad_re], 1)], 0
    ) * (2.0 / PERIOD)
    rows = dot3(split(block_ref[...]), split(mix))
    out_ref[...] = dot3(split(rows), (wh_ref[...], wl_ref[...]), NT)


def sum_blocks(part):
    axes = ("kern", "noise")
    count = lax.axis_size(axes)
    pieces = part.reshape(count, part.shape[0] // count, part.shape[1])
    got = lax.all_to_all(pieces, axes, 0, 0, tiled=True)
    mine = jnp.sum(got, 0, keepdims=True)
    return lax.all_to_all(jnp.broadcast_to(mine, pieces.shape), axes, 0, 0, tiled=True).reshape(part.shape)


def body(mask_values, kernels, weights, target, dose_noise):
    noise_count = lax.axis_size("noise")
    block = lax.axis_index("kern") * noise_count + lax.axis_index("noise")
    tile = lax.axis_index("tile")
    first = block * ROWS
    whole = pl.BlockSpec(memory_space=pltpu.VMEM)
    f32 = lambda *shape: jax.ShapeDtypeStruct(shape, F32)
    steps = KERNELS // GROUP

    scaled = kernels * jnp.sqrt(weights)[:, None, None, None]
    kern = lax.all_gather(scaled, "kern", axis=0, tiled=True)
    samples = lax.all_to_all(dose_noise, "noise", 1, 0, tiled=True)

    block_waves = lax.dynamic_slice(jnp.asarray(WAVES, F32), (first, 0), (ROWS, 2 * FREQ))
    reach_waves = lax.dynamic_slice(jnp.asarray(REACH_WAVES, F32), (first, 0), (REACH, 4 * FREQ))
    waves = (jnp.asarray(WAVES_HI), jnp.asarray(WAVES_LO))
    grid = (jnp.asarray(GRID_HI), jnp.asarray(GRID_LO))
    own = (jnp.asarray(OWN_HI), jnp.asarray(OWN_LO))
    cross = tuple(lax.dynamic_index_in_dim(jnp.asarray(t), tile, 0, keepdims=False) for t in (CROSS_HI, CROSS_LO))
    blur = jnp.asarray(ROW_BLUR, F32)

    part = call(spectrum_body, f32(2 * FREQ, FREQ), (mask_values, *waves, block_waves))
    spec = sum_blocks(part)

    def fixed(*shape):
        return pl.BlockSpec(shape, lambda i: (0,) * len(shape))

    kern_spec = pl.BlockSpec((GROUP, 2, FREQ, FREQ), lambda i: (i, 0, 0, 0))
    field_spec = pl.BlockSpec((GROUP * REACH, 2 * COARSE), lambda i: (i, 0))
    const_specs = [
        fixed(REACH, 4 * FREQ),
        fixed(2 * FREQ, 2 * COARSE),
        fixed(2 * FREQ, 2 * COARSE),
        fixed(ROWS, REACH),
    ]
    field, rows = call(
        field_body,
        (f32(KERNELS * REACH, 2 * COARSE), f32(ROWS, COARSE)),
        (spec, kern, reach_waves, *grid, blur),
        grid=(steps,),
        in_specs=[fixed(2 * FREQ, FREQ), kern_spec] + const_specs,
        out_specs=(field_spec, fixed(ROWS, COARSE)),
        scratch_shapes=[pltpu.VMEM((REACH, COARSE), F32)],
    )
    swap = [(0, 1), (1, 0)]
    rows_other = lax.ppermute(rows, "tile", swap)
    acid = call(own_body, f32(ROWS, PERIOD), (rows, *own))
    chunk = lambda: pl.BlockSpec((ROWS, CHUNK), lambda i: (0, i))
    grad, send = call(
        dose_body,
        (f32(ROWS, PERIOD), f32(ROWS, COARSE)),
        (acid, rows_other, *cross, target, samples),
        grid=(PERIOD // CHUNK,),
        in_specs=[
            chunk(),
            fixed(ROWS, COARSE),
            fixed(COARSE, 2 * EDGE),
            fixed(COARSE, 2 * EDGE),
            chunk(),
            pl.BlockSpec((SAMPLES, ROWS, CHUNK), lambda i: (0, 0, i)),
        ],
        out_specs=(chunk(), fixed(ROWS, COARSE)),
        scratch_shapes=[pltpu.VMEM((ROWS, 2 * EDGE), F32), pltpu.VMEM((ROWS, CHUNK), F32)],
    )
    grad_other = lax.ppermute(send, "tile", swap)
    grad_own = call(back_own_body, f32(ROWS, COARSE), (grad, *own))
    spec_part = call(
        back_body,
        f32(2 * FREQ, FREQ),
        (grad_own, grad_other, field, kern, reach_waves, *grid, blur),
        grid=(steps,),
        in_specs=[fixed(ROWS, COARSE), fixed(ROWS, COARSE), field_spec, kern_spec] + const_specs,
        out_specs=fixed(2 * FREQ, FREQ),
        scratch_shapes=[pltpu.VMEM((REACH, 2 * COARSE), F32)],
    )
    spec_grad = sum_blocks(spec_part)
    return call(final_body, f32(ROWS, PERIOD), (spec_grad, block_waves, *waves))


def solution(mesh):
    return jax.shard_map(
        body,
        mesh=mesh,
        in_specs=(
            P(("kern", "noise"), "tile"),
            P("kern", None, None, None),
            P("kern"),
            P(("kern", "noise"), "tile"),
            P("noise", "kern", "tile"),
        ),
        out_specs=P(("kern", "noise"), "tile"),
        check_vma=False,
    )
```

time: 1780 us -> 182 us (0.10)
  waiting for transfers between devices: 1300 us -> 47 us
  matrix products: 371 us -> 0 us
  blocking collectives: 11.4 us -> 58.9 us
  other arithmetic: 25.5 us -> 2.33 us
  Pallas kernels: 0 us -> 21.9 us
  starting transfers between devices: 34.4 us -> 16.3 us
    psum x3 -> x0, waiting for transfers between devices: 1060 us -> none  [the longest x1 478 us: body(): spectral = lax.psum(partial_spec, ('kern', 'noise'))]
    dot_general x112 -> x0, matrix products: 371 us -> none  [matmul(): jnp.dot(left, right, precision=lax.Precision.HIGHEST, preferred_element_t...]
    reduce_scatter x3 -> x0, waiting for transfers between devices: 181 us -> none  [the longest x1 80.6 us: body(): lax.psum_scatter(upper_sum, 'noise', scatter_dimension=0, tiled=True)]
    all_to_all x0 -> x3, blocking collectives: none -> 58.9 us  [the longest x2 46.3 us: sum_blocks(): got = lax.all_to_all(pieces, axes, 0, 0, tiled=True)]
    all_gather x1, waiting for transfers between devices: 55 us -> 0.02 us  [body(): kern = lax.all_gather(scaled, 'kern', axis=0, tiled=True)]
    all_to_all x0 -> x2, waiting for transfers between devices: none -> 46.2 us  [the longest x1 45.2 us: body(): samples = lax.all_to_all(dose_noise, 'noise', 1, 0, tiled=True)]
    ppermute x8 -> x2, starting transfers between devices: 33.3 us -> 5.17 us  [the longest x1 2.72 us: body(): grad_other = lax.ppermute(send, 'tile', swap)]
    pallas_call x0 -> x7, Pallas kernels: none -> 21.9 us  [call(): pl.pallas_call(body, out_shape=out_shape, compiler_params=pltpu.CompilerP...]
  transfers between devices with their start and end apart: 15 -> 5, of which waited for: 12 -> 3; matrix products, arithmetic and copies ran while one was open for 0% -> 8% of each run, Pallas kernels for 0% -> 4%
where the time goes in v1:
time: 182 us; the launch traced here: 181 us
  blocking collectives  58.9 us (32%)
  waiting for transfers between devices  47 us (26%)
  Pallas kernels  21.9 us (12%)
  local copies, waits for them, and re-layouts  21.1 us (12%)
  starting transfers between devices  16.3 us (9%)
  between operations  13.6 us (7%)
  other arithmetic  2.33 us (1%)
    all_to_all x2, blocking collectives, sum_blocks(): got = lax.all_to_all(pieces, axes, 0, 0, tiled=True)  46.3 us
    all_to_all x1, waiting for transfers between devices, body(): samples = lax.all_to_all(dose_noise, 'noise', 1, 0, tiled=True)  45.2 us
    pallas_call x7, Pallas kernels, call(): pl.pallas_call(body, out_shape=out_shape, compiler_params=pltpu.CompilerP...  21.9 us
    unnamed x31, local copies, waits for them, and re-layouts  13.8 us
    all_to_all x1, blocking collectives, sum_blocks(): lax.all_to_all(jnp.broadcast_to(mine, pieces.shape), axes, 0, 0, tiled=True)  12.6 us
    all_to_all x1, starting transfers between devices, body(): samples = lax.all_to_all(dose_noise, 'noise', 1, 0, tiled=True)  5.94 us
    all_to_all x1, starting transfers between devices, sum_blocks(): lax.all_to_all(jnp.broadcast_to(mine, pieces.shape), axes, 0, 0, tiled=True)  5.18 us
    all_to_all x1, local copies, waits for them, and re-layouts, body(): samples = lax.all_to_all(dose_noise, 'noise', 1, 0, tiled=True)  4.22 us
  transfers between devices with their start and end apart: 5, of which 3 were waited for; matrix products, arithmetic and copies ran while one was open for 8% of the time, Pallas kernels for 4%

profile of v1, /device:TPU:1, one launch (start us, length us, event | category | flops | bytes accessed | tf_op | source)
XLA Modules:
  0.0 181.2 jit_solution(6614200242973747223)
XLA Ops:
  6.5 0.0 all-gather.2.cloned.1.call-start
  6.5 0.7 sqrt.3
  7.2 2.2 %broadcast_multiply_fusion = f32[6,2,128,128]{3,2,1,0:T(8,128)} fusion(f32[6,2,128,128]{3,2,1,0:T(8,128)} %param.17, f32[6]{0:T(128)S(1)} %sqrt.3), kind=kLoop, calls=%fused_computation | loop fusion | flops 196608 | bytes 1572888 | tf_op jit(solution)/shard_map/mul | solution.py:274
  9.4 0.0 all-gather.2.cloned.1.call-update
  9.4 0.8 constant_dynamic-slice_fusion.1.block_ref
  10.2 0.0 copy-start.2
  10.2 1.2 copy-done.2
  11.4 0.0 copy-start.4
  11.4 1.2 copy-done.4
  12.6 0.0 copy-start.10
  12.6 0.9 copy-done.10
  13.6 1.0 shard_map.154
  14.6 20.1 %all_to_all.38 = f32[64,4,128]{2,1,0:T(4,128)S(1)} all-to-all(f32[64,4,128]{2,1,0:T(4,128)S(1)} %bitcast.16), channel_id=1, replica_groups=mesh['tile'=2,'kern'=4,'noise'=16] {'kern','noise'}, dimensions={0} | all-to-all | bytes 262144 | tf_op jit(solution)/shard_map/all_to_all | solution.py:260
  34.7 0.1 reduce_sum.18
  34.8 0.7 broadcast_in_dim.4
  35.5 5.2 %all-to-all-start.1 = ((f32[64,4,128]{2,1,0:T(4,128)}), f32[64,4,128]{2,1,0:T(4,128)S(1)}, u32[]{:S(2)}, u32[]{:S(2)}) async-start(f32[64,4,128]{2,1,0:T(4,128)} %broadcast_in_dim.4), calls=%async_computation.1 | async-start | bytes 262144 | tf_op jit(solution)/shard_map/all_to_all | solution.py:262
  40.7 8.6 %copy.18 = bf16[2,512,2048]{2,0,1:T(2,128)(2,1)} copy(bf16[2,512,2048]{2,1,0:T(8,128)(2,1)} %param.20) | data formatting | bytes 8388608 | tf_op args[4]
  49.3 0.0 copy-start.8
  49.3 0.0 copy-start.9
  49.3 0.0 copy-start.12
  49.3 1.0 all-to-all-done.1
  50.2 5.9 %all-to-all-start.2 = ((bf16[2,512,2048]{2,0,1:T(2,128)(2,1)}), bf16[2,512,2048]{2,0,1:T(2,128)(2,1)}, u32[]{:S(2)}, u32[]{:S(2)}) async-start(bf16[2,512,2048]{2,0,1:T(2,128)(2,1)} %copy.18), calls=%async_computation.2 | async-start | bytes 8388608 | tf_op jit(solution)/shard_map/all_to_all | solution.py:276
  56.2 0.0 copy-start.13
  56.2 0.0 copy-start.14
  56.2 1.0 constant_dynamic-slice_fusion.reach_ref
  57.2 0.0 all-gather.2.cloned.1.call-done.kern_ref
  57.2 0.0 copy-done.8
  57.2 0.0 copy-done.9
  57.2 0.0 copy-done.12
  57.2 5.1 %shard_map.155 = (f32[1536,512]{1,0:T(8,128)S(1)}, f32[32,256]{1,0:T(8,128)S(1)}) custom-call(f32[256,128]{1,0:T(8,128)S(1)} %bitcast.14, f32[24,2,128,128]{3,2,1,0:T(8,128)} %all-gather.2.cloned.1.call-done.kern_ref, f32[64,512]{1,0:T(8,128)S(1)} %constant_dynamic-slice_fusion.reach_ref, bf16[256,512]{1,0:T(8,128)(2,1)S(1)} %copy-done.9, ...), custom_call_target="tpu_custom_call" | custom-call | tf_op jit(solution)/shard_map/pallas_call | solution.py:100
  62.3 0.0 copy-start.6
  62.4 1.7 copy-done.6
  64.1 2.5 %collective-permute-start = (f32[32,256]{1,0:T(8,128)S(1)}, f32[32,256]{1,0:T(8,128)S(1)}, u32[]{:S(2)}, u32[]{:S(2)}) collective-permute-start(f32[32,256]{1,0:T(8,128)S(1)} %get-tuple-element.9.rows_ref), channel_id=1, source_target_pairs={{0,64},{64,0},{1,65},{65,1},{2,66},{66,2},{3,67},{67,3},{4,68},{68... | collective-permute-start | bytes 98312 | tf_op jit(solution)/shard_map/ppermute | solution.py:310
  66.5 0.0 copy-done.13
  66.5 0.0 copy-done.14
  66.6 45.2 %all-to-all-done.2 = bf16[2,512,2048]{2,0,1:T(2,128)(2,1)} async-done(((bf16[2,512,2048]{2,0,1:T(2,128)(2,1)}), bf16[2,512,2048]{2,0,1:T(2,128)(2,1)}, u32[]{:S(2)}, u32[]{:S(2)}) %all-to-all-start.2) | async-done | bytes 4194336 | tf_op jit(solution)/shard_map/all_to_all | solution.py:276
  111.8 0.0 copy-start
  111.8 0.0 copy-start.1
  111.8 0.0 copy-start.11
  111.8 4.2 %copy.19 = bf16[2,16,32,2048]{3,2,0,1:T(8,128)(2,1)S(1)} copy(bf16[2,16,32,2048]{3,0,2,1:T(2,128)(2,1)} %bitcast.4) | data formatting | bytes 8388608 | tf_op jit(solution)/shard_map/all_to_all | solution.py:276
  116.1 0.0 copy-done
  116.1 0.0 copy-done.1
  116.1 0.6 shard_map.156.own_ref
  116.7 0.0 copy-start.7
  116.7 0.0 collective-permute-done.other_ref
  116.7 0.0 copy-done.11
  116.7 4.9 %shard_map.157 = (f32[32,2048]{1,0:T(8,128)S(1)}, f32[32,256]{1,0:T(8,128)S(1)}) custom-call(f32[32,2048]{1,0:T(8,128)S(1)} %shard_map.156.own_ref, f32[32,256]{1,0:T(8,128)S(1)} %collective-permute-done.other_ref, bf16[256,256]{1,0:T(8,128)(2,1)S(1)} %get-tuple-element.14.ch_ref, bf16[256,256]{1,0:T(8,128)(2,1)S(1)} %get-tuple-element.13.cl_ref, ...), custom_call_target="tpu_custom_call" | custom-call | tf_op jit(solution)/shard_map/pallas_call | solution.py:100
  121.7 2.7 %collective-permute-start.1 = (f32[32,256]{1,0:T(8,128)S(1)}, f32[32,256]{1,0:T(8,128)S(1)}, u32[]{:S(2)}, u32[]{:S(2)}) collective-permute-start(f32[32,256]{1,0:T(8,128)S(1)} %get-tuple-element.11), channel_id=1, source_target_pairs={{0,64},{64,0},{1,65},{65,1},{2,66},{66,2},{3,67},{67,3},{4,68},{68... | collective-permute-start | bytes 98312 | tf_op jit(solution)/shard_map/ppermute | solution.py:329
  124.4 1.0 shard_map.158.own_ref
  125.4 0.0 copy-start.3
  125.4 0.0 copy-start.5
  125.4 0.8 collective-permute-done.1.other_ref
  126.2 0.0 copy-done.7
  126.2 7.3 %shard_map.159 = f32[256,128]{1,0:T(8,128)S(1)} custom-call(f32[32,256]{1,0:T(8,128)S(1)} %shard_map.158.own_ref, f32[32,256]{1,0:T(8,128)S(1)} %collective-permute-done.1.other_ref, f32[1536,512]{1,0:T(8,128)S(1)} %copy-done.7, f32[24,2,128,128]{3,2,1,0:T(8,128)} %all-gather.2.cloned.1.call-done.kern_ref, ...), custom_call_target="tpu_custom_call" | custom-call | tf_op jit(solution)/shard_map/pallas_call | solution.py:100
  133.5 26.2 %all_to_all.39 = f32[64,4,128]{2,1,0:T(4,128)S(1)} all-to-all(f32[64,4,128]{2,1,0:T(4,128)S(1)} %bitcast.13), channel_id=1, replica_groups=mesh['tile'=2,'kern'=4,'noise'=16] {'kern','noise'}, dimensions={0} | all-to-all | bytes 262144 | tf_op jit(solution)/shard_map/all_to_all | solution.py:260
  159.6 0.1 reduce_sum.19
  159.7 12.6 %all_to_all.40 = f32[64,4,128]{2,1,0:T(4,128)S(1)} all-to-all(f32[64,4,128]{2,1,0:T(4,128)S(1)} %broadcast_in_dim.5), channel_id=1, replica_groups=mesh['tile'=2,'kern'=4,'noise'=16] {'kern','noise'}, dimensions={0} | all-to-all | bytes 262144 | tf_op jit(solution)/shard_map/all_to_all | solution.py:262
  172.4 0.0 copy-done.3
  172.4 0.0 copy-done.5
  172.4 1.9 %shard_map.160 = f32[32,2048]{1,0:T(8,128)} custom-call(f32[256,128]{1,0:T(8,128)S(1)} %bitcast.15, f32[32,256]{1,0:T(8,128)S(1)} %constant_dynamic-slice_fusion.1.block_ref, bf16[2048,256]{1,0:T(8,128)(2,1)S(1)} %copy-done.5, bf16[2048,256]{1,0:T(8,128)(2,1)S(1)} %copy-done.3), custom_call_target="tpu_custom_call" | custom-call | tf_op jit(solution)/shard_map/pallas_call | solution.py:100
  (2 shorter events, 0.0 us)
Async XLA Ops:
  6.5 50.7 %all-gather.2.cloned.1.call-start = ((), (), s32[]{:S(2)}) async-start(), calls=%async_computation.5 | async-start | bytes 3932160 | tf_op jit(solution)/shard_map/all_gather | solution.py:275
  10.2 1.2 copy-start.2
  11.4 1.2 copy-start.4
  12.6 0.9 copy-start.10
  35.5 14.7 %all-to-all-start.1 = ((f32[64,4,128]{2,1,0:T(4,128)}), f32[64,4,128]{2,1,0:T(4,128)S(1)}, u32[]{:S(2)}, u32[]{:S(2)}) async-start(f32[64,4,128]{2,1,0:T(4,128)} %broadcast_in_dim.4), calls=%async_computation.1 | async-start | bytes 262144 | tf_op jit(solution)/shard_map/all_to_all | solution.py:262
  49.3 8.0 %copy-start.8 = (bf16[256,512]{1,0:T(8,128)(2,1)S(1)}, bf16[256,512]{1,0:T(8,128)(2,1)}, u32[]{:S(2)}) copy-start(bf16[256,512]{1,0:T(8,128)(2,1)} %constant.61.clone.gl_ref) | copy-start | bytes 786436
  49.3 8.0 %copy-start.9 = (bf16[256,512]{1,0:T(8,128)(2,1)S(1)}, bf16[256,512]{1,0:T(8,128)(2,1)}, u32[]{:S(2)}) copy-start(bf16[256,512]{1,0:T(8,128)(2,1)} %constant.60.clone.gh_ref) | copy-start | bytes 786436
  49.3 8.0 %copy-start.12 = (f32[32,64]{1,0:T(8,128)S(1)}, f32[32,64]{1,0:T(8,128)}, u32[]{:S(2)}) copy-start(f32[32,64]{1,0:T(8,128)} %constant.66.clone.blur_ref) | copy-start | bytes 24580
  50.2 61.6 %all-to-all-start.2 = ((bf16[2,512,2048]{2,0,1:T(2,128)(2,1)}), bf16[2,512,2048]{2,0,1:T(2,128)(2,1)}, u32[]{:S(2)}, u32[]{:S(2)}) async-start(bf16[2,512,2048]{2,0,1:T(2,128)(2,1)} %copy.18), calls=%async_computation.2 | async-start | bytes 8388608 | tf_op jit(solution)/shard_map/all_to_all | solution.py:276
  56.2 10.4 %copy-start.13 = (bf16[2,256,256]{2,1,0:T(8,128)(2,1)S(1)}, bf16[2,256,256]{2,1,0:T(8,128)(2,1)}, u32[]{:S(2)}) copy-start(bf16[2,256,256]{2,1,0:T(8,128)(2,1)} %constant.65.clone) | copy-start | bytes 786436
  56.2 10.4 %copy-start.14 = (bf16[2,256,256]{2,1,0:T(8,128)(2,1)S(1)}, bf16[2,256,256]{2,1,0:T(8,128)(2,1)}, u32[]{:S(2)}) copy-start(bf16[2,256,256]{2,1,0:T(8,128)(2,1)} %constant.64.clone) | copy-start | bytes 786436
  62.3 1.7 copy-start.6
  64.1 52.6 %collective-permute-start = (f32[32,256]{1,0:T(8,128)S(1)}, f32[32,256]{1,0:T(8,128)S(1)}, u32[]{:S(2)}, u32[]{:S(2)}) collective-permute-start(f32[32,256]{1,0:T(8,128)S(1)} %get-tuple-element.9.rows_ref), channel_id=1, source_target_pairs={{0,64},{64,0},{1,65},{65,1},{2,66},{66,2},{3,67},{67,3},{4,68},{68... | collective-permute-start | bytes 98312 | tf_op jit(solution)/shard_map/ppermute | solution.py:310
  111.8 4.2 %copy-start = (bf16[256,2048]{1,0:T(8,128)(2,1)S(1)}, bf16[256,2048]{1,0:T(8,128)(2,1)}, u32[]{:S(2)}) copy-start(bf16[256,2048]{1,0:T(8,128)(2,1)} %constant.63.clone.ol_ref) | copy-start | bytes 3145732
  111.8 4.2 %copy-start.1 = (bf16[256,2048]{1,0:T(8,128)(2,1)S(1)}, bf16[256,2048]{1,0:T(8,128)(2,1)}, u32[]{:S(2)}) copy-start(bf16[256,2048]{1,0:T(8,128)(2,1)} %constant.62.clone.oh_ref) | copy-start | bytes 3145732
  111.8 4.9 %copy-start.11 = (bf16[32,2048]{1,0:T(8,128)(2,1)S(1)}, bf16[32,2048]{1,0:T(8,128)(2,1)}, u32[]{:S(2)}) copy-start(bf16[32,2048]{1,0:T(8,128)(2,1)} %target_ref.1) | copy-start | bytes 393220
  116.7 9.5 %copy-start.7 = (f32[1536,512]{1,0:T(8,128)S(1)}, f32[1536,512]{1,0:T(8,128)}, u32[]{:S(2)}) copy-start(f32[1536,512]{1,0:T(8,128)} %copy-done.6) | copy-start | bytes 9437188
  121.7 4.5 %collective-permute-start.1 = (f32[32,256]{1,0:T(8,128)S(1)}, f32[32,256]{1,0:T(8,128)S(1)}, u32[]{:S(2)}, u32[]{:S(2)}) collective-permute-start(f32[32,256]{1,0:T(8,128)S(1)} %get-tuple-element.11), channel_id=1, source_target_pairs={{0,64},{64,0},{1,65},{65,1},{2,66},{66,2},{3,67},{67,3},{4,68},{68... | collective-permute-start | bytes 98312 | tf_op jit(solution)/shard_map/ppermute | solution.py:329
  125.4 47.0 %copy-start.3 = (bf16[2048,256]{1,0:T(8,128)(2,1)S(1)}, bf16[2048,256]{1,0:T(8,128)(2,1)}, u32[]{:S(2)}) copy-start(bf16[2048,256]{1,0:T(8,128)(2,1)} %constant.59.clone.wl_ref) | copy-start | bytes 3145732
  125.4 46.9 %copy-start.5 = (bf16[2048,256]{1,0:T(8,128)(2,1)S(1)}, bf16[2048,256]{1,0:T(8,128)(2,1)}, u32[]{:S(2)}) copy-start(bf16[2048,256]{1,0:T(8,128)(2,1)} %constant.58.clone.wh_ref) | copy-start | bytes 3145732
Sparse Core Ops, SparseCore 0:
  9.5 44.2 all-gather.1

commit v2 on v1

v2 whole, which is shorter than its diff:
```python
import math

import jax
import jax.numpy as jnp
import numpy as np
from jax import lax
from jax.experimental import pallas as pl
from jax.experimental.pallas import tpu as pltpu
from jax.sharding import PartitionSpec as P

HALO = 16
FREQ = 128
COARSE = 256
PERIOD = 2048
ROWS = 32
REACH = ROWS + 2 * HALO
EDGE = 128
GROUP = 6
PAIRS = GROUP // 2
KERN = 4
SAMPLES = 32
RANK = 16
MIB = 32
BF = jnp.bfloat16
F32 = jnp.float32


def np_split(table):
    table = np.asarray(table, np.float32)
    high = table.astype(jnp.bfloat16)
    low = (table - high.astype(np.float32)).astype(jnp.bfloat16)
    return high, low


def np_waves(ids):
    centred = np.arange(FREQ) - FREQ // 2
    angles = 2.0 * np.pi * ((centred[:, None] * ids[None, :]) % PERIOD) / PERIOD
    return np.cos(angles), np.sin(angles)


def line_tables():
    half = FREQ // 2
    pixels = np.arange(PERIOD)
    angle = lambda f: 2.0 * np.pi * ((f[:, None] * pixels[None, :]) % PERIOD) / PERIOD
    line = np.concatenate([np.cos(angle(np.arange(half + 1))), np.sin(angle(np.arange(1, half)))], 0)
    last = np.sin(angle(np.array([half])))
    unfold = np.zeros((FREQ, 2 * FREQ))
    for j in range(FREQ):
        f = j - half
        unfold[abs(f), j] = 1.0
        if 0 < abs(f) < half:
            unfold[half + abs(f), FREQ + j] = np.sign(f)
    row = np.arange(ROWS) - (ROWS - 1) / 2.0
    fine = np.arange(-half, half + 0.01, 0.25)
    wave = np.exp(2j * np.pi * np.outer(row, fine) / PERIOD)
    basis = np.linalg.svd(np.concatenate([wave.real, wave.imag], 1))[0][:, : RANK - 1]
    basis = np.concatenate([basis, np.zeros((ROWS, FREQ - RANK + 1))], 1)
    freqs = np.arange(FREQ) - half
    coef = np.exp(2j * np.pi * np.outer(freqs, row) / PERIOD) @ basis
    blocks = PERIOD // ROWS
    centre = ROWS * np.arange(blocks) + (ROWS - 1) / 2.0
    phase = np.exp(2j * np.pi * np.outer(freqs, centre) / PERIOD)
    rows = phase[:, :, None] * coef[:, None, :RANK]
    rows[:, :, RANK - 1] = 0.0
    spare = np.zeros_like(rows)
    spare[:, :, RANK - 1] = phase
    rows = rows.reshape(FREQ, blocks * RANK)
    spare = spare.reshape(FREQ, blocks * RANK)
    gather = np.concatenate([rows.real, rows.imag, spare.real, spare.imag], 0)
    return line, last, unfold, basis, np.stack([coef.real, coef.imag]), gather


def tables():
    cos, sin = np_waves(np.arange(PERIOD))
    reach = np.zeros((PERIOD + 2 * HALO, 4 * FREQ))
    reach[HALO:-HALO] = np.concatenate([cos, -sin, sin, cos], 0).T
    ccos, csin = np_waves(np.arange(COARSE) * (PERIOD // COARSE))
    grid = np.block([[ccos, csin], [-csin, ccos]]) / FREQ
    offsets = np.arange(-HALO, HALO + 1)
    taps = np.exp(-(offsets.astype(np.float64) ** 2) / (2.0 * (HALO / 2.0) ** 2))
    taps = taps / taps.sum()
    row_blur = np.zeros((ROWS, REACH))
    for row in range(ROWS):
        row_blur[row, row : row + 2 * HALO + 1] = taps
    shift = np.arange(PERIOD)[:, None] - (PERIOD // COARSE) * np.arange(COARSE)[None, :]
    freqs = np.arange(1, FREQ)
    line = (1.0 + 2.0 * np.cos(2.0 * np.pi * np.outer(np.arange(PERIOD), freqs) / PERIOD).sum(1)) / COARSE
    interp = line[shift % PERIOD]
    padded = np.zeros((PERIOD + 2 * HALO, COARSE))
    padded[HALO:-HALO] = interp
    own = np.zeros((PERIOD, COARSE))
    for index, tap in enumerate(taps):
        own += tap * padded[index : index + PERIOD]
    cross = np.zeros((2, COARSE, 2 * EDGE))
    for column in range(HALO):
        for index, offset in enumerate(offsets):
            if column + offset < 0:
                cross[1, :, column] += taps[index] * interp[PERIOD + column + offset]
            place = PERIOD - 1 - column + offset
            if place >= PERIOD:
                cross[0, :, 2 * EDGE - 1 - column] += taps[index] * interp[place - PERIOD]
    return reach, grid, row_blur, own, cross


LINE, LAST, UNFOLD, BASIS, COEF, GATHER = line_tables()
REACH_WAVES, GRID, ROW_BLUR, OWN, CROSS = tables()
BLOCKS = PERIOD // ROWS
GROUP_BLOCKS = BLOCKS // KERN
WAVE = np.stack(
    [
        np.concatenate([part[:, : 2 * FREQ], part[:, 2 * FREQ :]], 0)
        for part in (REACH_WAVES[first : first + REACH] for first in range(0, PERIOD, ROWS))
    ]
)
WAVE = WAVE.reshape(KERN, GROUP_BLOCKS, 2 * REACH, 2 * FREQ).transpose(1, 0, 2, 3)
WAVE = WAVE.reshape(GROUP_BLOCKS, KERN * 2 * REACH, 2 * FREQ)
GATHER_OWN = GATHER.reshape(4 * FREQ, KERN, GROUP_BLOCKS * RANK).transpose(1, 0, 2)
BLUR = np.kron(np.eye(KERN), ROW_BLUR)


def split(value):
    high = value.astype(BF)
    return high, (value - high.astype(F32)).astype(BF)


NN = (((1,), (0,)), ((), ()))


def dot3(left, right):
    lh, ll = left
    rh, rl = right

    def one(a, b):
        return lax.dot_general(a, b, NN, preferred_element_type=F32)

    return one(lh, rh) + (one(lh, rl) + one(ll, rh))


def dot_exact(left, right):
    high, low = left
    return jnp.dot(high, right, preferred_element_type=F32) + jnp.dot(low, right, preferred_element_type=F32)


def call(body, out_shape, args, place=None, **kw):
    params = pltpu.CompilerParams(vmem_limit_bytes=MIB * 1024 * 1024)
    if place is None:
        return pl.pallas_call(body, out_shape=out_shape, compiler_params=params, **kw)(*args)
    grid_spec = pltpu.PrefetchScalarGridSpec(num_scalar_prefetch=1, **kw)
    return pl.pallas_call(body, out_shape=out_shape, compiler_params=params, grid_spec=grid_spec)(place, *args)


def hbm(*values):
    return tuple(pltpu.with_memory_space_constraint(value, pltpu.HBM) for value in values)


def vmem(*values):
    return tuple(pltpu.with_memory_space_constraint(value, pltpu.VMEM) for value in values)


CHUNK = 512
LANES = 256


def front_body(mask_ref, basis_ref, lh_ref, ll_ref, last_ref, noise_ref, first_ref, second_ref, packed_ref):
    @pl.when(pl.program_id(0) == 0)
    def _():
        transmit = (2.0 * mask_ref[...] - 1.0) * (1.0 / PERIOD)
        rows = dot3(split(basis_ref[...]), split(transmit))
        part = dot3(split(rows), (lh_ref[...], ll_ref[...]))
        row = lax.broadcasted_iota(jnp.int32, (RANK, FREQ), 0)
        lane = lax.broadcasted_iota(jnp.int32, (RANK, FREQ), 1)
        apart = jnp.sum(rows * last_ref[...], 1, keepdims=True)
        apart = jnp.sum(jnp.where(row == lane, apart, 0.0), 0, keepdims=True)
        high, low = split(jnp.where(row == RANK - 1, apart, part))
        packed_ref[:RANK] = high
        packed_ref[RANK:] = low

    for which in range(first_ref.shape[0]):
        rows = slice(which * ROWS, (which + 1) * ROWS)
        first_ref[which, :, :PERIOD] = noise_ref[0, rows]
        first_ref[which, :, PERIOD:] = packed_ref[...]
        second_ref[which] = noise_ref[1, rows]


def spectrum_body(_, got_ref, gh_ref, gl_ref, unfold_ref, coef_ref, out_ref):
    high = got_ref[:, :RANK].reshape(GROUP_BLOCKS * RANK, FREQ)
    low = got_ref[:, RANK:].reshape(GROUP_BLOCKS * RANK, FREQ)
    both = dot3((gh_ref[0], gl_ref[0]), (high, low))
    waves = dot_exact(split(both[: 2 * FREQ]), unfold_ref[...])
    spare_cos, spare_sin = both[2 * FREQ : 3 * FREQ], both[3 * FREQ :]
    coef_re, coef_im = coef_ref[0], coef_ref[1]
    last_cos = jnp.sum(coef_re * spare_cos - coef_im * spare_sin, 1, keepdims=True)
    last_sin = jnp.sum(coef_re * spare_sin + coef_im * spare_cos, 1, keepdims=True)
    first = lax.broadcasted_iota(jnp.int32, (FREQ, FREQ), 1) == 0
    cos_cos, cos_sin = waves[:FREQ, :FREQ], waves[:FREQ, FREQ:]
    sin_cos, sin_sin = waves[FREQ:, :FREQ], waves[FREQ:, FREQ:]
    out_ref[:FREQ] = cos_cos - sin_sin + jnp.where(first, last_sin, 0.0)
    out_ref[FREQ:] = jnp.where(first, last_cos, 0.0) - cos_sin - sin_cos


def field_body(place_ref, weight_ref, s0_ref, s1_ref, s2_ref, s3_ref, kern_ref, *refs):
    wh_ref, wl_ref, gh_ref, gl_ref, blur_ref, field_ref = refs[:6]
    piece_refs, (spec_ref, total_ref, rows_ref) = refs[6 : 6 + KERN], refs[6 + KERN :]
    step = pl.program_id(0)

    @pl.when(step == 0)
    def _():
        spec_ref[...] = (s0_ref[...] + s1_ref[...]) + (s2_ref[...] + s3_ref[...])

    spec_re = spec_ref[:FREQ]
    spec_im = spec_ref[FREQ:]
    near_re, near_im = [], []
    for index in range(2):
        kern_re, kern_im = kern_ref[index, 0], kern_ref[index, 1]
        near_re.append(kern_re * spec_re - kern_im * spec_im)
        near_im.append(kern_re * spec_im + kern_im * spec_re)
    near = jnp.concatenate([jnp.concatenate(near_re, 1), jnp.concatenate(near_im, 1)], 0)
    left = dot3((wh_ref[0], wl_ref[0]), split(near))
    lefts = []
    for index in range(2):
        lanes = slice(index * FREQ, (index + 1) * FREQ)
        for group in range(KERN):
            first = 2 * group * REACH
            re, im = left[first : first + REACH, lanes], left[first + REACH : first + 2 * REACH, lanes]
            lefts.append(jnp.concatenate([re, im], 1))
    field = dot3(split(jnp.concatenate(lefts, 0)), (gh_ref[...], gl_ref[...]))
    field_ref[...] = field
    power = field * field
    power = power[:, :COARSE] + power[:, COARSE:]
    half = KERN * REACH
    total = weight_ref[2 * step] * power[:half] + weight_ref[2 * step + 1] * power[half:]

    @pl.when(step == 0)
    def _():
        total_ref[...] = total

    @pl.when(step > 0)
    def _():
        total_ref[...] += total

    @pl.when(step == pl.num_programs(0) - 1)
    def _():
        rows_ref[...] = dot3(split(blur_ref[...]), split(total_ref[...]))
        for shift, piece_ref in enumerate(piece_refs):
            group = lax.rem(place_ref[0] + shift, KERN)
            piece_ref[...] = rows_ref[pl.ds(pl.multiple_of(group * ROWS, ROWS), ROWS)]


def own_body(r0_ref, r1_ref, r2_ref, r3_ref, oh_ref, ol_ref, out_ref, rows_ref):
    rows = (r0_ref[...] + r1_ref[...]) + (r2_ref[...] + r3_ref[...])
    rows_ref[...] = rows
    out_ref[...] = dot3(split(rows), (oh_ref[...], ol_ref[...]))


def sample_sums(noise_ref, place, acid, sums):
    sum_u, sum_q, sum_qu = sums
    quarter = 0.25 * acid
    base = acid - 2.0
    for index in range(noise_ref.shape[0]):
        noise = noise_ref[(index,) + place].astype(F32)
        u = jnp.tanh(quarter * noise + base)
        q = (1.0 - u * u) * (1.0 + 0.25 * noise)
        sum_u, sum_q, sum_qu = sum_u + u, sum_q + q, sum_qu + q * u
    return sum_u, sum_q, sum_qu


def places(columns):
    width = min(columns, LANES)
    for row in range(0, ROWS, 16):
        for col in range(0, columns, width):
            yield slice(row, row + 16), slice(col, col + width)


def dose_first_body(_, own_ref, other_ref, ch_ref, cl_ref, noise_ref, sums_ref, edge_ref):
    step = pl.program_id(0)
    last = pl.num_programs(0) - 1
    sums_ref[0] = own_ref[...]

    @pl.when(step == 0)
    def _():
        edge_ref[...] = dot3(split(other_ref[...]), (ch_ref[0], cl_ref[0]))
        sums_ref[0, :, :EDGE] += edge_ref[:, :EDGE]

    @pl.when(step == last)
    def _():
        sums_ref[0, :, CHUNK - EDGE :] += edge_ref[:, EDGE:]

    for place in places(CHUNK):
        acid = sums_ref[(0,) + place]
        zero = jnp.zeros(acid.shape, F32)
        for index, value in enumerate(sample_sums(noise_ref, place, acid, (zero, zero, zero))):
            sums_ref[(index + 1,) + place] = value


def acid_grads(sums_ref, target_ref, noise_ref, grad_ref):
    for place in places(grad_ref.shape[1]):
        acid, *sums = [sums_ref[(index,) + place] for index in range(4)]
        sum_u, sum_q, sum_qu = sample_sums(noise_ref, place, acid, sums)
        target = target_ref[place].astype(F32)
        inner = 0.25 - sum_u * (1.0 / SAMPLES) - 0.5 * target
        grad_ref[place] = (1.0 / 16.0) * (sum_q * inner + 1.25 * sum_qu)


def dose_edge_body(_, sums_ref, target_ref, noise_ref, ch_ref, cl_ref, send_ref, grad_ref):
    acid_grads(sums_ref, target_ref, noise_ref, grad_ref)
    part = dot3(split(grad_ref[...]), (ch_ref[0], cl_ref[0]))

    @pl.when(pl.program_id(0) == 0)
    def _():
        send_ref[...] = part

    @pl.when(pl.program_id(0) > 0)
    def _():
        send_ref[...] += part


def dose_body(sums_ref, target_ref, noise_ref, oh_ref, ol_ref, out_ref, grad_ref):
    acid_grads(sums_ref, target_ref, noise_ref, grad_ref)
    part = dot3(split(grad_ref[...]), (oh_ref[...], ol_ref[...]))

    @pl.when(pl.program_id(0) == 0)
    def _():
        out_ref[...] = part

    @pl.when(pl.program_id(0) > 0)
    def _():
        out_ref[...] += part


def back_body(place_ref, weight_ref, p0_ref, p1_ref, p2_ref, p3_ref, field_ref, kern_ref, *refs):
    wh_ref, wl_ref, gh_ref, gl_ref, blur_ref, th_ref, tl_ref, fold_ref, coef_ref = refs[:9]
    out_ref, rows_ref, grad_ref, sum_ref, table, table_sems = refs[9:]
    step = pl.program_id(0)
    fetches = [
        pltpu.make_async_copy(ref, table.at[index], table_sems.at[index])
        for index, ref in enumerate((th_ref, tl_ref))
    ]

    @pl.when(step == 0)
    def _():
        for fetch in fetches:
            fetch.start()
        for shift, piece_ref in enumerate((p0_ref, p1_ref, p2_ref, p3_ref)):
            group = lax.rem(place_ref[0] - shift + KERN, KERN)
            rows_ref[pl.ds(pl.multiple_of(group * ROWS, ROWS), ROWS)] = piece_ref[...]
        part = 2.0 * dot3(split(blur_ref[...]), split(rows_ref[...]))
        grad_ref[:, :COARSE] = part
        grad_ref[:, COARSE:] = part
        sum_ref[...] = jnp.zeros_like(sum_ref)

    grad = grad_ref[...]
    half = KERN * REACH
    pulled = jnp.concatenate(
        [
            field_ref[index * half : (index + 1) * half] * (weight_ref[2 * step + index] * grad)
            for index in range(2)
        ],
        0,
    )
    lefts = dot3(split(pulled), (gh_ref[...], gl_ref[...]))
    stack = []
    for index in range(2):
        column = []
        for group in range(KERN):
            first = index * half + group * REACH
            left = lefts[first : first + REACH]
            column += [left[:, :FREQ], left[:, FREQ:]]
        stack.append(jnp.concatenate(column, 0))
    near = dot3((wh_ref[0], wl_ref[0]), split(jnp.concatenate(stack, 1)))
    sum_re = sum_ref[:FREQ]
    sum_im = sum_ref[FREQ:]
    for index in range(2):
        near_re = near[:FREQ, index * FREQ : (index + 1) * FREQ]
        near_im = near[FREQ:, index * FREQ : (index + 1) * FREQ]
        kern_re, kern_im = kern_ref[index, 0], kern_ref[index, 1]
        sum_re = sum_re + (kern_re * near_re + kern_im * near_im)
        sum_im = sum_im + (kern_re * near_im - kern_im * near_re)
    sum_ref[:FREQ] = sum_re
    sum_ref[FREQ:] = sum_im

    @pl.when(step == pl.num_programs(0) - 1)
    def _():
        grad_re, grad_im = sum_re * (2.0 / PERIOD), sum_im * (2.0 / PERIOD)
        mix = jnp.concatenate(
            [jnp.concatenate([grad_re, -grad_im], 1), jnp.concatenate([-grad_im, -grad_re], 1)], 0
        )
        folded = dot_exact(split(mix), fold_ref[...])
        coef_re, coef_im = coef_ref[0], coef_ref[1]
        by_cos, by_sin = grad_im[:, :1], grad_re[:, :1]
        spare_cos = coef_re * by_cos + coef_im * by_sin
        spare_sin = coef_re * by_sin - coef_im * by_cos
        mixed = jnp.concatenate([folded, spare_cos, spare_sin], 0)
        for fetch in fetches:
            fetch.wait()
        spread = dot3((table[0], table[1]), split(mixed))
        out_ref[...] = spread.reshape(out_ref.shape)


def final_body(got_ref, basis_ref, wh_ref, wl_ref, last_ref, out_ref):
    total = got_ref[0]
    for index in range(1, got_ref.shape[0]):
        total = total + got_ref[index]
    basis = basis_ref[...]
    rows = dot3(split(basis[:, :RANK]), split(total))
    spare = jnp.sum(basis * total[RANK - 1 :], 1, keepdims=True)
    out_ref[...] = dot3(split(rows), (wh_ref[...], wl_ref[...])) + spare * last_ref[...]


def to_const(table):
    return hbm(*(jnp.asarray(part) for part in np_split(table)))


def shifted(values, shifts):
    count = lax.axis_size("kern")
    return [
        lax.ppermute(value, "kern", [(source, (source + shift) % count) for source in range(count)])
        for value, shift in zip(values, shifts)
    ]


def body(mask_values, kernels, weights, target, dose_noise):
    noise_count = lax.axis_size("noise")
    f32 = lambda *shape: jax.ShapeDtypeStruct(shape, F32)
    bf16 = lambda *shape: jax.ShapeDtypeStruct(shape, BF)
    smem = pl.BlockSpec(memory_space=pltpu.SMEM)
    columns = PERIOD // CHUNK
    shifts = range(1, KERN)

    def fixed(*shape):
        return pl.BlockSpec(shape, lambda i, *_: (0,) * len(shape))

    def chunk(rows):
        return pl.BlockSpec((rows, CHUNK), lambda i, *_: (0, i))

    def moved_spec(width):
        return pl.BlockSpec((noise_count // columns, ROWS, width), lambda i: (i, 0, 0))

    moved_first, moved = call(
        front_body,
        (bf16(noise_count, ROWS, PERIOD + FREQ), bf16(noise_count, ROWS, PERIOD)),
        (mask_values, jnp.asarray(BASIS.T[:RANK], F32), *to_const(LINE.T), jnp.asarray(LAST, F32), dose_noise),
        grid=(columns,),
        in_specs=[fixed(ROWS, PERIOD), fixed(RANK, ROWS)]
        + [fixed(PERIOD, FREQ)] * 2
        + [fixed(1, PERIOD), pl.BlockSpec((2, dose_noise.shape[1] // columns, PERIOD), lambda i: (0, i, 0))],
        out_specs=(moved_spec(PERIOD + FREQ), moved_spec(PERIOD)),
        scratch_shapes=[pltpu.VMEM((2 * RANK, FREQ), BF)],
    )
    place = jnp.stack([lax.axis_index(axis).astype(jnp.int32) for axis in ("kern", "noise", "tile")])
    moved_first, place = lax.optimization_barrier((moved_first, place))
    got = lax.all_to_all(moved_first, "noise", 0, 0, tiled=True)
    got, moved, kernels, weights, target, place = lax.optimization_barrier(
        (got, moved, kernels, weights, target, place)
    )
    got_last = lax.all_to_all(moved, "noise", 0, 0, tiled=True)

    def at_place(which, table):
        return [pl.BlockSpec((1,) + table.shape[1:], lambda i, place: (place[which], 0, 0))] * 2

    waves_t = WAVE.transpose(0, 2, 1)
    cross_t = CROSS.transpose(0, 2, 1)
    coef = hbm(jnp.asarray(COEF, F32))
    spec = call(
        spectrum_body,
        f32(2 * FREQ, FREQ),
        (got, *to_const(GATHER_OWN), *hbm(jnp.asarray(UNFOLD, BF)), *coef),
        place=place,
        grid=(1,),
        in_specs=[pl.BlockSpec((noise_count, ROWS, FREQ), lambda i, _: (0, 0, PERIOD // FREQ))]
        + at_place(0, GATHER_OWN)
        + [fixed(*UNFOLD.shape), fixed(*COEF.shape)],
        out_specs=fixed(2 * FREQ, FREQ),
    )
    specs = [spec] + shifted([spec] * len(shifts), shifts)
    pair_spec = pl.BlockSpec((2, 2, FREQ, FREQ), lambda i, *_: (i, 0, 0, 0))
    field_rows = 2 * KERN * REACH
    field_spec = pl.BlockSpec((field_rows, 2 * COARSE), lambda i, *_: (i, 0))
    field, *pieces = call(
        field_body,
        (f32(PAIRS * field_rows, 2 * COARSE),) + (f32(ROWS, COARSE),) * KERN,
        (weights, *specs, *hbm(kernels), *to_const(WAVE), *to_const(GRID), *hbm(jnp.asarray(BLUR, F32))),
        place=place,
        grid=(PAIRS,),
        in_specs=[smem]
        + [fixed(2 * FREQ, FREQ)] * KERN
        + [pair_spec]
        + at_place(1, WAVE)
        + [fixed(*GRID.shape)] * 2
        + [fixed(*BLUR.shape)],
        out_specs=(field_spec,) + (fixed(ROWS, COARSE),) * KERN,
        scratch_shapes=[
            pltpu.VMEM((2 * FREQ, FREQ), F32),
            pltpu.VMEM((KERN * REACH, COARSE), F32),
            pltpu.VMEM((KERN * ROWS, COARSE), F32),
        ],
    )
    pieces = pieces[:1] + shifted(pieces[1:], shifts)
    acid, rows = call(own_body, (f32(ROWS, PERIOD), f32(ROWS, COARSE)), (*pieces, *to_const(OWN.T)))
    swap = [(0, 1), (1, 0)]
    rows_other = lax.ppermute(rows, "tile", swap)
    got_spec = pl.BlockSpec((noise_count, ROWS, CHUNK), lambda i, *_: (0, 0, i))
    sums = call(
        dose_first_body,
        f32(4, ROWS, PERIOD),
        (acid, rows_other, *to_const(CROSS), got),
        place=place,
        grid=(columns,),
        in_specs=[chunk(ROWS), fixed(ROWS, COARSE)] + at_place(2, CROSS) + [got_spec],
        out_specs=pl.BlockSpec((4, ROWS, CHUNK), lambda i, *_: (0, 0, i)),
        scratch_shapes=[pltpu.VMEM((ROWS, 2 * EDGE), F32)],
    )
    far = PERIOD // EDGE - 1
    (target,) = hbm(target)
    (sums,) = vmem(sums)
    send = call(
        dose_edge_body,
        f32(ROWS, COARSE),
        (sums, target, got_last, *to_const(cross_t)),
        place=place,
        grid=(2,),
        in_specs=[
            pl.BlockSpec((4, ROWS, EDGE), lambda i, _: (0, 0, i * far)),
            pl.BlockSpec((ROWS, EDGE), lambda i, _: (0, i * far)),
            pl.BlockSpec((noise_count, ROWS, EDGE), lambda i, _: (0, 0, i * far)),
        ]
        + [pl.BlockSpec((1, EDGE, COARSE), lambda i, place: (place[2], i, 0))] * 2,
        out_specs=fixed(ROWS, COARSE),
        scratch_shapes=[pltpu.VMEM((ROWS, EDGE), F32)],
    )
    grad_other = lax.ppermute(send, "tile", swap)
    grad_own = call(
        dose_body,
        f32(ROWS, COARSE),
        (sums, target, got_last, *to_const(OWN)),
        grid=(columns,),
        in_specs=[pl.BlockSpec((4, ROWS, CHUNK), lambda i: (0, 0, i)), chunk(ROWS), got_spec]
        + [pl.BlockSpec((CHUNK, COARSE), lambda i: (i, 0))] * 2,
        out_specs=fixed(ROWS, COARSE),
        scratch_shapes=[pltpu.VMEM((ROWS, CHUNK), F32)],
    )
    grad = grad_own + grad_other
    grads = [grad] + shifted([grad] * len(shifts), shifts)
    spread = call(
        back_body,
        f32(BLOCKS, RANK, FREQ),
        (
            weights,
            *grads,
            *vmem(field),
            *hbm(kernels),
            *to_const(waves_t),
            *to_const(GRID.T),
            *hbm(jnp.asarray(BLUR.T, F32)),
            *to_const(GATHER.T),
            *hbm(jnp.asarray(UNFOLD.T, BF)),
            *coef,
        ),
        place=place,
        grid=(PAIRS,),
        in_specs=[smem]
        + [fixed(ROWS, COARSE)] * KERN
        + [field_spec, pair_spec]
        + at_place(1, waves_t)
        + [fixed(*GRID.T.shape)] * 2
        + [fixed(*BLUR.T.shape)]
        + [pl.BlockSpec(memory_space=pltpu.HBM)] * 2
        + [fixed(*UNFOLD.T.shape), fixed(*COEF.shape)],
        out_specs=fixed(BLOCKS, RANK, FREQ),
        scratch_shapes=[
            pltpu.VMEM((KERN * ROWS, COARSE), F32),
            pltpu.VMEM((KERN * REACH, 2 * COARSE), F32),
            pltpu.VMEM((2 * FREQ, FREQ), F32),
            pltpu.VMEM((2,) + GATHER.T.shape, BF),
            pltpu.SemaphoreType.DMA((2,)),
        ],
    )
    back = lax.all_to_all(spread, ("kern", "noise"), 0, 0, tiled=True)
    return call(
        final_body,
        f32(ROWS, PERIOD),
        (back, jnp.asarray(BASIS, F32), *to_const(LINE), jnp.asarray(LAST, F32)),
    )


def solution(mesh):
    return jax.shard_map(
        body,
        mesh=mesh,
        in_specs=(
            P(("kern", "noise"), "tile"),
            P("kern", None, None, None),
            P("kern"),
            P(("kern", "noise"), "tile"),
            P("noise", "kern", "tile"),
        ),
        out_specs=P(("kern", "noise"), "tile"),
        check_vma=False,
    )
```

time: 182 us -> 131 us (0.72)
  waiting for transfers between devices: 47 us -> 11.8 us
  local copies, waits for them, and re-layouts: 21.1 us -> 7.5 us
  between operations: 13.6 us -> 0.14 us
  Pallas kernels: 21.9 us -> 33.8 us
  starting transfers between devices: 16.3 us -> 19.5 us
  other arithmetic: 2.33 us -> 0.08 us
    all_to_all x2 -> x1, waiting for transfers between devices: 46.2 us -> 0.01 us  [body(): got_last = lax.all_to_all(moved, 'noise', 0, 0, tiled=True)]
    pallas_call x7 -> x9, Pallas kernels: 21.9 us -> 33.8 us  [the longest x5 22.2 us: call(): pl.pallas_call(body, out_shape=out_shape, compiler_params=params, grid_sp...]
    ppermute x0 -> x9, waiting for transfers between devices: none -> 10 us  [shifted(): lax.ppermute(value, 'kern', [(source, (source + shift) % count) for sourc...]
    ppermute x0 -> x9, starting transfers between devices: none -> 9.93 us  [shifted(): lax.ppermute(value, 'kern', [(source, (source + shift) % count) for sourc...]
    all_to_all x2 -> x1, starting transfers between devices: 11.1 us -> 4.56 us  [body(): got_last = lax.all_to_all(moved, 'noise', 0, 0, tiled=True)]
    unnamed x31 -> x20, local copies, waits for them, and re-layouts: 13.8 us -> 7.5 us
    all_to_all x1 -> x0, local copies, waits for them, and re-layouts: 4.22 us -> none  [body(): samples = lax.all_to_all(dose_noise, 'noise', 1, 0, tiled=True)]
    mul x1 -> x0, other arithmetic: 2.18 us -> none  [body(): scaled = kernels * jnp.sqrt(weights)[:, None, None, None]]
  transfers between devices with their start and end apart: 5 -> 12, of which waited for: 3 -> 8; matrix products, arithmetic and copies ran while one was open for 8% -> 0% of each run, Pallas kernels for 4% -> 15%
where the time goes in v2:
time: 131 us
  blocking collectives  57.9 us (44%)
  Pallas kernels  33.8 us (26%)
  starting transfers between devices  19.5 us (15%)
  waiting for transfers between devices  11.8 us (9%)
  local copies, waits for them, and re-layouts  7.5 us (6%)
    all_to_all x1, blocking collectives, body(): got = lax.all_to_all(moved_first, 'noise', 0, 0, tiled=True)  37.1 us
    pallas_call x5, Pallas kernels, call(): pl.pallas_call(body, out_shape=out_shape, compiler_params=params, grid_sp...  22.2 us
    all_to_all x1, blocking collectives, body(): back = lax.all_to_all(spread, ('kern', 'noise'), 0, 0, tiled=True)  20.8 us
    pallas_call x4, Pallas kernels, call(): pl.pallas_call(body, out_shape=out_shape, compiler_params=params, **kw)  11.6 us
    ppermute x9, waiting for transfers between devices, shifted(): lax.ppermute(value, 'kern', [(source, (source + shift) % count) for sourc...  10 us
    ppermute x9, starting transfers between devices, shifted(): lax.ppermute(value, 'kern', [(source, (source + shift) % count) for sourc...  9.93 us
    unnamed x20, local copies, waits for them, and re-layouts  7.5 us
    all_to_all x1, starting transfers between devices, body(): got_last = lax.all_to_all(moved, 'noise', 0, 0, tiled=True)  4.56 us
  transfers between devices with their start and end apart: 12, of which 8 were waited for; matrix products, arithmetic and copies ran while one was open for 0% of the time, Pallas kernels for 15%

profile of v2, /device:TPU:1, one launch (start us, length us, event | category | flops | bytes accessed | tf_op | source)
XLA Modules:
  0.0 130.8 jit_solution(5764809419159703532)
XLA Ops:
  0.0 0.1 pad_add_fusion._.place_ref
  0.1 0.0 copy-start
  0.1 2.2 %copy-done = bf16[2,512,2048]{2,1,0:T(8,128)(2,1)S(1)} copy-done((bf16[2,512,2048]{2,1,0:T(8,128)(2,1)S(1)}, bf16[2,512,2048]{2,1,0:T(8,128)(2,1)}, u32[]{:S(2)}) %copy-start) | copy-done | bytes 4194328
  2.3 0.0 copy-start.4
  2.3 0.9 copy-done.4
  3.2 0.0 copy-start.5
  3.2 0.7 copy-done.5
  3.9 0.0 copy-start.8
  3.9 0.7 copy-done.8
  4.6 2.3 %shard_map.352 = (bf16[16,32,2176]{2,1,0:T(8,128)(2,1)S(1)}, bf16[16,32,2048]{2,1,0:T(8,128)(2,1)S(1)}) custom-call(f32[32,2048]{1,0:T(8,128)S(1)} %copy-done.4, f32[16,32]{1,0:T(8,128)S(1)} %copy-done.8, bf16[2048,128]{1,0:T(8,128)(2,1)} %constant.80.clone.lh_ref, bf16[2048,128]{1,0:T(8,128)(2,1)} %constant.81.clone.ll_ref, f32[1,2048]{1,0:T(1,128)S(1)} %copy-done.5, ...), custom_call_target="tpu_custom_call" | custom-call | tf_op jit(solution)/shard_map/pallas_call | solution.py:147
  6.9 0.0 copy-start.3
  6.9 1.3 %copy-done.3 = bf16[16,32,2048]{2,1,0:T(8,128)(2,1)} copy-done((bf16[16,32,2048]{2,1,0:T(8,128)(2,1)}, bf16[16,32,2048]{2,1,0:T(8,128)(2,1)S(1)}, u32[]{:S(2)}) %copy-start.3) | copy-done | bytes 2097176
  8.3 37.1 %all_to_all.15.got_ref.noise_ref = bf16[16,32,2176]{2,1,0:T(8,128)(2,1)S(1)} all-to-all(bf16[16,32,2176]{2,1,0:T(8,128)(2,1)S(1)} %get-tuple-element.23), channel_id=1, replica_groups=mesh['tile'=2,'kern'=4,'noise'=16] {'noise'}, dimensions={0} | all-to-all | bytes 4456448 | tf_op jit(solution)/shard_map/all_to_all | solution.py:451
  45.4 0.0 copy-start.9
  45.4 4.6 %all-to-all-start.1 = ((bf16[16,32,2048]{2,1,0:T(8,128)(2,1)}), bf16[16,32,2048]{2,1,0:T(8,128)(2,1)}, u32[]{:S(2)}, u32[]{:S(2)}) async-start(bf16[16,32,2048]{2,1,0:T(8,128)(2,1)} %copy-done.3), calls=%async_computation.1 | async-start | bytes 4194304 | tf_op jit(solution)/shard_map/all_to_all | solution.py:455
  50.0 2.2 %shard_map.353.s0_ref = f32[256,128]{1,0:T(8,128)S(1)} custom-call(s32[3]{0:T(128)S(1)} %pad_add_fusion._.place_ref, bf16[16,32,2176]{2,1,0:T(8,128)(2,1)S(1)} %all_to_all.15.got_ref.noise_ref, bf16[4,512,256]{2,1,0:T(8,128)(2,1)} %constant.84.clone.gh_ref, bf16[4,512,256]{2,1,0:T(8,128)(2,1)} %constant.85.clone.gl_ref, ...), custom_call_target="tpu_custom_call" | custom-call | tf_op jit(solution)/shard_map/pallas_call | solution.py:149
  52.2 2.1 %collective-permute-start.2 = (f32[256,128]{1,0:T(8,128)S(1)}, f32[256,128]{1,0:T(8,128)S(1)}, u32[]{:S(2)}, u32[]{:S(2)}) collective-permute-start(f32[256,128]{1,0:T(8,128)S(1)} %shard_map.353.s0_ref), channel_id=1, source_target_pairs={{0,48},{16,0},{32,16},{48,32},{1,49},{17,1},{33,17},{49,33},{2,50}... | collective-permute-start | bytes 393224 | tf_op jit(solution)/shard_map/ppermute | solution.py:416
  54.3 1.2 collective-permute-start.1
  55.5 0.5 collective-permute-start
  56.0 3.7 %collective-permute-done.2.s3_ref = f32[256,128]{1,0:T(8,128)S(1)} collective-permute-done((f32[256,128]{1,0:T(8,128)S(1)}, f32[256,128]{1,0:T(8,128)S(1)}, u32[]{:S(2)}, u32[]{:S(2)}) %collective-permute-start.2) | collective-permute-done | bytes 131104 | tf_op jit(solution)/shard_map/ppermute | solution.py:416
  59.8 0.2 collective-permute-done.1.s2_ref
  59.9 0.7 collective-permute-done.s1_ref
  60.6 0.0 copy-done.9
  60.6 6.2 %shard_map.354 = (f32[1536,512]{1,0:T(8,128)S(1)}, f32[32,256]{1,0:T(8,128)S(1)}, f32[32,256]{1,0:T(8,128)S(1)}, f32[32,256]{1,0:T(8,128)S(1)}, f32[32,256]{1,0:T(8,128)S(1)}) custom-call(s32[3]{0:T(128)S(1)} %pad_add_fusion._.place_ref, f32[6]{0:T(128)S(1)} %copy-done.9, f32[256,128]{1,0:T(8,128)S(1)} %shard_map.353.s0_ref, ...), custom_call_target="tpu_custom_call" | custom-call | tf_op jit(solution)/shard_map/pallas_call | solution.py:149
  66.8 0.0 copy-start.1
  66.8 1.6 %copy-done.1 = f32[1536,512]{1,0:T(8,128)} copy-done((f32[1536,512]{1,0:T(8,128)}, f32[1536,512]{1,0:T(8,128)S(1)}, u32[]{:S(2)}) %copy-start.1) | copy-done | bytes 3145752
  68.4 2.5 %collective-permute-start.3 = (f32[32,256]{1,0:T(8,128)S(1)}, f32[32,256]{1,0:T(8,128)S(1)}, u32[]{:S(2)}, u32[]{:S(2)}) collective-permute-start(f32[32,256]{1,0:T(8,128)S(1)} %get-tuple-element.31), channel_id=1, source_target_pairs={{0,16},{16,32},{32,48},{48,0},{1,17},{17,33},{33,49},{49,1},{2,18}... | collective-permute-start | bytes 98312 | tf_op jit(solution)/shard_map/ppermute | solution.py:416
  70.9 1.2 collective-permute-start.4
  72.1 0.0 collective-permute-start.5
  72.1 0.0 collective-permute-done.3.r1_ref
  72.1 2.2 %collective-permute-done.4.r2_ref = f32[32,256]{1,0:T(8,128)S(1)} collective-permute-done((f32[32,256]{1,0:T(8,128)S(1)}, f32[32,256]{1,0:T(8,128)S(1)}, u32[]{:S(2)}, u32[]{:S(2)}) %collective-permute-start.4) | collective-permute-done | bytes 32800 | tf_op jit(solution)/shard_map/ppermute | solution.py:416
  74.3 1.5 %collective-permute-done.5.r3_ref = f32[32,256]{1,0:T(8,128)S(1)} collective-permute-done((f32[32,256]{1,0:T(8,128)S(1)}, f32[32,256]{1,0:T(8,128)S(1)}, u32[]{:S(2)}, u32[]{:S(2)}) %collective-permute-start.5) | collective-permute-done | bytes 32800 | tf_op jit(solution)/shard_map/ppermute | solution.py:416
  75.8 2.2 %shard_map.355 = (f32[32,2048]{1,0:T(8,128)S(1)}, f32[32,256]{1,0:T(8,128)S(1)}) custom-call(f32[32,256]{1,0:T(8,128)S(1)} %get-tuple-element.30.r0_ref, f32[32,256]{1,0:T(8,128)S(1)} %collective-permute-done.3.r1_ref, f32[32,256]{1,0:T(8,128)S(1)} %collective-permute-done.4.r2_ref, f32[32,256]{1,0:T(8,128)S(1)} %collective-permute-done.5.r3_ref, ...), custom_call_target="tpu_custom_call" | custom-call | tf_op jit(solution)/shard_map/pallas_call | solution.py:147
  78.0 2.5 %collective-permute-start.6 = (f32[32,256]{1,0:T(8,128)S(1)}, f32[32,256]{1,0:T(8,128)S(1)}, u32[]{:S(2)}, u32[]{:S(2)}) collective-permute-start(f32[32,256]{1,0:T(8,128)S(1)} %get-tuple-element.35), channel_id=1, source_target_pairs={{0,64},{64,0},{1,65},{65,1},{2,66},{66,2},{3,67},{67,3},{4,68},{68... | collective-permute-start | bytes 98312 | tf_op jit(solution)/shard_map/ppermute | solution.py:500
  80.5 1.8 %collective-permute-done.6.other_ref = f32[32,256]{1,0:T(8,128)S(1)} collective-permute-done((f32[32,256]{1,0:T(8,128)S(1)}, f32[32,256]{1,0:T(8,128)S(1)}, u32[]{:S(2)}, u32[]{:S(2)}) %collective-permute-start.6) | collective-permute-done | bytes 32800 | tf_op jit(solution)/shard_map/ppermute | solution.py:500
  82.3 4.1 %shard_map.356.sums_ref = f32[4,32,2048]{2,1,0:T(8,128)S(1)} custom-call(s32[3]{0:T(128)S(1)} %pad_add_fusion._.place_ref, f32[32,2048]{1,0:T(8,128)S(1)} %get-tuple-element.34.own_ref, f32[32,256]{1,0:T(8,128)S(1)} %collective-permute-done.6.other_ref, bf16[2,256,256]{2,1,0:T(8,128)(2,1)} %constant.94.clone.ch_ref, ...), custom_call_target="tpu_custom_call" | custom-call | tf_op jit(solution)/shard_map/pallas_call | solution.py:149
  86.5 0.0 all-to-all-done.1.noise_ref
  86.5 0.0 copy-start.2
  86.5 2.4 %shard_map.358 = f32[32,256]{1,0:T(8,128)S(1)} custom-call(s32[3]{0:T(128)S(1)} %pad_add_fusion._.place_ref, f32[4,32,2048]{2,1,0:T(8,128)S(1)} %shard_map.356.sums_ref, bf16[32,2048]{1,0:T(8,128)(2,1)} %target_ref.1, bf16[16,32,2048]{2,1,0:T(8,128)(2,1)} %all-to-all-done.1.noise_ref, bf16[2,256,256]{2,1,0:T(8,128)(2,1)} %constant.96.clone.ch_ref, ...), custom_call_target="tpu_custom_call" | custom-call | tf_op jit(solution)/shard_map/pallas_call | solution.py:149
  88.9 2.5 %collective-permute-start.7 = (f32[32,256]{1,0:T(8,128)S(1)}, f32[32,256]{1,0:T(8,128)S(1)}, u32[]{:S(2)}, u32[]{:S(2)}) collective-permute-start(f32[32,256]{1,0:T(8,128)S(1)} %shard_map.358), channel_id=1, source_target_pairs={{0,64},{64,0},{1,65},{65,1},{2,66},{66,2},{3,67},{67,3},{4,68},{68... | collective-permute-start | bytes 98312 | tf_op jit(solution)/shard_map/ppermute | solution.py:530
  91.4 4.7 %shard_map.357 = f32[32,256]{1,0:T(8,128)S(1)} custom-call(f32[4,32,2048]{2,1,0:T(8,128)S(1)} %shard_map.356.sums_ref, bf16[32,2048]{1,0:T(8,128)(2,1)} %target_ref.1, bf16[16,32,2048]{2,1,0:T(8,128)(2,1)} %all-to-all-done.1.noise_ref, bf16[2048,256]{1,0:T(8,128)(2,1)} %constant.98.clone.oh_ref, bf16[2048,256]{1,0:T(8,128)(2,1)} %constant.99.clone.ol_ref), custom_call_target="tpu_custom_call" | custom-call | tf_op jit(solution)/shard_map/pallas_call | solution.py:147
  96.1 0.0 collective-permute-done.7
  96.1 0.6 collective-permute-start.10
  96.8 0.0 collective-permute-start.9
  96.8 1.7 %collective-permute-start.8 = (f32[32,256]{1,0:T(8,128)S(1)}, f32[32,256]{1,0:T(8,128)S(1)}, u32[]{:S(2)}, u32[]{:S(2)}) collective-permute-start(f32[32,256]{1,0:T(8,128)S(1)} %add.3.p0_ref), channel_id=1, source_target_pairs={{0,16},{16,32},{32,48},{48,0},{1,17},{17,33},{33,49},{49,1},{2,18}... | collective-permute-start | bytes 98312 | tf_op jit(solution)/shard_map/ppermute | solution.py:416
  98.5 1.4 %collective-permute-done.10.p3_ref = f32[32,256]{1,0:T(8,128)S(1)} collective-permute-done((f32[32,256]{1,0:T(8,128)S(1)}, f32[32,256]{1,0:T(8,128)S(1)}, u32[]{:S(2)}, u32[]{:S(2)}) %collective-permute-start.10) | collective-permute-done | bytes 32800 | tf_op jit(solution)/shard_map/ppermute | solution.py:416
  99.9 0.3 collective-permute-done.9.p2_ref
  100.2 0.0 collective-permute-done.8.p1_ref
  100.2 0.0 copy-done.2
  100.2 0.0 copy-start.6
  100.2 0.0 copy-start.7
  100.2 7.4 %shard_map.359 = f32[64,16,128]{2,1,0:T(8,128)S(1)} custom-call(s32[3]{0:T(128)S(1)} %pad_add_fusion._.place_ref, f32[6]{0:T(128)S(1)} %copy-done.9, f32[32,256]{1,0:T(8,128)S(1)} %add.3.p0_ref, f32[32,256]{1,0:T(8,128)S(1)} %collective-permute-done.8.p1_ref, f32[32,256]{1,0:T(8,128)S(1)} %collective-permute-done.9.p2_ref, ...), custom_call_target="tpu_custom_call" | custom-call | tf_op jit(solution)/shard_map/pallas_call | solution.py:149
  107.6 20.8 %all_to_all.16.got_ref = f32[64,16,128]{2,1,0:T(8,128)S(1)} all-to-all(f32[64,16,128]{2,1,0:T(8,128)S(1)} %shard_map.359), channel_id=1, replica_groups=mesh['tile'=2,'kern'=4,'noise'=16] {'kern','noise'}, dimensions={0} | all-to-all | bytes 1048576 | tf_op jit(solution)/shard_map/all_to_all | solution.py:577
  128.3 0.0 copy-done.6
  128.3 0.0 copy-done.7
  128.3 2.4 %shard_map.360 = f32[32,2048]{1,0:T(8,128)} custom-call(f32[64,16,128]{2,1,0:T(8,128)S(1)} %all_to_all.16.got_ref, f32[32,128]{1,0:T(8,128)S(1)} %copy-done.7, bf16[128,2048]{1,0:T(8,128)(2,1)} %constant.109.clone.wh_ref, bf16[128,2048]{1,0:T(8,128)(2,1)} %constant.110.clone.wl_ref, f32[1,2048]{1,0:T(1,128)S(1)} %copy-done.6), custom_call_target="tpu_custom_call" | custom-call | tf_op jit(solution)/shard_map/pallas_call | solution.py:147
  (1 shorter events, 0.0 us)
Async XLA Ops:
  0.1 2.2 %copy-start = (bf16[2,512,2048]{2,1,0:T(8,128)(2,1)S(1)}, bf16[2,512,2048]{2,1,0:T(8,128)(2,1)}, u32[]{:S(2)}) copy-start(bf16[2,512,2048]{2,1,0:T(8,128)(2,1)} %noise_ref.1) | copy-start | bytes 12582916
  2.3 0.9 copy-start.4
  3.2 0.7 copy-start.5
  3.9 0.7 copy-start.8
  6.9 1.3 %copy-start.3 = (bf16[16,32,2048]{2,1,0:T(8,128)(2,1)}, bf16[16,32,2048]{2,1,0:T(8,128)(2,1)S(1)}, u32[]{:S(2)}) copy-start(bf16[16,32,2048]{2,1,0:T(8,128)(2,1)S(1)} %get-tuple-element.37) | copy-start | bytes 6291460
  45.4 15.2 %copy-start.9 = (f32[6]{0:T(128)S(1)}, f32[6]{0:T(128)}, u32[]{:S(2)}) copy-start(f32[6]{0:T(128)} %weight_ref.1) | copy-start | bytes 76
  45.4 41.1 %all-to-all-start.1 = ((bf16[16,32,2048]{2,1,0:T(8,128)(2,1)}), bf16[16,32,2048]{2,1,0:T(8,128)(2,1)}, u32[]{:S(2)}, u32[]{:S(2)}) async-start(bf16[16,32,2048]{2,1,0:T(8,128)(2,1)} %copy-done.3), calls=%async_computation.1 | async-start | bytes 4194304 | tf_op jit(solution)/shard_map/all_to_all | solution.py:455
  52.2 7.6 %collective-permute-start.2 = (f32[256,128]{1,0:T(8,128)S(1)}, f32[256,128]{1,0:T(8,128)S(1)}, u32[]{:S(2)}, u32[]{:S(2)}) collective-permute-start(f32[256,128]{1,0:T(8,128)S(1)} %shard_map.353.s0_ref), channel_id=1, source_target_pairs={{0,48},{16,0},{32,16},{48,32},{1,49},{17,1},{33,17},{49,33},{2,50}... | collective-permute-start | bytes 393224 | tf_op jit(solution)/shard_map/ppermute | solution.py:416
  54.3 5.6 %collective-permute-start.1 = (f32[256,128]{1,0:T(8,128)S(1)}, f32[256,128]{1,0:T(8,128)S(1)}, u32[]{:S(2)}, u32[]{:S(2)}) collective-permute-start(f32[256,128]{1,0:T(8,128)S(1)} %shard_map.353.s0_ref), channel_id=1, source_target_pairs={{0,32},{16,48},{32,0},{48,16},{1,33},{17,49},{33,1},{49,17},{2,34}... | collective-permute-start | bytes 393224 | tf_op jit(solution)/shard_map/ppermute | solution.py:416
  55.5 5.1 %collective-permute-start = (f32[256,128]{1,0:T(8,128)S(1)}, f32[256,128]{1,0:T(8,128)S(1)}, u32[]{:S(2)}, u32[]{:S(2)}) collective-permute-start(f32[256,128]{1,0:T(8,128)S(1)} %shard_map.353.s0_ref), channel_id=1, source_target_pairs={{0,16},{16,32},{32,48},{48,0},{1,17},{17,33},{33,49},{49,1},{2,18}... | collective-permute-start | bytes 393224 | tf_op jit(solution)/shard_map/ppermute | solution.py:416
  66.8 1.6 %copy-start.1 = (f32[1536,512]{1,0:T(8,128)}, f32[1536,512]{1,0:T(8,128)S(1)}, u32[]{:S(2)}) copy-start(f32[1536,512]{1,0:T(8,128)S(1)} %get-tuple-element.38.field_ref) | copy-start | bytes 9437188
  68.4 3.7 %collective-permute-start.3 = (f32[32,256]{1,0:T(8,128)S(1)}, f32[32,256]{1,0:T(8,128)S(1)}, u32[]{:S(2)}, u32[]{:S(2)}) collective-permute-start(f32[32,256]{1,0:T(8,128)S(1)} %get-tuple-element.31), channel_id=1, source_target_pairs={{0,16},{16,32},{32,48},{48,0},{1,17},{17,33},{33,49},{49,1},{2,18}... | collective-permute-start | bytes 98312 | tf_op jit(solution)/shard_map/ppermute | solution.py:416
  70.9 3.4 %collective-permute-start.4 = (f32[32,256]{1,0:T(8,128)S(1)}, f32[32,256]{1,0:T(8,128)S(1)}, u32[]{:S(2)}, u32[]{:S(2)}) collective-permute-start(f32[32,256]{1,0:T(8,128)S(1)} %get-tuple-element.32), channel_id=1, source_target_pairs={{0,32},{16,48},{32,0},{48,16},{1,33},{17,49},{33,1},{49,17},{2,34}... | collective-permute-start | bytes 98312 | tf_op jit(solution)/shard_map/ppermute | solution.py:416
  72.1 3.7 %collective-permute-start.5 = (f32[32,256]{1,0:T(8,128)S(1)}, f32[32,256]{1,0:T(8,128)S(1)}, u32[]{:S(2)}, u32[]{:S(2)}) collective-permute-start(f32[32,256]{1,0:T(8,128)S(1)} %get-tuple-element.33), channel_id=1, source_target_pairs={{0,48},{16,0},{32,16},{48,32},{1,49},{17,1},{33,17},{49,33},{2,50}... | collective-permute-start | bytes 98312 | tf_op jit(solution)/shard_map/ppermute | solution.py:416
  78.0 4.3 %collective-permute-start.6 = (f32[32,256]{1,0:T(8,128)S(1)}, f32[32,256]{1,0:T(8,128)S(1)}, u32[]{:S(2)}, u32[]{:S(2)}) collective-permute-start(f32[32,256]{1,0:T(8,128)S(1)} %get-tuple-element.35), channel_id=1, source_target_pairs={{0,64},{64,0},{1,65},{65,1},{2,66},{66,2},{3,67},{67,3},{4,68},{68... | collective-permute-start | bytes 98312 | tf_op jit(solution)/shard_map/ppermute | solution.py:500
  86.5 13.7 %copy-start.2 = (f32[1536,512]{1,0:T(8,128)S(1)}, f32[1536,512]{1,0:T(8,128)}, u32[]{:S(2)}) copy-start(f32[1536,512]{1,0:T(8,128)} %copy-done.1) | copy-start | bytes 9437188
  88.9 7.2 %collective-permute-start.7 = (f32[32,256]{1,0:T(8,128)S(1)}, f32[32,256]{1,0:T(8,128)S(1)}, u32[]{:S(2)}, u32[]{:S(2)}) collective-permute-start(f32[32,256]{1,0:T(8,128)S(1)} %shard_map.358), channel_id=1, source_target_pairs={{0,64},{64,0},{1,65},{65,1},{2,66},{66,2},{3,67},{67,3},{4,68},{68... | collective-permute-start | bytes 98312 | tf_op jit(solution)/shard_map/ppermute | solution.py:530
  96.1 3.7 %collective-permute-start.10 = (f32[32,256]{1,0:T(8,128)S(1)}, f32[32,256]{1,0:T(8,128)S(1)}, u32[]{:S(2)}, u32[]{:S(2)}) collective-permute-start(f32[32,256]{1,0:T(8,128)S(1)} %add.3.p0_ref), channel_id=1, source_target_pairs={{0,48},{16,0},{32,16},{48,32},{1,49},{17,1},{33,17},{49,33},{2,50}... | collective-permute-start | bytes 98312 | tf_op jit(solution)/shard_map/ppermute | solution.py:416
  96.8 3.4 %collective-permute-start.9 = (f32[32,256]{1,0:T(8,128)S(1)}, f32[32,256]{1,0:T(8,128)S(1)}, u32[]{:S(2)}, u32[]{:S(2)}) collective-permute-start(f32[32,256]{1,0:T(8,128)S(1)} %add.3.p0_ref), channel_id=1, source_target_pairs={{0,32},{16,48},{32,0},{48,16},{1,33},{17,49},{33,1},{49,17},{2,34}... | collective-permute-start | bytes 98312 | tf_op jit(solution)/shard_map/ppermute | solution.py:416
  96.8 3.4 %collective-permute-start.8 = (f32[32,256]{1,0:T(8,128)S(1)}, f32[32,256]{1,0:T(8,128)S(1)}, u32[]{:S(2)}, u32[]{:S(2)}) collective-permute-start(f32[32,256]{1,0:T(8,128)S(1)} %add.3.p0_ref), channel_id=1, source_target_pairs={{0,16},{16,32},{32,48},{48,0},{1,17},{17,33},{33,49},{49,1},{2,18}... | collective-permute-start | bytes 98312 | tf_op jit(solution)/shard_map/ppermute | solution.py:416
  100.2 28.1 %copy-start.6 = (f32[1,2048]{1,0:T(1,128)S(1)}, f32[1,2048]{1,0:T(1,128)}, u32[]{:S(2)}) copy-start(f32[1,2048]{1,0:T(1,128)} %constant.82.clone.last_ref) | copy-start | bytes 24580
  100.2 28.1 %copy-start.7 = (f32[32,128]{1,0:T(8,128)S(1)}, f32[32,128]{1,0:T(8,128)}, u32[]{:S(2)}) copy-start(f32[32,128]{1,0:T(8,128)} %constant.108.clone.basis_ref) | copy-start | bytes 49156

commit v3 on v2

--- a/solution.py
+++ b/solution.py
@@ -114,6 +114,12 @@
 )
 WAVE = WAVE.reshape(KERN, GROUP_BLOCKS, 2 * REACH, 2 * FREQ).transpose(1, 0, 2, 3)
 WAVE = WAVE.reshape(GROUP_BLOCKS, KERN * 2 * REACH, 2 * FREQ)
+LOW = 4
+HIGH = RANK - LOW
+SPREAD = GATHER.reshape(4 * FREQ, BLOCKS, RANK)
+SPREAD = np.concatenate([SPREAD[:, :, : HIGH - 1], SPREAD[:, :, RANK - 1 :], SPREAD[:, :, :LOW]], 2)
+SPREAD = SPREAD.reshape(4 * FREQ, BLOCKS * RANK).T
+BASIS_BACK = np.concatenate([BASIS[:, : HIGH - 1], np.zeros((ROWS, 1)), BASIS[:, :LOW]], 1)
 GATHER_OWN = GATHER.reshape(4 * FREQ, KERN, GROUP_BLOCKS * RANK).transpose(1, 0, 2)
 BLUR = np.kron(np.eye(KERN), ROW_BLUR)
 
@@ -133,7 +139,11 @@
     def one(a, b):
         return lax.dot_general(a, b, NN, preferred_element_type=F32)
 
-    return one(lh, rh) + (one(lh, rl) + one(ll, rh))
+    count = lh.shape[0]
+    if count > 64:
+        return one(lh, rh) + (one(lh, rl) + one(ll, rh))
+    both = one(jnp.concatenate([lh, ll], 0), rh)
+    return both[:count] + (one(lh, rl) + both[count:])
 
 
 def dot_exact(left, right):
@@ -246,12 +256,6 @@
             piece_ref[...] = rows_ref[pl.ds(pl.multiple_of(group * ROWS, ROWS), ROWS)]
 
 
-def own_body(r0_ref, r1_ref, r2_ref, r3_ref, oh_ref, ol_ref, out_ref, rows_ref):
-    rows = (r0_ref[...] + r1_ref[...]) + (r2_ref[...] + r3_ref[...])
-    rows_ref[...] = rows
-    out_ref[...] = dot3(split(rows), (oh_ref[...], ol_ref[...]))
-
-
 def sample_sums(noise_ref, place, acid, sums):
     sum_u, sum_q, sum_qu = sums
     quarter = 0.25 * acid
@@ -271,20 +275,8 @@
             yield slice(row, row + 16), slice(col, col + width)
 
 
-def dose_first_body(_, own_ref, other_ref, ch_ref, cl_ref, noise_ref, sums_ref, edge_ref):
-    step = pl.program_id(0)
-    last = pl.num_programs(0) - 1
-    sums_ref[0] = own_ref[...]
-
-    @pl.when(step == 0)
-    def _():
-        edge_ref[...] = dot3(split(other_ref[...]), (ch_ref[0], cl_ref[0]))
-        sums_ref[0, :, :EDGE] += edge_ref[:, :EDGE]
-
-    @pl.when(step == last)
-    def _():
-        sums_ref[0, :, CHUNK - EDGE :] += edge_ref[:, EDGE:]
-
+def dose_first_body(rows_ref, oh_ref, ol_ref, noise_ref, sums_ref):
+    sums_ref[0] = dot3(split(rows_ref[...]), (oh_ref[...], ol_ref[...]))
     for place in places(CHUNK):
         acid = sums_ref[(0,) + place]
         zero = jnp.zeros(acid.shape, F32)
@@ -292,37 +284,55 @@
             sums_ref[(index + 1,) + place] = value
 
 
-def acid_grads(sums_ref, target_ref, noise_ref, grad_ref):
-    for place in places(grad_ref.shape[1]):
+def acid_grad(sums, target):
+    sum_u, sum_q, sum_qu = sums
+    inner = 0.25 - sum_u * (1.0 / SAMPLES) - 0.5 * target.astype(F32)
+    return (1.0 / 16.0) * (sum_q * inner + 1.25 * sum_qu)
+
+
+def dose_edge_body(
+    _, acid_ref, other_ref, target_ref, first_ref, second_ref, ch_ref, cl_ref, th_ref, tl_ref, grad_ref, send_ref
+):
+    halo = dot3(split(other_ref[...]), (ch_ref[0], cl_ref[0]))
+    for place in places(EDGE):
+        acid = acid_ref[(0,) + place] + halo[place]
+        zero = jnp.zeros(acid.shape, F32)
+        sums = sample_sums(first_ref, place, acid, (zero, zero, zero))
+        sums = sample_sums(second_ref, place, acid, sums)
+        grad_ref[place] = acid_grad(sums, target_ref[place])
+    part = dot3(split(grad_ref[...]), (th_ref[0], tl_ref[0]))
+
+    @pl.when(pl.program_id(0) == 0)
+    def _():
+        send_ref[...] = part
+
+    @pl.when(pl.program_id(0) > 0)
+    def _():
+        send_ref[...] += part
+
+
+def dose_body(sums_ref, edge_ref, target_ref, noise_ref, oh_ref, ol_ref, out_ref, grad_ref):
+    step = pl.program_id(0)
+    for place in places(CHUNK):
         acid, *sums = [sums_ref[(index,) + place] for index in range(4)]
-        sum_u, sum_q, sum_qu = sample_sums(noise_ref, place, acid, sums)
-        target = target_ref[place].astype(F32)
-        inner = 0.25 - sum_u * (1.0 / SAMPLES) - 0.5 * target
-        grad_ref[place] = (1.0 / 16.0) * (sum_q * inner + 1.25 * sum_qu)
-
-
-def dose_edge_body(_, sums_ref, target_ref, noise_ref, ch_ref, cl_ref, send_ref, grad_ref):
-    acid_grads(sums_ref, target_ref, noise_ref, grad_ref)
-    part = dot3(split(grad_ref[...]), (ch_ref[0], cl_ref[0]))
-
-    @pl.when(pl.program_id(0) == 0)
-    def _():
-        send_ref[...] = part
-
-    @pl.when(pl.program_id(0) > 0)
-    def _():
-        send_ref[...] += part
-
-
-def dose_body(sums_ref, target_ref, noise_ref, oh_ref, ol_ref, out_ref, grad_ref):
-    acid_grads(sums_ref, target_ref, noise_ref, grad_ref)
+        sums = sample_sums(noise_ref, place, acid, sums)
+        grad_ref[place] = acid_grad(sums, target_ref[place])
+
+    @pl.when(step == 0)
+    def _():
+        grad_ref[:, :EDGE] = edge_ref[:, :EDGE]
+
+    @pl.when(step == pl.num_programs(0) - 1)
+    def _():
+        grad_ref[:, CHUNK - EDGE :] = edge_ref[:, EDGE:]
+
     part = dot3(split(grad_ref[...]), (oh_ref[...], ol_ref[...]))
 
-    @pl.when(pl.program_id(0) == 0)
+    @pl.when(step == 0)
     def _():
         out_ref[...] = part
 
-    @pl.when(pl.program_id(0) > 0)
+    @pl.when(step > 0)
     def _():
         out_ref[...] += part
 
@@ -392,17 +402,17 @@
         mixed = jnp.concatenate([folded, spare_cos, spare_sin], 0)
         for fetch in fetches:
             fetch.wait()
-        spread = dot3((table[0], table[1]), split(mixed))
-        out_ref[...] = spread.reshape(out_ref.shape)
-
-
-def final_body(got_ref, basis_ref, wh_ref, wl_ref, last_ref, out_ref):
-    total = got_ref[0]
+        high, low = split(dot3((table[0], table[1]), split(mixed)).reshape(out_ref.shape))
+        row = lax.broadcasted_iota(jnp.int32, out_ref.shape, 1)
+        out_ref[...] = jnp.where(row < HIGH, high.astype(F32), low.astype(F32)).astype(BF)
+
+
+def final_body(got_ref, back_ref, basis_ref, wh_ref, wl_ref, last_ref, out_ref):
+    total = got_ref[0].astype(F32)
     for index in range(1, got_ref.shape[0]):
-        total = total + got_ref[index]
-    basis = basis_ref[...]
-    rows = dot3(split(basis[:, :RANK]), split(total))
-    spare = jnp.sum(basis * total[RANK - 1 :], 1, keepdims=True)
+        total = total + got_ref[index].astype(F32)
+    rows = dot3(split(back_ref[...]), split(total))
+    spare = jnp.sum(basis_ref[...] * total[HIGH - 1 : HIGH], 1, keepdims=True)
     out_ref[...] = dot3(split(rows), (wh_ref[...], wl_ref[...])) + spare * last_ref[...]
 
 
@@ -437,8 +447,10 @@
 
     moved_first, moved = call(
         front_body,
-        (bf16(noise_count, ROWS, PERIOD + FREQ), bf16(noise_count, ROWS, PERIOD)),
-        (mask_values, jnp.asarray(BASIS.T[:RANK], F32), *to_const(LINE.T), jnp.asarray(LAST, F32), dose_noise),
+        (pltpu.HBM((noise_count, ROWS, PERIOD + FREQ), BF), pltpu.HBM((noise_count, ROWS, PERIOD), BF)),
+        hbm(mask_values, jnp.asarray(BASIS.T[:RANK], F32))
+        + to_const(LINE.T)
+        + hbm(jnp.asarray(LAST, F32), dose_noise),
         grid=(columns,),
         in_specs=[fixed(ROWS, PERIOD), fixed(RANK, ROWS)]
         + [fixed(PERIOD, FREQ)] * 2
@@ -477,7 +489,7 @@
     field_spec = pl.BlockSpec((field_rows, 2 * COARSE), lambda i, *_: (i, 0))
     field, *pieces = call(
         field_body,
-        (f32(PAIRS * field_rows, 2 * COARSE),) + (f32(ROWS, COARSE),) * KERN,
+        (pltpu.HBM((PAIRS * field_rows, 2 * COARSE), F32),) + (f32(ROWS, COARSE),) * KERN,
         (weights, *specs, *hbm(kernels), *to_const(WAVE), *to_const(GRID), *hbm(jnp.asarray(BLUR, F32))),
         place=place,
         grid=(PAIRS,),
@@ -495,45 +507,47 @@
         ],
     )
     pieces = pieces[:1] + shifted(pieces[1:], shifts)
-    acid, rows = call(own_body, (f32(ROWS, PERIOD), f32(ROWS, COARSE)), (*pieces, *to_const(OWN.T)))
+    rows = (pieces[0] + pieces[1]) + (pieces[2] + pieces[3])
     swap = [(0, 1), (1, 0)]
     rows_other = lax.ppermute(rows, "tile", swap)
-    got_spec = pl.BlockSpec((noise_count, ROWS, CHUNK), lambda i, *_: (0, 0, i))
+    got_spec = pl.BlockSpec((noise_count, ROWS, CHUNK), lambda i: (0, 0, i))
+    sums_spec = pl.BlockSpec((4, ROWS, CHUNK), lambda i: (0, 0, i))
     sums = call(
         dose_first_body,
         f32(4, ROWS, PERIOD),
-        (acid, rows_other, *to_const(CROSS), got),
-        place=place,
+        (rows, *to_const(OWN.T), got),
         grid=(columns,),
-        in_specs=[chunk(ROWS), fixed(ROWS, COARSE)] + at_place(2, CROSS) + [got_spec],
-        out_specs=pl.BlockSpec((4, ROWS, CHUNK), lambda i, *_: (0, 0, i)),
-        scratch_shapes=[pltpu.VMEM((ROWS, 2 * EDGE), F32)],
+        in_specs=[fixed(ROWS, COARSE)] + [chunk(COARSE)] * 2 + [got_spec],
+        out_specs=sums_spec,
     )
     far = PERIOD // EDGE - 1
     (target,) = hbm(target)
     (sums,) = vmem(sums)
-    send = call(
+    edge_spec = pl.BlockSpec((noise_count, ROWS, EDGE), lambda i, _: (0, 0, i * far))
+    edges, send = call(
         dose_edge_body,
-        f32(ROWS, COARSE),
-        (sums, target, got_last, *to_const(cross_t)),
+        (f32(ROWS, 2 * EDGE), f32(ROWS, COARSE)),
+        (sums, rows_other, target, got, got_last, *to_const(CROSS), *to_const(cross_t)),
         place=place,
         grid=(2,),
         in_specs=[
-            pl.BlockSpec((4, ROWS, EDGE), lambda i, _: (0, 0, i * far)),
+            pl.BlockSpec((1, ROWS, EDGE), lambda i, _: (0, 0, i * far)),
+            fixed(ROWS, COARSE),
             pl.BlockSpec((ROWS, EDGE), lambda i, _: (0, i * far)),
-            pl.BlockSpec((noise_count, ROWS, EDGE), lambda i, _: (0, 0, i * far)),
+            edge_spec,
+            edge_spec,
         ]
+        + [pl.BlockSpec((1, COARSE, EDGE), lambda i, place: (place[2], 0, i))] * 2
         + [pl.BlockSpec((1, EDGE, COARSE), lambda i, place: (place[2], i, 0))] * 2,
-        out_specs=fixed(ROWS, COARSE),
-        scratch_shapes=[pltpu.VMEM((ROWS, EDGE), F32)],
+        out_specs=(pl.BlockSpec((ROWS, EDGE), lambda i, _: (0, i)), fixed(ROWS, COARSE)),
     )
     grad_other = lax.ppermute(send, "tile", swap)
     grad_own = call(
         dose_body,
         f32(ROWS, COARSE),
-        (sums, target, got_last, *to_const(OWN)),
+        (sums, edges, target, got_last, *to_const(OWN)),
         grid=(columns,),
-        in_specs=[pl.BlockSpec((4, ROWS, CHUNK), lambda i: (0, 0, i)), chunk(ROWS), got_spec]
+        in_specs=[sums_spec, fixed(ROWS, 2 * EDGE), chunk(ROWS), got_spec]
         + [pl.BlockSpec((CHUNK, COARSE), lambda i: (i, 0))] * 2,
         out_specs=fixed(ROWS, COARSE),
         scratch_shapes=[pltpu.VMEM((ROWS, CHUNK), F32)],
@@ -542,16 +556,15 @@
     grads = [grad] + shifted([grad] * len(shifts), shifts)
     spread = call(
         back_body,
-        f32(BLOCKS, RANK, FREQ),
+        bf16(BLOCKS, RANK, FREQ),
         (
             weights,
             *grads,
-            *vmem(field),
-            *hbm(kernels),
+            *hbm(field, kernels),
             *to_const(waves_t),
             *to_const(GRID.T),
             *hbm(jnp.asarray(BLUR.T, F32)),
-            *to_const(GATHER.T),
+            *to_const(SPREAD),
             *hbm(jnp.asarray(UNFOLD.T, BF)),
             *coef,
         ),
@@ -570,7 +583,7 @@
             pltpu.VMEM((KERN * ROWS, COARSE), F32),
             pltpu.VMEM((KERN * REACH, 2 * COARSE), F32),
             pltpu.VMEM((2 * FREQ, FREQ), F32),
-            pltpu.VMEM((2,) + GATHER.T.shape, BF),
+            pltpu.VMEM((2,) + SPREAD.shape, BF),
             pltpu.SemaphoreType.DMA((2,)),
         ],
     )
@@ -578,7 +591,7 @@
     return call(
         final_body,
         f32(ROWS, PERIOD),
-        (back, jnp.asarray(BASIS, F32), *to_const(LINE), jnp.asarray(LAST, F32)),
+        (back, jnp.asarray(BASIS_BACK, F32), jnp.asarray(BASIS, F32), *(jnp.asarray(t) for t in np_split(LINE)), jnp.asarray(LAST, F32)),
     )
 
 

time: 131 us -> 120 us (0.916)
  local copies, waits for them, and re-layouts: 7.5 us -> 0.03 us
  waiting for transfers between devices: 11.8 us -> 9.39 us
  blocking collectives: 57.9 us -> 55.8 us
  Pallas kernels: 33.8 us -> 35.3 us
    unnamed x20 -> x12, local copies, waits for them, and re-layouts: 7.5 us -> 0.03 us
    pallas_call x4, Pallas kernels: 11.6 us -> 15.5 us  [call(): pl.pallas_call(body, out_shape=out_shape, compiler_params=params, **kw)]
    pallas_call x5 -> x4, Pallas kernels: 22.2 us -> 19.8 us  [call(): pl.pallas_call(body, out_shape=out_shape, compiler_params=params, grid_sp...]
    all_to_all x1, blocking collectives: 20.8 us -> 18.4 us  [body(): back = lax.all_to_all(spread, ('kern', 'noise'), 0, 0, tiled=True)]
    ppermute x1, starting transfers between devices: 2.53 us -> 0.6 us  [body(): grad_other = lax.ppermute(send, 'tile', swap)]
    ppermute x1, waiting for transfers between devices: 1.82 us -> 0.01 us  [body(): rows_other = lax.ppermute(rows, 'tile', swap)]
  transfers between devices with their start and end apart: 12 -> 12, of which waited for: 8 -> 7; matrix products, arithmetic and copies ran while one was open for 0% -> 0% of each run, Pallas kernels for 15% -> 15%
where the time goes in v3:
time: 120 us; the launch traced here: 119 us
  blocking collectives  55.8 us (46%)
  Pallas kernels  35.3 us (29%)
  starting transfers between devices  18.3 us (15%)
  waiting for transfers between devices  9.39 us (8%)
    all_to_all x1, blocking collectives, body(): got = lax.all_to_all(moved_first, 'noise', 0, 0, tiled=True)  37.3 us
    pallas_call x4, Pallas kernels, call(): pl.pallas_call(body, out_shape=out_shape, compiler_params=params, grid_sp...  19.8 us
    all_to_all x1, blocking collectives, body(): back = lax.all_to_all(spread, ('kern', 'noise'), 0, 0, tiled=True)  18.4 us
    pallas_call x4, Pallas kernels, call(): pl.pallas_call(body, out_shape=out_shape, compiler_params=params, **kw)  15.5 us
    ppermute x9, starting transfers between devices, shifted(): lax.ppermute(value, 'kern', [(source, (source + shift) % count) for sourc...  10.6 us
    ppermute x9, waiting for transfers between devices, shifted(): lax.ppermute(value, 'kern', [(source, (source + shift) % count) for sourc...  9.38 us
    all_to_all x1, starting transfers between devices, body(): got_last = lax.all_to_all(moved, 'noise', 0, 0, tiled=True)  4.57 us
    ppermute x1, starting transfers between devices, body(): rows_other = lax.ppermute(rows, 'tile', swap)  2.53 us
  transfers between devices with their start and end apart: 12, of which 7 were waited for; matrix products, arithmetic and copies ran while one was open for 0% of the time, Pallas kernels for 15%

profile of v3, /device:TPU:1, one launch (start us, length us, event | category | flops | bytes accessed | tf_op | source)
XLA Modules:
  0.0 119.0 jit_solution(11290765080948766704)
XLA Ops:
  0.0 0.1 pad_add_fusion._.place_ref
  0.1 5.6 %shard_map.361 = (bf16[16,32,2176]{2,1,0:T(8,128)(2,1)}, bf16[16,32,2048]{2,1,0:T(8,128)(2,1)}) custom-call(f32[32,2048]{1,0:T(8,128)} %mask_ref.1, f32[16,32]{1,0:T(8,128)} %constant.81.clone.basis_ref, bf16[2048,128]{1,0:T(8,128)(2,1)} %constant.82.clone.lh_ref, bf16[2048,128]{1,0:T(8,128)(2,1)} %constant.83.clone.ll_ref, ...), custom_call_target="tpu_custom_call" | custom-call | tf_op jit(solution)/shard_map/pallas_call | solution.py:157
  5.7 37.3 %all_to_all.15.got_ref.noise_ref.first_ref = bf16[16,32,2176]{2,1,0:T(8,128)(2,1)S(1)} all-to-all(bf16[16,32,2176]{2,1,0:T(8,128)(2,1)} %get-tuple-element.23), channel_id=1, replica_groups=mesh['tile'=2,'kern'=4,'noise'=16] {'noise'}, dimensions={0} | all-to-all | bytes 4456448 | tf_op jit(solution)/shard_map/all_to_all | solution.py:463
  43.0 0.0 copy-start.5
  43.0 4.6 %all-to-all-start.1 = ((bf16[16,32,2048]{2,1,0:T(8,128)(2,1)}), bf16[16,32,2048]{2,1,0:T(8,128)(2,1)}, u32[]{:S(2)}, u32[]{:S(2)}) async-start(bf16[16,32,2048]{2,1,0:T(8,128)(2,1)} %get-tuple-element.35), calls=%async_computation.1 | async-start | bytes 4194304 | tf_op jit(solution)/shard_map/all_to_all | solution.py:467
  47.6 2.2 %shard_map.362.s0_ref = f32[256,128]{1,0:T(8,128)S(1)} custom-call(s32[3]{0:T(128)S(1)} %pad_add_fusion._.place_ref, bf16[16,32,2176]{2,1,0:T(8,128)(2,1)S(1)} %all_to_all.15.got_ref.noise_ref.first_ref, bf16[4,512,256]{2,1,0:T(8,128)(2,1)} %constant.86.clone.gh_ref, bf16[4,512,256]{2,1,0:T(8,128)(2,1)} %constant.87.clone.gl_ref, ...), custom_call_target="tpu_custom_call" | custom-call | tf_op jit(solution)/shard_map/pallas_call | solution.py:159
  49.8 2.1 %collective-permute-start.2 = (f32[256,128]{1,0:T(8,128)S(1)}, f32[256,128]{1,0:T(8,128)S(1)}, u32[]{:S(2)}, u32[]{:S(2)}) collective-permute-start(f32[256,128]{1,0:T(8,128)S(1)} %shard_map.362.s0_ref), channel_id=1, source_target_pairs={{0,48},{16,0},{32,16},{48,32},{1,49},{17,1},{33,17},{49,33},{2,50}... | collective-permute-start | bytes 393224 | tf_op jit(solution)/shard_map/ppermute | solution.py:426
  51.9 1.2 %collective-permute-start.1 = (f32[256,128]{1,0:T(8,128)S(1)}, f32[256,128]{1,0:T(8,128)S(1)}, u32[]{:S(2)}, u32[]{:S(2)}) collective-permute-start(f32[256,128]{1,0:T(8,128)S(1)} %shard_map.362.s0_ref), channel_id=1, source_target_pairs={{0,32},{16,48},{32,0},{48,16},{1,33},{17,49},{33,1},{49,17},{2,34}... | collective-permute-start | bytes 393224 | tf_op jit(solution)/shard_map/ppermute | solution.py:426
  53.1 0.5 collective-permute-start
  53.7 3.7 %collective-permute-done.2.s3_ref = f32[256,128]{1,0:T(8,128)S(1)} collective-permute-done((f32[256,128]{1,0:T(8,128)S(1)}, f32[256,128]{1,0:T(8,128)S(1)}, u32[]{:S(2)}, u32[]{:S(2)}) %collective-permute-start.2) | collective-permute-done | bytes 131104 | tf_op jit(solution)/shard_map/ppermute | solution.py:426
  57.4 0.2 collective-permute-done.1.s2_ref
  57.6 0.7 collective-permute-done.s1_ref
  58.2 0.0 copy-done.5
  58.2 7.1 %shard_map.363 = (f32[1536,512]{1,0:T(8,128)}, f32[32,256]{1,0:T(8,128)S(1)}, f32[32,256]{1,0:T(8,128)S(1)}, f32[32,256]{1,0:T(8,128)S(1)}, f32[32,256]{1,0:T(8,128)S(1)}) custom-call(s32[3]{0:T(128)S(1)} %pad_add_fusion._.place_ref, f32[6]{0:T(128)S(1)} %copy-done.5, f32[256,128]{1,0:T(8,128)S(1)} %shard_map.362.s0_ref, ...), custom_call_target="tpu_custom_call" | custom-call | tf_op jit(solution)/shard_map/pallas_call | solution.py:159
  65.4 2.5 %collective-permute-start.3 = (f32[32,256]{1,0:T(8,128)S(1)}, f32[32,256]{1,0:T(8,128)S(1)}, u32[]{:S(2)}, u32[]{:S(2)}) collective-permute-start(f32[32,256]{1,0:T(8,128)S(1)} %get-tuple-element.31), channel_id=1, source_target_pairs={{0,16},{16,32},{32,48},{48,0},{1,17},{17,33},{33,49},{49,1},{2,18}... | collective-permute-start | bytes 98312 | tf_op jit(solution)/shard_map/ppermute | solution.py:426
  67.8 1.2 %collective-permute-start.4 = (f32[32,256]{1,0:T(8,128)S(1)}, f32[32,256]{1,0:T(8,128)S(1)}, u32[]{:S(2)}, u32[]{:S(2)}) collective-permute-start(f32[32,256]{1,0:T(8,128)S(1)} %get-tuple-element.32), channel_id=1, source_target_pairs={{0,32},{16,48},{32,0},{48,16},{1,33},{17,49},{33,1},{49,17},{2,34}... | collective-permute-start | bytes 98312 | tf_op jit(solution)/shard_map/ppermute | solution.py:426
  69.1 0.0 collective-permute-start.5
  69.1 0.0 collective-permute-done.3
  69.1 2.2 %collective-permute-done.4 = f32[32,256]{1,0:T(8,128)S(1)} collective-permute-done((f32[32,256]{1,0:T(8,128)S(1)}, f32[32,256]{1,0:T(8,128)S(1)}, u32[]{:S(2)}, u32[]{:S(2)}) %collective-permute-start.4) | collective-permute-done | bytes 32800 | tf_op jit(solution)/shard_map/ppermute | solution.py:426
  71.3 1.5 %collective-permute-done.5 = f32[32,256]{1,0:T(8,128)S(1)} collective-permute-done((f32[32,256]{1,0:T(8,128)S(1)}, f32[32,256]{1,0:T(8,128)S(1)}, u32[]{:S(2)}, u32[]{:S(2)}) %collective-permute-start.5) | collective-permute-done | bytes 32800 | tf_op jit(solution)/shard_map/ppermute | solution.py:426
  72.8 2.5 %collective-permute-start.6 = (f32[32,256]{1,0:T(8,128)S(1)}, f32[32,256]{1,0:T(8,128)S(1)}, u32[]{:S(2)}, u32[]{:S(2)}) collective-permute-start(f32[32,256]{1,0:T(8,128)S(1)} %add_add_fusion.rows_ref), channel_id=1, source_target_pairs={{0,64},{64,0},{1,65},{65,1},{2,66},{66,2},{3,67},{67,3},{4,68},{68... | collective-permute-start | bytes 98312 | tf_op jit(solution)/shard_map/ppermute | solution.py:512
  75.3 4.1 %shard_map.364.acid_ref.sums_ref = f32[4,32,2048]{2,1,0:T(8,128)S(1)} custom-call(f32[32,256]{1,0:T(8,128)S(1)} %add_add_fusion.rows_ref, bf16[256,2048]{1,0:T(8,128)(2,1)} %constant.94.clone.oh_ref, bf16[256,2048]{1,0:T(8,128)(2,1)} %constant.95.clone.ol_ref, bf16[16,32,2176]{2,1,0:T(8,128)(2,1)S(1)} %all_to_all.15.got_ref.noise_ref.first_ref), custom_call_target="tpu_custom_call" | custom-call | tf_op jit(solution)/shard_map/pallas_call | solution.py:157
  79.5 0.0 collective-permute-done.6.other_ref
  79.5 0.0 all-to-all-done.1.second_ref.noise_ref
  79.5 2.8 %shard_map.365 = (f32[32,256]{1,0:T(8,128)S(1)}, f32[32,256]{1,0:T(8,128)S(1)}) custom-call(s32[3]{0:T(128)S(1)} %pad_add_fusion._.place_ref, f32[4,32,2048]{2,1,0:T(8,128)S(1)} %shard_map.364.acid_ref.sums_ref, f32[32,256]{1,0:T(8,128)S(1)} %collective-permute-done.6.other_ref, bf16[32,2048]{1,0:T(8,128)(2,1)} %target_ref.1, ...), custom_call_target="tpu_custom_call" | custom-call | tf_op jit(solution)/shard_map/pallas_call | solution.py:159
  82.3 0.6 collective-permute-start.7
  82.9 4.6 %shard_map.366 = f32[32,256]{1,0:T(8,128)S(1)} custom-call(f32[4,32,2048]{2,1,0:T(8,128)S(1)} %shard_map.364.acid_ref.sums_ref, f32[32,256]{1,0:T(8,128)S(1)} %get-tuple-element.36.edge_ref, bf16[32,2048]{1,0:T(8,128)(2,1)} %target_ref.1, bf16[16,32,2048]{2,1,0:T(8,128)(2,1)} %all-to-all-done.1.second_ref.noise_ref, ...), custom_call_target="tpu_custom_call" | custom-call | tf_op jit(solution)/shard_map/pallas_call | solution.py:157
  87.5 0.0 collective-permute-done.7
  87.6 1.3 %collective-permute-start.10 = (f32[32,256]{1,0:T(8,128)S(1)}, f32[32,256]{1,0:T(8,128)S(1)}, u32[]{:S(2)}, u32[]{:S(2)}) collective-permute-start(f32[32,256]{1,0:T(8,128)S(1)} %add.15.p0_ref), channel_id=1, source_target_pairs={{0,48},{16,0},{32,16},{48,32},{1,49},{17,1},{33,17},{49,33},{2,50}... | collective-permute-start | bytes 98312 | tf_op jit(solution)/shard_map/ppermute | solution.py:426
  88.9 0.3 collective-permute-start.9
  89.2 1.4 %collective-permute-start.8 = (f32[32,256]{1,0:T(8,128)S(1)}, f32[32,256]{1,0:T(8,128)S(1)}, u32[]{:S(2)}, u32[]{:S(2)}) collective-permute-start(f32[32,256]{1,0:T(8,128)S(1)} %add.15.p0_ref), channel_id=1, source_target_pairs={{0,16},{16,32},{32,48},{48,0},{1,17},{17,33},{33,49},{49,1},{2,18}... | collective-permute-start | bytes 98312 | tf_op jit(solution)/shard_map/ppermute | solution.py:426
  90.6 0.4 collective-permute-done.10.p3_ref
  91.0 0.7 collective-permute-done.9.p2_ref
  91.7 0.0 collective-permute-done.8.p1_ref
  91.7 0.0 copy-start
  91.7 0.0 copy-start.1
  91.7 0.0 copy-start.2
  91.7 0.0 copy-start.3
  91.7 0.0 copy-start.4
  91.7 7.7 %shard_map.367 = bf16[64,16,128]{2,1,0:T(8,128)(2,1)S(1)} custom-call(s32[3]{0:T(128)S(1)} %pad_add_fusion._.place_ref, f32[6]{0:T(128)S(1)} %copy-done.5, f32[32,256]{1,0:T(8,128)S(1)} %add.15.p0_ref, f32[32,256]{1,0:T(8,128)S(1)} %collective-permute-done.8.p1_ref, f32[32,256]{1,0:T(8,128)S(1)} %collective-permute-done.9.p2_ref, ...), custom_call_target="tpu_custom_call" | custom-call | tf_op jit(solution)/shard_map/pallas_call | solution.py:159
  99.4 18.4 %all_to_all.16.got_ref = bf16[64,16,128]{2,1,0:T(8,128)(2,1)S(1)} all-to-all(bf16[64,16,128]{2,1,0:T(8,128)(2,1)S(1)} %shard_map.367), channel_id=1, replica_groups=mesh['tile'=2,'kern'=4,'noise'=16] {'kern','noise'}, dimensions={0} | all-to-all | bytes 524288 | tf_op jit(solution)/shard_map/all_to_all | solution.py:590
  117.8 0.0 copy-done
  117.8 0.0 copy-done.1
  117.8 0.0 copy-done.2
  117.8 0.0 copy-done.3
  117.8 0.0 copy-done.4
  117.9 1.2 shard_map.368
  (2 shorter events, 0.0 us)
Async XLA Ops:
  43.0 15.2 %copy-start.5 = (f32[6]{0:T(128)S(1)}, f32[6]{0:T(128)}, u32[]{:S(2)}) copy-start(f32[6]{0:T(128)} %weight_ref.1) | copy-start | bytes 76
  43.0 36.5 %all-to-all-start.1 = ((bf16[16,32,2048]{2,1,0:T(8,128)(2,1)}), bf16[16,32,2048]{2,1,0:T(8,128)(2,1)}, u32[]{:S(2)}, u32[]{:S(2)}) async-start(bf16[16,32,2048]{2,1,0:T(8,128)(2,1)} %get-tuple-element.35), calls=%async_computation.1 | async-start | bytes 4194304 | tf_op jit(solution)/shard_map/all_to_all | solution.py:467
  49.8 7.6 %collective-permute-start.2 = (f32[256,128]{1,0:T(8,128)S(1)}, f32[256,128]{1,0:T(8,128)S(1)}, u32[]{:S(2)}, u32[]{:S(2)}) collective-permute-start(f32[256,128]{1,0:T(8,128)S(1)} %shard_map.362.s0_ref), channel_id=1, source_target_pairs={{0,48},{16,0},{32,16},{48,32},{1,49},{17,1},{33,17},{49,33},{2,50}... | collective-permute-start | bytes 393224 | tf_op jit(solution)/shard_map/ppermute | solution.py:426
  51.9 5.6 %collective-permute-start.1 = (f32[256,128]{1,0:T(8,128)S(1)}, f32[256,128]{1,0:T(8,128)S(1)}, u32[]{:S(2)}, u32[]{:S(2)}) collective-permute-start(f32[256,128]{1,0:T(8,128)S(1)} %shard_map.362.s0_ref), channel_id=1, source_target_pairs={{0,32},{16,48},{32,0},{48,16},{1,33},{17,49},{33,1},{49,17},{2,34}... | collective-permute-start | bytes 393224 | tf_op jit(solution)/shard_map/ppermute | solution.py:426
  53.1 5.1 %collective-permute-start = (f32[256,128]{1,0:T(8,128)S(1)}, f32[256,128]{1,0:T(8,128)S(1)}, u32[]{:S(2)}, u32[]{:S(2)}) collective-permute-start(f32[256,128]{1,0:T(8,128)S(1)} %shard_map.362.s0_ref), channel_id=1, source_target_pairs={{0,16},{16,32},{32,48},{48,0},{1,17},{17,33},{33,49},{49,1},{2,18}... | collective-permute-start | bytes 393224 | tf_op jit(solution)/shard_map/ppermute | solution.py:426
  65.4 3.7 %collective-permute-start.3 = (f32[32,256]{1,0:T(8,128)S(1)}, f32[32,256]{1,0:T(8,128)S(1)}, u32[]{:S(2)}, u32[]{:S(2)}) collective-permute-start(f32[32,256]{1,0:T(8,128)S(1)} %get-tuple-element.31), channel_id=1, source_target_pairs={{0,16},{16,32},{32,48},{48,0},{1,17},{17,33},{33,49},{49,1},{2,18}... | collective-permute-start | bytes 98312 | tf_op jit(solution)/shard_map/ppermute | solution.py:426
  67.8 3.4 %collective-permute-start.4 = (f32[32,256]{1,0:T(8,128)S(1)}, f32[32,256]{1,0:T(8,128)S(1)}, u32[]{:S(2)}, u32[]{:S(2)}) collective-permute-start(f32[32,256]{1,0:T(8,128)S(1)} %get-tuple-element.32), channel_id=1, source_target_pairs={{0,32},{16,48},{32,0},{48,16},{1,33},{17,49},{33,1},{49,17},{2,34}... | collective-permute-start | bytes 98312 | tf_op jit(solution)/shard_map/ppermute | solution.py:426
  69.1 3.7 %collective-permute-start.5 = (f32[32,256]{1,0:T(8,128)S(1)}, f32[32,256]{1,0:T(8,128)S(1)}, u32[]{:S(2)}, u32[]{:S(2)}) collective-permute-start(f32[32,256]{1,0:T(8,128)S(1)} %get-tuple-element.33), channel_id=1, source_target_pairs={{0,48},{16,0},{32,16},{48,32},{1,49},{17,1},{33,17},{49,33},{2,50}... | collective-permute-start | bytes 98312 | tf_op jit(solution)/shard_map/ppermute | solution.py:426
  72.8 6.7 %collective-permute-start.6 = (f32[32,256]{1,0:T(8,128)S(1)}, f32[32,256]{1,0:T(8,128)S(1)}, u32[]{:S(2)}, u32[]{:S(2)}) collective-permute-start(f32[32,256]{1,0:T(8,128)S(1)} %add_add_fusion.rows_ref), channel_id=1, source_target_pairs={{0,64},{64,0},{1,65},{65,1},{2,66},{66,2},{3,67},{67,3},{4,68},{68... | collective-permute-start | bytes 98312 | tf_op jit(solution)/shard_map/ppermute | solution.py:512
  82.3 5.2 %collective-permute-start.7 = (f32[32,256]{1,0:T(8,128)S(1)}, f32[32,256]{1,0:T(8,128)S(1)}, u32[]{:S(2)}, u32[]{:S(2)}) collective-permute-start(f32[32,256]{1,0:T(8,128)S(1)} %get-tuple-element.37), channel_id=1, source_target_pairs={{0,64},{64,0},{1,65},{65,1},{2,66},{66,2},{3,67},{67,3},{4,68},{68... | collective-permute-start | bytes 98312 | tf_op jit(solution)/shard_map/ppermute | solution.py:544
  87.6 3.4 %collective-permute-start.10 = (f32[32,256]{1,0:T(8,128)S(1)}, f32[32,256]{1,0:T(8,128)S(1)}, u32[]{:S(2)}, u32[]{:S(2)}) collective-permute-start(f32[32,256]{1,0:T(8,128)S(1)} %add.15.p0_ref), channel_id=1, source_target_pairs={{0,48},{16,0},{32,16},{48,32},{1,49},{17,1},{33,17},{49,33},{2,50}... | collective-permute-start | bytes 98312 | tf_op jit(solution)/shard_map/ppermute | solution.py:426
  88.9 2.8 %collective-permute-start.9 = (f32[32,256]{1,0:T(8,128)S(1)}, f32[32,256]{1,0:T(8,128)S(1)}, u32[]{:S(2)}, u32[]{:S(2)}) collective-permute-start(f32[32,256]{1,0:T(8,128)S(1)} %add.15.p0_ref), channel_id=1, source_target_pairs={{0,32},{16,48},{32,0},{48,16},{1,33},{17,49},{33,1},{49,17},{2,34}... | collective-permute-start | bytes 98312 | tf_op jit(solution)/shard_map/ppermute | solution.py:426
  89.2 2.5 %collective-permute-start.8 = (f32[32,256]{1,0:T(8,128)S(1)}, f32[32,256]{1,0:T(8,128)S(1)}, u32[]{:S(2)}, u32[]{:S(2)}) collective-permute-start(f32[32,256]{1,0:T(8,128)S(1)} %add.15.p0_ref), channel_id=1, source_target_pairs={{0,16},{16,32},{32,48},{48,0},{1,17},{17,33},{33,49},{49,1},{2,18}... | collective-permute-start | bytes 98312 | tf_op jit(solution)/shard_map/ppermute | solution.py:426
  91.7 26.2 %copy-start = (bf16[128,2048]{1,0:T(8,128)(2,1)S(1)}, bf16[128,2048]{1,0:T(8,128)(2,1)}, u32[]{:S(2)}) copy-start(bf16[128,2048]{1,0:T(8,128)(2,1)} %constant.113.clone.wl_ref) | copy-start | bytes 1572868
  91.7 26.2 %copy-start.1 = (bf16[128,2048]{1,0:T(8,128)(2,1)S(1)}, bf16[128,2048]{1,0:T(8,128)(2,1)}, u32[]{:S(2)}) copy-start(bf16[128,2048]{1,0:T(8,128)(2,1)} %constant.112.clone.wh_ref) | copy-start | bytes 1572868
  91.7 26.2 %copy-start.2 = (f32[1,2048]{1,0:T(1,128)S(1)}, f32[1,2048]{1,0:T(1,128)}, u32[]{:S(2)}) copy-start(f32[1,2048]{1,0:T(1,128)} %constant.84.clone.last_ref) | copy-start | bytes 24580
  91.7 26.2 %copy-start.3 = (f32[32,128]{1,0:T(8,128)S(1)}, f32[32,128]{1,0:T(8,128)}, u32[]{:S(2)}) copy-start(f32[32,128]{1,0:T(8,128)} %constant.111.clone.basis_ref) | copy-start | bytes 49156
  91.7 26.2 %copy-start.4 = (f32[32,16]{1,0:T(8,128)S(1)}, f32[32,16]{1,0:T(8,128)}, u32[]{:S(2)}) copy-start(f32[32,16]{1,0:T(8,128)} %constant.110.clone.back_ref) | copy-start | bytes 6148

commit v4 on v3

v4 whole, which is shorter than its diff:
```python
import math

import jax
import jax.numpy as jnp
import numpy as np
from jax import lax
from jax.experimental import pallas as pl
from jax.experimental.pallas import tpu as pltpu
from jax.sharding import PartitionSpec as P

HALO = 16
FREQ = 128
COARSE = 256
PERIOD = 2048
ROWS = 32
REACH = 24
EDGE = 128
GROUP = 6
PAIRS = GROUP // 2
KERN = 4
SAMPLES = 32
RANK = 16
MIB = 32
BF = jnp.bfloat16
F32 = jnp.float32


def np_split(table):
    table = np.asarray(table, np.float32)
    high = table.astype(jnp.bfloat16)
    low = (table - high.astype(np.float32)).astype(jnp.bfloat16)
    return high, low


def np_waves(ids):
    centred = np.arange(FREQ) - FREQ // 2
    angles = 2.0 * np.pi * ((centred[:, None] * ids[None, :]) % PERIOD) / PERIOD
    return np.cos(angles), np.sin(angles)


def line_tables():
    half = FREQ // 2
    pixels = np.arange(PERIOD)
    angle = lambda f: 2.0 * np.pi * ((f[:, None] * pixels[None, :]) % PERIOD) / PERIOD
    line = np.concatenate([np.cos(angle(np.arange(half + 1))), np.sin(angle(np.arange(1, half)))], 0)
    last = np.sin(angle(np.array([half])))
    unfold = np.zeros((FREQ, 2 * FREQ))
    for j in range(FREQ):
        f = j - half
        unfold[abs(f), j] = 1.0
        if 0 < abs(f) < half:
            unfold[half + abs(f), FREQ + j] = np.sign(f)
    row = np.arange(ROWS) - (ROWS - 1) / 2.0
    fine = np.arange(-half, half + 0.01, 0.25)
    wave = np.exp(2j * np.pi * np.outer(row, fine) / PERIOD)
    basis = np.linalg.svd(np.concatenate([wave.real, wave.imag], 1))[0][:, : RANK - 1]
    basis = np.concatenate([basis, np.zeros((ROWS, FREQ - RANK + 1))], 1)
    freqs = np.arange(FREQ) - half
    coef = np.exp(2j * np.pi * np.outer(freqs, row) / PERIOD) @ basis
    blocks = PERIOD // ROWS
    centre = ROWS * np.arange(blocks) + (ROWS - 1) / 2.0
    phase = np.exp(2j * np.pi * np.outer(freqs, centre) / PERIOD)
    rows = phase[:, :, None] * coef[:, None, :RANK]
    rows[:, :, RANK - 1] = 0.0
    spare = np.zeros_like(rows)
    spare[:, :, RANK - 1] = phase
    rows = rows.reshape(FREQ, blocks * RANK)
    spare = spare.reshape(FREQ, blocks * RANK)
    gather = np.concatenate([rows.real, rows.imag, spare.real, spare.imag], 0)
    return line, last, unfold, basis, np.stack([coef.real, coef.imag]), gather


def tables():
    ccos, csin = np_waves(np.arange(COARSE) * (PERIOD // COARSE))
    grid = np.block([[ccos, csin], [-csin, ccos]]) / FREQ
    offsets = np.arange(-HALO, HALO + 1)
    taps = np.exp(-(offsets.astype(np.float64) ** 2) / (2.0 * (HALO / 2.0) ** 2))
    taps = taps / taps.sum()
    nodes = np.cos(np.pi * (np.arange(REACH) + 0.5) / REACH) * (ROWS / 2 + HALO - 0.5) + (ROWS - 1) / 2.0
    freqs = np.arange(1 - FREQ, FREQ)
    at = lambda places: np.exp(2j * np.pi * np.outer(places, freqs) / PERIOD)
    both = lambda value: np.concatenate([value.real, value.imag], 1)
    row_blur = np.zeros((PERIOD // ROWS, ROWS, REACH))
    near = np.arange(-HALO, ROWS + HALO)
    full = np.zeros((ROWS, ROWS + 2 * HALO))
    for row in range(ROWS):
        full[row, row : row + 2 * HALO + 1] = taps
    for block in range(PERIOD // ROWS):
        inside = (near + block * ROWS >= 0) & (near + block * ROWS < PERIOD)
        wanted = both((full * inside) @ at(near))
        row_blur[block] = np.linalg.lstsq(both(at(nodes)).T, wanted.T, rcond=1e-12)[0].T
    places = ROWS * np.arange(PERIOD // ROWS)[:, None] + nodes[None, :]
    angles = 2.0 * np.pi * (places[:, :, None] * (np.arange(FREQ) - FREQ // 2)) / PERIOD
    cos, sin = np.cos(angles), np.sin(angles)
    reach = np.concatenate([np.concatenate([cos, -sin], 2), np.concatenate([sin, cos], 2)], 1)
    shift = np.arange(PERIOD)[:, None] - (PERIOD // COARSE) * np.arange(COARSE)[None, :]
    freqs = np.arange(1, FREQ)
    line = (1.0 + 2.0 * np.cos(2.0 * np.pi * np.outer(np.arange(PERIOD), freqs) / PERIOD).sum(1)) / COARSE
    interp = line[shift % PERIOD]
    padded = np.zeros((PERIOD + 2 * HALO, COARSE))
    padded[HALO:-HALO] = interp
    own = np.zeros((PERIOD, COARSE))
    for index, tap in enumerate(taps):
        own += tap * padded[index : index + PERIOD]
    cross = np.zeros((2, COARSE, 2 * EDGE))
    for column in range(HALO):
        for index, offset in enumerate(offsets):
            if column + offset < 0:
                cross[1, :, column] += taps[index] * interp[PERIOD + column + offset]
            place = PERIOD - 1 - column + offset
            if place >= PERIOD:
                cross[0, :, 2 * EDGE - 1 - column] += taps[index] * interp[place - PERIOD]
    return reach, grid, row_blur, own, cross


LINE, LAST, UNFOLD, BASIS, COEF, GATHER = line_tables()
REACH_WAVES, GRID, ROW_BLUR, OWN, CROSS = tables()
BLOCKS = PERIOD // ROWS
GROUP_BLOCKS = BLOCKS // KERN
WAVE = REACH_WAVES
WAVE = WAVE.reshape(KERN, GROUP_BLOCKS, 2 * REACH, 2 * FREQ).transpose(1, 0, 2, 3)
WAVE = WAVE.reshape(GROUP_BLOCKS, KERN * 2 * REACH, 2 * FREQ)
LOW = 4
HIGH = RANK - LOW
SPREAD = GATHER.reshape(4 * FREQ, BLOCKS, RANK)
SPREAD = np.concatenate([SPREAD[:, :, : HIGH - 1], SPREAD[:, :, RANK - 1 :], SPREAD[:, :, :LOW]], 2)
SPREAD = SPREAD.reshape(4 * FREQ, BLOCKS * RANK).T
BASIS_BACK = np.concatenate([BASIS[:, : HIGH - 1], np.zeros((ROWS, 1)), BASIS[:, :LOW]], 1)
GATHER_OWN = GATHER.reshape(4 * FREQ, KERN, GROUP_BLOCKS * RANK).transpose(1, 0, 2)
BLUR = np.zeros((GROUP_BLOCKS, KERN, ROWS, KERN, REACH))
for group in range(KERN):
    BLUR[:, group, :, group] = ROW_BLUR.reshape(KERN, GROUP_BLOCKS, ROWS, REACH)[group]
BLUR = BLUR.reshape(GROUP_BLOCKS, KERN * ROWS, KERN * REACH)


def split(value):
    high = value.astype(BF)
    return high, (value - high.astype(F32)).astype(BF)


NN = (((1,), (0,)), ((), ()))


def dot3(left, right):
    lh, ll = left
    rh, rl = right

    def one(a, b):
        return lax.dot_general(a, b, NN, preferred_element_type=F32)

    count = lh.shape[0]
    if count > 64:
        return one(jnp.concatenate([lh, ll, lh], 1), jnp.concatenate([rh, rh, rl], 0))
    both = one(jnp.concatenate([lh, ll], 0), rh)
    return both[:count] + (one(lh, rl) + both[count:])


def dot_exact(left, right):
    high, low = left
    return jnp.dot(high, right, preferred_element_type=F32) + jnp.dot(low, right, preferred_element_type=F32)


def call(body, out_shape, args, place=None, **kw):
    params = pltpu.CompilerParams(vmem_limit_bytes=MIB * 1024 * 1024)
    if place is None:
        return pl.pallas_call(body, out_shape=out_shape, compiler_params=params, **kw)(*args)
    grid_spec = pltpu.PrefetchScalarGridSpec(num_scalar_prefetch=1, **kw)
    return pl.pallas_call(body, out_shape=out_shape, compiler_params=params, grid_spec=grid_spec)(place, *args)


def hbm(*values):
    return tuple(pltpu.with_memory_space_constraint(value, pltpu.HBM) for value in values)


def vmem(*values):
    return tuple(pltpu.with_memory_space_constraint(value, pltpu.VMEM) for value in values)


CHUNK = 1024
LANES = 256
PARTS = 4


def front_body(mask_ref, basis_ref, lh_ref, ll_ref, last_ref, noise_ref, first_ref, second_ref, *scratch):
    mask, basis, lh, ll, last, first, second, sems = scratch
    tables = [
        pltpu.make_async_copy(source, target, sems.at[index])
        for index, (source, target) in enumerate(
            zip((mask_ref, basis_ref, lh_ref, ll_ref, last_ref), (mask, basis, lh, ll, last))
        )
    ]
    part = first.shape[0] // PARTS
    loads, stores = [], []
    for index in range(2 * PARTS):
        which, rows = index // PARTS, pl.ds(index % PARTS * part, part)
        held, out_ref = (first, first_ref) if which == 0 else (second, second_ref)
        there = held.at[rows, :, pl.ds(0, PERIOD)] if which == 0 else held.at[rows]
        loads.append(pltpu.make_async_copy(noise_ref.at[which, rows], there, sems.at[5 + index]))
        stores.append(pltpu.make_async_copy(held.at[rows], out_ref.at[rows], sems.at[5 + 2 * PARTS + index]))
    for copy in tables + loads:
        copy.start()
    for copy in tables:
        copy.wait()
    transmit = (2.0 * mask[...] - 1.0) * (1.0 / PERIOD)
    rows = dot3(split(basis[...]), split(transmit))
    line = dot3(split(rows), (lh[...], ll[...]))
    row = lax.broadcasted_iota(jnp.int32, (RANK, FREQ), 0)
    lane = lax.broadcasted_iota(jnp.int32, (RANK, FREQ), 1)
    apart = jnp.sum(rows * last[...], 1, keepdims=True)
    apart = jnp.sum(jnp.where(row == lane, apart, 0.0), 0, keepdims=True)
    packed = jnp.concatenate(split(jnp.where(row == RANK - 1, apart, line)), 0)
    for index in range(first.shape[0]):
        first[index, :, PERIOD:] = packed
    for load, store in zip(loads, stores):
        load.wait()
        store.start()
    for store in stores:
        store.wait()


def spectrum_body(_, got_ref, gh_ref, gl_ref, unfold_ref, coef_ref, out_ref):
    high = got_ref[:, :RANK].reshape(GROUP_BLOCKS * RANK, FREQ)
    low = got_ref[:, RANK:].reshape(GROUP_BLOCKS * RANK, FREQ)
    both = dot3((gh_ref[0], gl_ref[0]), (high, low))
    waves = dot_exact(split(both[: 2 * FREQ]), unfold_ref[...])
    spare_cos, spare_sin = both[2 * FREQ : 3 * FREQ], both[3 * FREQ :]
    coef_re, coef_im = coef_ref[0], coef_ref[1]
    last_cos = jnp.sum(coef_re * spare_cos - coef_im * spare_sin, 1, keepdims=True)
    last_sin = jnp.sum(coef_re * spare_sin + coef_im * spare_cos, 1, keepdims=True)
    first = lax.broadcasted_iota(jnp.int32, (FREQ, FREQ), 1) == 0
    cos_cos, cos_sin = waves[:FREQ, :FREQ], waves[:FREQ, FREQ:]
    sin_cos, sin_sin = waves[FREQ:, :FREQ], waves[FREQ:, FREQ:]
    out_ref[:FREQ] = cos_cos - sin_sin + jnp.where(first, last_sin, 0.0)
    out_ref[FREQ:] = jnp.where(first, last_cos, 0.0) - cos_sin - sin_cos


def field_body(place_ref, weight_ref, *refs):
    ins, outs, scratch = refs[:10], refs[10 : 11 + KERN], refs[11 + KERN :]
    spec_refs, (kern_ref, wh_ref, wl_ref, gh_ref, gl_ref, blur_ref) = ins[:KERN], ins[KERN:]
    field_ref, piece_refs = outs[0], outs[1:]
    specs, kern, wave, grid, blur, field, total_ref, sems = scratch
    block = place_ref[1]
    copies = fetches(
        list(spec_refs) + [kern_ref, wh_ref.at[block], wl_ref.at[block], gh_ref, gl_ref, blur_ref.at[block]],
        [specs.at[index] for index in range(KERN)]
        + [kern, wave.at[0], wave.at[1], grid.at[0], grid.at[1], blur],
        sems,
    )
    for copy in copies[:7]:
        copy.wait()
    spec = (specs[0] + specs[1]) + (specs[2] + specs[3])
    spec_re = spec[:FREQ]
    spec_im = spec[FREQ:]
    half = KERN * REACH
    total, stores = None, []
    for pair in range(PAIRS):
        near_re, near_im = [], []
        for index in (2 * pair, 2 * pair + 1):
            kern_re, kern_im = kern[index, 0], kern[index, 1]
            near_re.append(kern_re * spec_re - kern_im * spec_im)
            near_im.append(kern_re * spec_im + kern_im * spec_re)
        near = jnp.concatenate([jnp.concatenate(near_re, 1), jnp.concatenate(near_im, 1)], 0)
        left = dot3((wave[0], wave[1]), split(near))
        lefts = []
        for index in range(2):
            lanes = slice(index * FREQ, (index + 1) * FREQ)
            for group in range(KERN):
                first = 2 * group * REACH
                re, im = left[first : first + REACH, lanes], left[first + REACH : first + 2 * REACH, lanes]
                lefts.append(jnp.concatenate([re, im], 1))
        if pair == 0:
            for copy in copies[7:9]:
                copy.wait()
        held = field.at[pl.ds(pair * 2 * half, 2 * half)]
        held[...] = dot3(split(jnp.concatenate(lefts, 0)), (grid[0], grid[1]))
        stores.append(pltpu.make_async_copy(held, field_ref.at[pl.ds(pair * 2 * half, 2 * half)], sems.at[10 + pair]))
        stores[-1].start()
        for index in range(2):
            own = held[index * half : (index + 1) * half]
            own = own * own
            own = weight_ref[2 * pair + index] * (own[:, :COARSE] + own[:, COARSE:])
            total = own if total is None else total + own
    copies[9].wait()
    total_ref[...] = dot3(split(blur[...]), split(total))
    for shift, piece_ref in enumerate(piece_refs):
        group = lax.rem(place_ref[0] + shift, KERN)
        piece_ref[...] = total_ref[pl.ds(pl.multiple_of(group * ROWS, ROWS), ROWS)]
    for store in stores:
        store.wait()


def sample_sums(noise_ref, place, acid, sums):
    sum_u, sum_q, sum_qu = sums
    quarter = 0.25 * acid
    base = acid - 2.0
    for index in range(noise_ref.shape[0]):
        noise = noise_ref[(index,) + place].astype(F32)
        u = jnp.tanh(quarter * noise + base)
        q = (1.0 - u * u) * (1.0 + 0.25 * noise)
        sum_u, sum_q, sum_qu = sum_u + u, sum_q + q, sum_qu + q * u
    return sum_u, sum_q, sum_qu


def places(columns):
    width = min(columns, LANES)
    for row in range(0, ROWS, 16):
        for col in range(0, columns, width):
            yield slice(row, row + 16), slice(col, col + width)


def dose_first_body(rows_ref, oh_ref, ol_ref, noise_ref, sums_ref):
    sums_ref[0] = dot3(split(rows_ref[...]), (oh_ref[...], ol_ref[...]))
    for place in places(CHUNK):
        acid = sums_ref[(0,) + place]
        zero = jnp.zeros(acid.shape, F32)
        for index, value in enumerate(sample_sums(noise_ref, place, acid, (zero, zero, zero))):
            sums_ref[(index + 1,) + place] = value


def acid_grad(sums, target):
    sum_u, sum_q, sum_qu = sums
    inner = 0.25 - sum_u * (1.0 / SAMPLES) - 0.5 * target.astype(F32)
    return (1.0 / 16.0) * (sum_q * inner + 1.25 * sum_qu)


def dose_edge_body(
    _, acid_ref, other_ref, target_ref, first_ref, second_ref, ch_ref, cl_ref, th_ref, tl_ref, grad_ref, send_ref
):
    halo = dot3(split(other_ref[...]), (ch_ref[0], cl_ref[0]))
    for place in places(EDGE):
        acid = acid_ref[(0,) + place] + halo[place]
        zero = jnp.zeros(acid.shape, F32)
        sums = sample_sums(first_ref, place, acid, (zero, zero, zero))
        sums = sample_sums(second_ref, place, acid, sums)
        grad_ref[place] = acid_grad(sums, target_ref[place])
    part = dot3(split(grad_ref[...]), (th_ref[0], tl_ref[0]))
    send_ref[...] = jnp.where(pl.program_id(0) == 0, 0.0, send_ref[...]) + part


def dose_body(sums_ref, edge_ref, target_ref, noise_ref, oh_ref, ol_ref, out_ref):
    step = pl.program_id(0)
    last = pl.num_programs(0) - 1
    total = jnp.where(step == 0, 0.0, out_ref[...])
    for col in range(0, CHUNK, LANES):
        lanes = slice(col, col + LANES)
        grads = []
        for row in range(0, ROWS, 16):
            place = (slice(row, row + 16), lanes)
            acid, *sums = [sums_ref[(index,) + place] for index in range(4)]
            grads.append(acid_grad(sample_sums(noise_ref, place, acid, sums), target_ref[place]))
        grad = jnp.concatenate(grads, 0)
        if col == 0:
            grad = jnp.concatenate([jnp.where(step == 0, edge_ref[:, :EDGE], grad[:, :EDGE]), grad[:, EDGE:]], 1)
        if col == CHUNK - LANES:
            here = jnp.where(step == last, edge_ref[:, EDGE:], grad[:, LANES - EDGE :])
            grad = jnp.concatenate([grad[:, : LANES - EDGE], here], 1)
        total = total + dot3(split(grad), (oh_ref[lanes], ol_ref[lanes]))
    out_ref[...] = total


def fetches(sources, targets, sems):
    copies = [
        pltpu.make_async_copy(source, target, sems.at[index])
        for index, (source, target) in enumerate(zip(sources, targets))
    ]
    for copy in copies:
        copy.start()
    return copies


def back_body(place_ref, weight_ref, *refs):
    piece_refs, ins = refs[:KERN], refs[KERN : KERN + 11]
    field_ref, kern_ref, wh_ref, wl_ref, gh_ref, gl_ref, blur_ref, th_ref, tl_ref, fold_ref, coef_ref = ins
    out_ref, rows, blur, grid, field, wave, kern, fold, coef, table, sems = refs[KERN + 11 :]
    block = place_ref[1]
    group = [lax.rem(place_ref[0] - shift + KERN, KERN) * ROWS for shift in range(KERN)]
    size = 2 * KERN * REACH
    pairs = [pl.ds(pair * size, size) for pair in range(PAIRS)]
    copies = fetches(
        list(piece_refs)
        + [blur_ref.at[block], field_ref.at[pairs[0]], gh_ref, gl_ref, wh_ref.at[block], wl_ref.at[block], kern_ref]
        + [field_ref.at[pair] for pair in pairs[1:]]
        + [fold_ref, coef_ref, th_ref, tl_ref],
        [rows.at[pl.ds(pl.multiple_of(first, ROWS), ROWS)] for first in group]
        + [blur, field.at[pairs[0]], grid.at[0], grid.at[1], wave.at[0], wave.at[1], kern]
        + [field.at[pair] for pair in pairs[1:]]
        + [fold, coef, table.at[0], table.at[1]],
        sems,
    )
    for copy in copies[:5]:
        copy.wait()
    part = 2.0 * dot3(split(blur[...]), split(rows[...]))
    grad = jnp.concatenate([part, part], 1)
    half = KERN * REACH
    sum_re = sum_im = None
    for pair in range(PAIRS):
        for copy in copies[5:8] if pair == 0 else copies[10 + pair : 11 + pair]:
            copy.wait()
        pulled = [
            field[index * half : (index + 1) * half] * (weight_ref[index] * grad)
            for index in (2 * pair, 2 * pair + 1)
        ]
        lefts = dot3(split(jnp.concatenate(pulled, 0)), (grid[0], grid[1]))
        stack = []
        for index in range(2):
            column = []
            for which in range(KERN):
                first = index * half + which * REACH
                left = lefts[first : first + REACH]
                column += [left[:, :FREQ], left[:, FREQ:]]
            stack.append(jnp.concatenate(column, 0))
        if pair == 0:
            for copy in copies[8:11]:
                copy.wait()
        near = dot3((wave[0], wave[1]), split(jnp.concatenate(stack, 1)))
        for index in range(2):
            near_re = near[:FREQ, index * FREQ : (index + 1) * FREQ]
            near_im = near[FREQ:, index * FREQ : (index + 1) * FREQ]
            kern_re, kern_im = kern[2 * pair + index, 0], kern[2 * pair + index, 1]
            own_re = kern_re * near_re + kern_im * near_im
            own_im = kern_re * near_im - kern_im * near_re
            sum_re = own_re if sum_re is None else sum_re + own_re
            sum_im = own_im if sum_im is None else sum_im + own_im
    grad_re, grad_im = sum_re * (2.0 / PERIOD), sum_im * (2.0 / PERIOD)
    mix = jnp.concatenate(
        [jnp.concatenate([grad_re, -grad_im], 1), jnp.concatenate([-grad_im, -grad_re], 1)], 0
    )
    for copy in copies[13:]:
        copy.wait()
    folded = dot_exact(split(mix), fold[...])
    coef_re, coef_im = coef[0], coef[1]
    by_cos, by_sin = grad_im[:, :1], grad_re[:, :1]
    spare_cos = coef_re * by_cos + coef_im * by_sin
    spare_sin = coef_re * by_sin - coef_im * by_cos
    mixed = jnp.concatenate([folded, spare_cos, spare_sin], 0)
    high, low = split(dot3((table[0], table[1]), split(mixed)).reshape(out_ref.shape))
    row = lax.broadcasted_iota(jnp.int32, out_ref.shape, 1)
    out_ref[...] = jnp.where(row < HIGH, high.astype(F32), low.astype(F32)).astype(BF)


def final_body(got_ref, back_ref, basis_ref, wh_ref, wl_ref, last_ref, out_ref):
    total = got_ref[0].astype(F32)
    for index in range(1, got_ref.shape[0]):
        total = total + got_ref[index].astype(F32)
    rows = dot3(split(back_ref[...]), split(total))
    spare = jnp.sum(basis_ref[...] * total[HIGH - 1 : HIGH], 1, keepdims=True)
    out_ref[...] = dot3(split(rows), (wh_ref[...], wl_ref[...])) + spare * last_ref[...]


def to_const(table):
    return hbm(*near_const(table))


def near_const(table):
    return tuple(jnp.asarray(part) for part in np_split(table))


def shifted(values, shifts):
    count = lax.axis_size("kern")
    return [
        lax.ppermute(value, "kern", [(source, (source + shift) % count) for source in range(count)])
        for value, shift in zip(values, shifts)
    ]


def body(mask_values, kernels, weights, target, dose_noise):
    noise_count = lax.axis_size("noise")
    f32 = lambda *shape: jax.ShapeDtypeStruct(shape, F32)
    bf16 = lambda *shape: jax.ShapeDtypeStruct(shape, BF)
    smem = pl.BlockSpec(memory_space=pltpu.SMEM)
    columns = PERIOD // CHUNK
    shifts = range(1, KERN)

    def fixed(*shape):
        return pl.BlockSpec(shape, lambda i, *_: (0,) * len(shape))

    def chunk(rows):
        return pl.BlockSpec((rows, CHUNK), lambda i, *_: (0, i))

    def moved_spec(width):
        return pl.BlockSpec((noise_count // columns, ROWS, width), lambda i: (i, 0, 0))

    lines = to_const(LINE.T)
    basis = jnp.asarray(BASIS.T[:RANK], F32)
    last = jnp.asarray(LAST, F32)
    far_noise = dose_noise.reshape(2, noise_count, ROWS, PERIOD)
    anywhere = pl.BlockSpec(memory_space=pltpu.HBM)
    held = (mask_values, basis, *lines, last)
    moved_first, moved = call(
        front_body,
        (pltpu.HBM((noise_count, ROWS, PERIOD + FREQ), BF), pltpu.HBM((noise_count, ROWS, PERIOD), BF)),
        hbm(*held, far_noise),
        in_specs=[anywhere] * 6,
        out_specs=(anywhere, anywhere),
        scratch_shapes=[pltpu.VMEM(value.shape, value.dtype) for value in held]
        + [
            pltpu.VMEM((noise_count, ROWS, PERIOD + FREQ), BF),
            pltpu.VMEM((noise_count, ROWS, PERIOD), BF),
            pltpu.SemaphoreType.DMA((5 + 4 * PARTS,)),
        ],
    )
    place = jnp.stack([lax.axis_index(axis).astype(jnp.int32) for axis in ("kern", "noise", "tile")])
    moved_first, place = lax.optimization_barrier((moved_first, place))
    got = lax.all_to_all(moved_first, "noise", 0, 0, tiled=True)
    got, moved, kernels, weights, target, place = lax.optimization_barrier(
        (got, moved, kernels, weights, target, place)
    )
    got_last = lax.all_to_all(moved, "noise", 0, 0, tiled=True)

    def at_place(which, table):
        return [pl.BlockSpec((1,) + table.shape[1:], lambda i, place: (place[which], 0, 0))] * 2

    waves_t = WAVE.transpose(0, 2, 1)
    cross_t = CROSS.transpose(0, 2, 1)
    coef = hbm(jnp.asarray(COEF, F32))
    spec = call(
        spectrum_body,
        f32(2 * FREQ, FREQ),
        (got, *to_const(GATHER_OWN), jnp.asarray(UNFOLD, BF), jnp.asarray(COEF, F32)),
        place=place,
        grid=(1,),
        in_specs=[pl.BlockSpec((noise_count, ROWS, FREQ), lambda i, _: (0, 0, PERIOD // FREQ))]
        + at_place(0, GATHER_OWN)
        + [fixed(*UNFOLD.shape), fixed(*COEF.shape)],
        out_specs=fixed(2 * FREQ, FREQ),
    )
    specs = [spec] + shifted([spec] * len(shifts), shifts)
    field_rows = 2 * KERN * REACH
    field_shape = (PAIRS * field_rows, 2 * COARSE)
    blur = jnp.asarray(BLUR, F32)
    ins = (*specs, kernels, *to_const(WAVE), *to_const(GRID), blur)
    field, *pieces = call(
        field_body,
        (pltpu.HBM(field_shape, F32),) + (f32(ROWS, COARSE),) * KERN,
        (place, weights, *hbm(*ins)),
        in_specs=[smem] * 2 + [anywhere] * len(ins),
        out_specs=(anywhere,) + (pl.BlockSpec((ROWS, COARSE), lambda: (0, 0)),) * KERN,
        scratch_shapes=[
            pltpu.VMEM((KERN,) + spec.shape, F32),
            pltpu.VMEM(kernels.shape, F32),
            pltpu.VMEM((2,) + WAVE.shape[1:], BF),
            pltpu.VMEM((2,) + GRID.shape, BF),
            pltpu.VMEM(BLUR.shape[1:], F32),
            pltpu.VMEM(field_shape, F32),
            pltpu.VMEM((KERN * ROWS, COARSE), F32),
            pltpu.SemaphoreType.DMA((10 + PAIRS,)),
        ],
    )
    pieces = pieces[:1] + shifted(pieces[1:], shifts)
    rows = (pieces[0] + pieces[1]) + (pieces[2] + pieces[3])
    swap = [(0, 1), (1, 0)]
    rows_other = lax.ppermute(rows, "tile", swap)
    got_spec = pl.BlockSpec((noise_count, ROWS, CHUNK), lambda i: (0, 0, i))
    sums_spec = pl.BlockSpec((4, ROWS, CHUNK), lambda i: (0, 0, i))
    sums = call(
        dose_first_body,
        f32(4, ROWS, PERIOD),
        (rows, *near_const(OWN.T), got),
        grid=(columns,),
        in_specs=[fixed(ROWS, COARSE)] + [chunk(COARSE)] * 2 + [got_spec],
        out_specs=sums_spec,
    )
    far = PERIOD // EDGE - 1
    (target,) = hbm(target)
    (sums,) = vmem(sums)
    edge_spec = pl.BlockSpec((noise_count, ROWS, EDGE), lambda i, _: (0, 0, i * far))
    edges, send = call(
        dose_edge_body,
        (f32(ROWS, 2 * EDGE), f32(ROWS, COARSE)),
        (sums, rows_other, target, got, got_last, *to_const(CROSS), *to_const(cross_t)),
        place=place,
        grid=(2,),
        in_specs=[
            pl.BlockSpec((1, ROWS, EDGE), lambda i, _: (0, 0, i * far)),
            fixed(ROWS, COARSE),
            pl.BlockSpec((ROWS, EDGE), lambda i, _: (0, i * far)),
            edge_spec,
            edge_spec,
        ]
        + [pl.BlockSpec((1, COARSE, EDGE), lambda i, place: (place[2], 0, i))] * 2
        + [pl.BlockSpec((1, EDGE, COARSE), lambda i, place: (place[2], i, 0))] * 2,
        out_specs=(pl.BlockSpec((ROWS, EDGE), lambda i, _: (0, i)), fixed(ROWS, COARSE)),
    )
    grad_other = lax.ppermute(send, "tile", swap)
    grad_own = call(
        dose_body,
        f32(ROWS, COARSE),
        (sums, edges, target, got_last, *to_const(OWN)),
        grid=(columns,),
        in_specs=[sums_spec, fixed(ROWS, 2 * EDGE), chunk(ROWS), got_spec]
        + [pl.BlockSpec((CHUNK, COARSE), lambda i: (i, 0))] * 2,
        out_specs=fixed(ROWS, COARSE),
    )
    grad = grad_own + grad_other
    grads = [grad] + shifted([grad] * len(shifts), shifts)
    blur_t, fold = jnp.asarray(BLUR.transpose(0, 2, 1), F32), jnp.asarray(UNFOLD.T, BF)
    ins = (*grads, field, kernels, *to_const(waves_t), *to_const(GRID.T), blur_t, *to_const(SPREAD), fold, *coef)
    spread = call(
        back_body,
        bf16(BLOCKS, RANK, FREQ),
        (place, weights, *hbm(*ins)),
        in_specs=[smem] * 2 + [anywhere] * len(ins),
        out_specs=pl.BlockSpec((BLOCKS, RANK, FREQ), lambda: (0, 0, 0)),
        scratch_shapes=[
            pltpu.VMEM((KERN * ROWS, COARSE), F32),
            pltpu.VMEM(BLUR.shape[:0:-1], F32),
            pltpu.VMEM((2,) + GRID.T.shape, BF),
            pltpu.VMEM(field_shape, F32),
            pltpu.VMEM((2,) + waves_t.shape[1:], BF),
            pltpu.VMEM(kernels.shape, F32),
            pltpu.VMEM(fold.shape, BF),
            pltpu.VMEM(COEF.shape, F32),
            pltpu.VMEM((2,) + SPREAD.shape, BF),
            pltpu.SemaphoreType.DMA((KERN + 13,)),
        ],
    )
    back = lax.all_to_all(spread, ("kern", "noise"), 0, 0, tiled=True)
    return call(
        final_body,
        f32(ROWS, PERIOD),
        (back, jnp.asarray(BASIS_BACK, F32), jnp.asarray(BASIS, F32), *(jnp.asarray(t) for t in np_split(LINE)), jnp.asarray(LAST, F32)),
    )


def solution(mesh):
    return jax.shard_map(
        body,
        mesh=mesh,
        in_specs=(
            P(("kern", "noise"), "tile"),
            P("kern", None, None, None),
            P("kern"),
            P(("kern", "noise"), "tile"),
            P("noise", "kern", "tile"),
        ),
        out_specs=P(("kern", "noise"), "tile"),
        check_vma=False,
    )
```

time: 120 us -> 113 us (0.942)
  Pallas kernels: 35.3 us -> 26.7 us
  starting transfers between devices: 18.3 us -> 21.7 us
  blocking collectives: 55.8 us -> 53.7 us
  local copies, waits for them, and re-layouts: 0.03 us -> 1.31 us
    pallas_call x4 -> x2, Pallas kernels: 19.8 us -> 4.89 us  [call(): pl.pallas_call(body, out_shape=out_shape, compiler_params=params, grid_sp...]
    pallas_call x4 -> x6, Pallas kernels: 15.5 us -> 21.8 us  [call(): pl.pallas_call(body, out_shape=out_shape, compiler_params=params, **kw)]
    ppermute x9, starting transfers between devices: 10.6 us -> 12.9 us  [shifted(): lax.ppermute(value, 'kern', [(source, (source + shift) % count) for sourc...]
    all_to_all x1, blocking collectives: 18.4 us -> 16.3 us  [body(): back = lax.all_to_all(spread, ('kern', 'noise'), 0, 0, tiled=True)]
    ppermute x1, starting transfers between devices: 0.6 us -> 1.92 us  [body(): grad_other = lax.ppermute(send, 'tile', swap)]
    unnamed x12 -> x36, local copies, waits for them, and re-layouts: 0.03 us -> 1.31 us
  transfers between devices with their start and end apart: 12 -> 12, of which waited for: 7 -> 7; matrix products, arithmetic and copies ran while one was open for 0% -> 0% of each run, Pallas kernels for 15% -> 12%
where the time goes in v4:
time: 113 us
  blocking collectives  53.7 us (48%)
  Pallas kernels  26.7 us (24%)
  starting transfers between devices  21.7 us (19%)
  waiting for transfers between devices  9.38 us (8%)
  local copies, waits for them, and re-layouts  1.31 us (1%)
    all_to_all x1, blocking collectives, body(): got = lax.all_to_all(moved_first, 'noise', 0, 0, tiled=True)  37.4 us
    pallas_call x6, Pallas kernels, call(): pl.pallas_call(body, out_shape=out_shape, compiler_params=params, **kw)  21.8 us
    all_to_all x1, blocking collectives, body(): back = lax.all_to_all(spread, ('kern', 'noise'), 0, 0, tiled=True)  16.3 us
    ppermute x9, starting transfers between devices, shifted(): lax.ppermute(value, 'kern', [(source, (source + shift) % count) for sourc...  12.9 us
    ppermute x9, waiting for transfers between devices, shifted(): lax.ppermute(value, 'kern', [(source, (source + shift) % count) for sourc...  9.37 us
    pallas_call x2, Pallas kernels, call(): pl.pallas_call(body, out_shape=out_shape, compiler_params=params, grid_sp...  4.89 us
    all_to_all x1, starting transfers between devices, body(): got_last = lax.all_to_all(moved, 'noise', 0, 0, tiled=True)  4.57 us
    ppermute x1, starting transfers between devices, body(): rows_other = lax.ppermute(rows, 'tile', swap)  2.32 us
  transfers between devices with their start and end apart: 12, of which 7 were waited for; matrix products, arithmetic and copies ran while one was open for 0% of the time, Pallas kernels for 12%

profile of v4, /device:TPU:1, one launch (start us, length us, event | category | flops | bytes accessed | tf_op | source)
XLA Modules:
  0.0 113.1 jit_solution(4058671308244747278)
XLA Ops:
  0.0 0.1 pad_add_fusion._.place_ref
  0.1 3.9 %shard_map.370 = (bf16[16,32,2176]{2,1,0:T(8,128)(2,1)}, bf16[16,32,2048]{2,1,0:T(8,128)(2,1)}) custom-call(f32[32,2048]{1,0:T(8,128)} %mask_ref.1, f32[16,32]{1,0:T(8,128)} %constant.83.clone.basis_ref, bf16[2048,128]{1,0:T(8,128)(2,1)} %constant.81.clone.lh_ref, bf16[2048,128]{1,0:T(8,128)(2,1)} %constant.82.clone.ll_ref, ...), custom_call_target="tpu_custom_call" | custom-call | tf_op jit(solution)/shard_map/pallas_call | solution.py:166
  4.0 37.4 %all_to_all.15.got_ref.noise_ref.first_ref = bf16[16,32,2176]{2,1,0:T(8,128)(2,1)S(1)} all-to-all(bf16[16,32,2176]{2,1,0:T(8,128)(2,1)} %get-tuple-element.23), channel_id=1, replica_groups=mesh['tile'=2,'kern'=4,'noise'=16] {'noise'}, dimensions={0} | all-to-all | bytes 4456448 | tf_op jit(solution)/shard_map/all_to_all | solution.py:504
  41.4 0.0 copy-start.2
  41.4 0.0 copy-start.6
  41.4 4.6 %all-to-all-start.1 = ((bf16[16,32,2048]{2,1,0:T(8,128)(2,1)}), bf16[16,32,2048]{2,1,0:T(8,128)(2,1)}, u32[]{:S(2)}, u32[]{:S(2)}) async-start(bf16[16,32,2048]{2,1,0:T(8,128)(2,1)} %get-tuple-element.35), calls=%async_computation.1 | async-start | bytes 4194304 | tf_op jit(solution)/shard_map/all_to_all | solution.py:508
  46.0 0.0 copy-done.2
  46.0 0.0 copy-done.6
  46.0 0.0 copy-start.10
  46.0 2.2 %shard_map.371.refs_0_ = f32[256,128]{1,0:T(8,128)S(1)} custom-call(s32[3]{0:T(128)S(1)} %pad_add_fusion._.place_ref, bf16[16,32,2176]{2,1,0:T(8,128)(2,1)S(1)} %all_to_all.15.got_ref.noise_ref.first_ref, bf16[4,512,256]{2,1,0:T(8,128)(2,1)} %constant.86.clone.gh_ref, bf16[4,512,256]{2,1,0:T(8,128)(2,1)} %constant.87.clone.gl_ref, ...), custom_call_target="tpu_custom_call" | custom-call | tf_op jit(solution)/shard_map/pallas_call | solution.py:168
  48.2 0.0 copy-start.5
  48.2 0.0 copy-start
  48.2 0.0 copy-start.1
  48.2 2.1 %collective-permute-start.2 = (f32[256,128]{1,0:T(8,128)S(1)}, f32[256,128]{1,0:T(8,128)S(1)}, u32[]{:S(2)}, u32[]{:S(2)}) collective-permute-start(f32[256,128]{1,0:T(8,128)S(1)} %shard_map.371.refs_0_), channel_id=1, source_target_pairs={{0,48},{16,0},{32,16},{48,32},{1,49},{17,1},{33,17},{49,33},{2,50}... | collective-permute-start | bytes 393224 | tf_op jit(solution)/shard_map/ppermute | solution.py:461
  50.3 1.2 %collective-permute-start.1 = (f32[256,128]{1,0:T(8,128)S(1)}, f32[256,128]{1,0:T(8,128)S(1)}, u32[]{:S(2)}, u32[]{:S(2)}) collective-permute-start(f32[256,128]{1,0:T(8,128)S(1)} %shard_map.371.refs_0_), channel_id=1, source_target_pairs={{0,32},{16,48},{32,0},{48,16},{1,33},{17,49},{33,1},{49,17},{2,34}... | collective-permute-start | bytes 393224 | tf_op jit(solution)/shard_map/ppermute | solution.py:461
  51.6 0.5 collective-permute-start
  52.1 3.7 %collective-permute-done.2.refs_3_ = f32[256,128]{1,0:T(8,128)S(1)} collective-permute-done((f32[256,128]{1,0:T(8,128)S(1)}, f32[256,128]{1,0:T(8,128)S(1)}, u32[]{:S(2)}, u32[]{:S(2)}) %collective-permute-start.2) | collective-permute-done | bytes 131104 | tf_op jit(solution)/shard_map/ppermute | solution.py:461
  55.8 0.0 copy-start.12
  55.8 0.2 collective-permute-done.1.refs_2_
  56.0 0.0 copy-start.13
  56.0 0.7 collective-permute-done.refs_1_
  56.7 0.0 copy-done.5
  56.7 0.0 copy-done.12
  56.7 0.0 copy-done.13
  56.7 0.0 copy-start.14
  56.7 0.6 copy-done.14
  57.3 0.0 copy-done.10
  57.3 4.4 %shard_map.372 = (f32[576,512]{1,0:T(8,128)}, f32[32,256]{1,0:T(8,128)S(1)}, f32[32,256]{1,0:T(8,128)S(1)}, f32[32,256]{1,0:T(8,128)S(1)}, f32[32,256]{1,0:T(8,128)S(1)}) custom-call(s32[3]{0:T(128)S(1)} %pad_add_fusion._.place_ref, f32[6]{0:T(128)S(1)} %copy-done.10, f32[256,128]{1,0:T(8,128)} %copy-done.5, f32[256,128]{1,0:T(8,128)} %copy-done.14, ...), custom_call_target="tpu_custom_call" | custom-call | tf_op jit(solution)/shard_map/pallas_call | solution.py:166
  61.7 2.6 %collective-permute-start.3 = (f32[32,256]{1,0:T(8,128)S(1)}, f32[32,256]{1,0:T(8,128)S(1)}, u32[]{:S(2)}, u32[]{:S(2)}) collective-permute-start(f32[32,256]{1,0:T(8,128)S(1)} %get-tuple-element.31), channel_id=1, source_target_pairs={{0,16},{16,32},{32,48},{48,0},{1,17},{17,33},{33,49},{49,1},{2,18}... | collective-permute-start | bytes 98312 | tf_op jit(solution)/shard_map/ppermute | solution.py:461
  64.3 1.8 %collective-permute-start.4 = (f32[32,256]{1,0:T(8,128)S(1)}, f32[32,256]{1,0:T(8,128)S(1)}, u32[]{:S(2)}, u32[]{:S(2)}) collective-permute-start(f32[32,256]{1,0:T(8,128)S(1)} %get-tuple-element.32), channel_id=1, source_target_pairs={{0,32},{16,48},{32,0},{48,16},{1,33},{17,49},{33,1},{49,17},{2,34}... | collective-permute-start | bytes 98312 | tf_op jit(solution)/shard_map/ppermute | solution.py:461
  66.0 0.0 collective-permute-start.5
  66.0 0.0 collective-permute-done.3
  66.0 2.1 %collective-permute-done.4 = f32[32,256]{1,0:T(8,128)S(1)} collective-permute-done((f32[32,256]{1,0:T(8,128)S(1)}, f32[32,256]{1,0:T(8,128)S(1)}, u32[]{:S(2)}, u32[]{:S(2)}) %collective-permute-start.4) | collective-permute-done | bytes 32800 | tf_op jit(solution)/shard_map/ppermute | solution.py:461
  68.2 1.6 %collective-permute-done.5 = f32[32,256]{1,0:T(8,128)S(1)} collective-permute-done((f32[32,256]{1,0:T(8,128)S(1)}, f32[32,256]{1,0:T(8,128)S(1)}, u32[]{:S(2)}, u32[]{:S(2)}) %collective-permute-start.5) | collective-permute-done | bytes 32800 | tf_op jit(solution)/shard_map/ppermute | solution.py:461
  69.8 2.3 %collective-permute-start.6 = (f32[32,256]{1,0:T(8,128)S(1)}, f32[32,256]{1,0:T(8,128)S(1)}, u32[]{:S(2)}, u32[]{:S(2)}) collective-permute-start(f32[32,256]{1,0:T(8,128)S(1)} %add_add_fusion.rows_ref), channel_id=1, source_target_pairs={{0,64},{64,0},{1,65},{65,1},{2,66},{66,2},{3,67},{67,3},{4,68},{68... | collective-permute-start | bytes 98312 | tf_op jit(solution)/shard_map/ppermute | solution.py:552
  72.1 0.0 copy-done
  72.1 0.0 copy-done.1
  72.1 2.8 %shard_map.373.acid_ref.sums_ref = f32[4,32,2048]{2,1,0:T(8,128)S(1)} custom-call(f32[32,256]{1,0:T(8,128)S(1)} %add_add_fusion.rows_ref, bf16[256,2048]{1,0:T(8,128)(2,1)S(1)} %copy-done.1, bf16[256,2048]{1,0:T(8,128)(2,1)S(1)} %copy-done, bf16[16,32,2176]{2,1,0:T(8,128)(2,1)S(1)} %all_to_all.15.got_ref.noise_ref.first_ref), custom_call_target="tpu_custom_call" | custom-call | tf_op jit(solution)/shard_map/pallas_call | solution.py:166
  74.9 0.0 collective-permute-done.6.other_ref
  74.9 0.0 all-to-all-done.1.second_ref.noise_ref
  74.9 2.7 %shard_map.374 = (f32[32,256]{1,0:T(8,128)S(1)}, f32[32,256]{1,0:T(8,128)S(1)}) custom-call(s32[3]{0:T(128)S(1)} %pad_add_fusion._.place_ref, f32[4,32,2048]{2,1,0:T(8,128)S(1)} %shard_map.373.acid_ref.sums_ref, f32[32,256]{1,0:T(8,128)S(1)} %collective-permute-done.6.other_ref, bf16[32,2048]{1,0:T(8,128)(2,1)} %target_ref.1, ...), custom_call_target="tpu_custom_call" | custom-call | tf_op jit(solution)/shard_map/pallas_call | solution.py:168
  77.7 1.9 %collective-permute-start.7 = (f32[32,256]{1,0:T(8,128)S(1)}, f32[32,256]{1,0:T(8,128)S(1)}, u32[]{:S(2)}, u32[]{:S(2)}) collective-permute-start(f32[32,256]{1,0:T(8,128)S(1)} %get-tuple-element.37), channel_id=1, source_target_pairs={{0,64},{64,0},{1,65},{65,1},{2,66},{66,2},{3,67},{67,3},{4,68},{68... | collective-permute-start | bytes 98312 | tf_op jit(solution)/shard_map/ppermute | solution.py:584
  79.6 4.0 %shard_map.375 = f32[32,256]{1,0:T(8,128)S(1)} custom-call(f32[4,32,2048]{2,1,0:T(8,128)S(1)} %shard_map.373.acid_ref.sums_ref, f32[32,256]{1,0:T(8,128)S(1)} %get-tuple-element.36.edge_ref, bf16[32,2048]{1,0:T(8,128)(2,1)} %target_ref.1, bf16[16,32,2048]{2,1,0:T(8,128)(2,1)} %all-to-all-done.1.second_ref.noise_ref, ...), custom_call_target="tpu_custom_call" | custom-call | tf_op jit(solution)/shard_map/pallas_call | solution.py:166
  83.6 0.0 collective-permute-done.7
  83.6 0.0 copy-start.11
  83.6 3.0 %collective-permute-start.10 = (f32[32,256]{1,0:T(8,128)S(1)}, f32[32,256]{1,0:T(8,128)S(1)}, u32[]{:S(2)}, u32[]{:S(2)}) collective-permute-start(f32[32,256]{1,0:T(8,128)S(1)} %add.15.refs_0_), channel_id=1, source_target_pairs={{0,48},{16,0},{32,16},{48,32},{1,49},{17,1},{33,17},{49,33},{2,50}... | collective-permute-start | bytes 98312 | tf_op jit(solution)/shard_map/ppermute | solution.py:461
  86.6 0.3 collective-permute-start.9
  86.9 1.4 %collective-permute-start.8 = (f32[32,256]{1,0:T(8,128)S(1)}, f32[32,256]{1,0:T(8,128)S(1)}, u32[]{:S(2)}, u32[]{:S(2)}) collective-permute-start(f32[32,256]{1,0:T(8,128)S(1)} %add.15.refs_0_), channel_id=1, source_target_pairs={{0,16},{16,32},{32,48},{48,0},{1,17},{17,33},{33,49},{49,1},{2,18}... | collective-permute-start | bytes 98312 | tf_op jit(solution)/shard_map/ppermute | solution.py:461
  88.3 0.1 collective-permute-done.10.refs_3_
  88.4 1.0 collective-permute-done.9.refs_2_
  89.4 0.0 collective-permute-done.8.refs_1_
  89.4 0.0 copy-done.11
  89.4 0.0 copy-done.15
  89.4 0.6 copy-done.16
  90.0 0.0 copy-done.17
  90.0 0.0 copy-start.9
  90.0 5.6 %shard_map.376 = bf16[64,16,128]{2,1,0:T(8,128)(2,1)S(1)} custom-call(s32[3]{0:T(128)S(1)} %pad_add_fusion._.place_ref, f32[6]{0:T(128)S(1)} %copy-done.10, f32[32,256]{1,0:T(8,128)} %copy-done.11, f32[32,256]{1,0:T(8,128)} %copy-done.17, f32[32,256]{1,0:T(8,128)} %copy-done.16, f32[32,256]{1,0:T(8,128)} %copy-done.15, ...), custom_call_target="tpu_custom_call" | custom-call | tf_op jit(solution)/shard_map/pallas_call | solution.py:166
  95.6 16.3 %all_to_all.16.got_ref = bf16[64,16,128]{2,1,0:T(8,128)(2,1)S(1)} all-to-all(bf16[64,16,128]{2,1,0:T(8,128)(2,1)S(1)} %shard_map.376), channel_id=1, replica_groups=mesh['tile'=2,'kern'=4,'noise'=16] {'kern','noise'}, dimensions={0} | all-to-all | bytes 524288 | tf_op jit(solution)/shard_map/all_to_all | solution.py:617
  111.9 0.0 copy-done.3
  111.9 0.0 copy-done.4
  111.9 0.0 copy-done.7
  112.0 0.0 copy-done.8
  112.0 0.0 copy-done.9
  112.0 1.2 %shard_map.377 = f32[32,2048]{1,0:T(8,128)} custom-call(bf16[64,16,128]{2,1,0:T(8,128)(2,1)S(1)} %all_to_all.16.got_ref, f32[32,16]{1,0:T(8,128)S(1)} %copy-done.9, f32[32,128]{1,0:T(8,128)S(1)} %copy-done.8, bf16[128,2048]{1,0:T(8,128)(2,1)S(1)} %copy-done.4, bf16[128,2048]{1,0:T(8,128)(2,1)S(1)} %copy-done.3, f32[1,2048]{1,0:T(1,128)S(1)} %copy-done.7), custom_call_target="tpu_custom_call" | custom-call | tf_op jit(solution)/shard_map/pallas_call | solution.py:166
  (9 shorter events, 0.0 us)
Async XLA Ops:
  41.4 4.6 %copy-start.2 = (f32[2,128,128]{2,1,0:T(8,128)S(1)}, f32[2,128,128]{2,1,0:T(8,128)}, u32[]{:S(2)}) copy-start(f32[2,128,128]{2,1,0:T(8,128)} %constant.85.clone.coef_ref.refs_14_) | copy-start | bytes 393220
  41.4 4.6 %copy-start.6 = (bf16[128,256]{1,0:T(8,128)(2,1)S(1)}, bf16[128,256]{1,0:T(8,128)(2,1)}, u32[]{:S(2)}) copy-start(bf16[128,256]{1,0:T(8,128)(2,1)} %constant.88.clone.unfold_ref) | copy-start | bytes 196612
  41.4 33.5 %all-to-all-start.1 = ((bf16[16,32,2048]{2,1,0:T(8,128)(2,1)}), bf16[16,32,2048]{2,1,0:T(8,128)(2,1)}, u32[]{:S(2)}, u32[]{:S(2)}) async-start(bf16[16,32,2048]{2,1,0:T(8,128)(2,1)} %get-tuple-element.35), calls=%async_computation.1 | async-start | bytes 4194304 | tf_op jit(solution)/shard_map/all_to_all | solution.py:508
  46.0 11.3 %copy-start.10 = (f32[6]{0:T(128)S(1)}, f32[6]{0:T(128)}, u32[]{:S(2)}) copy-start(f32[6]{0:T(128)} %weight_ref.1) | copy-start | bytes 76
  48.2 8.5 %copy-start.5 = (f32[256,128]{1,0:T(8,128)}, f32[256,128]{1,0:T(8,128)S(1)}, u32[]{:S(2)}) copy-start(f32[256,128]{1,0:T(8,128)S(1)} %shard_map.371.refs_0_) | copy-start | bytes 393220
  48.2 23.9 %copy-start = (bf16[256,2048]{1,0:T(8,128)(2,1)S(1)}, bf16[256,2048]{1,0:T(8,128)(2,1)}, u32[]{:S(2)}) copy-start(bf16[256,2048]{1,0:T(8,128)(2,1)} %constant.95.clone.ol_ref) | copy-start | bytes 3145732
  48.2 23.9 %copy-start.1 = (bf16[256,2048]{1,0:T(8,128)(2,1)S(1)}, bf16[256,2048]{1,0:T(8,128)(2,1)}, u32[]{:S(2)}) copy-start(bf16[256,2048]{1,0:T(8,128)(2,1)} %constant.94.clone.oh_ref) | copy-start | bytes 3145732
  48.2 7.6 %collective-permute-start.2 = (f32[256,128]{1,0:T(8,128)S(1)}, f32[256,128]{1,0:T(8,128)S(1)}, u32[]{:S(2)}, u32[]{:S(2)}) collective-permute-start(f32[256,128]{1,0:T(8,128)S(1)} %shard_map.371.refs_0_), channel_id=1, source_target_pairs={{0,48},{16,0},{32,16},{48,32},{1,49},{17,1},{33,17},{49,33},{2,50}... | collective-permute-start | bytes 393224 | tf_op jit(solution)/shard_map/ppermute | solution.py:461
  50.3 5.6 %collective-permute-start.1 = (f32[256,128]{1,0:T(8,128)S(1)}, f32[256,128]{1,0:T(8,128)S(1)}, u32[]{:S(2)}, u32[]{:S(2)}) collective-permute-start(f32[256,128]{1,0:T(8,128)S(1)} %shard_map.371.refs_0_), channel_id=1, source_target_pairs={{0,32},{16,48},{32,0},{48,16},{1,33},{17,49},{33,1},{49,17},{2,34}... | collective-permute-start | bytes 393224 | tf_op jit(solution)/shard_map/ppermute | solution.py:461
  51.6 5.1 %collective-permute-start = (f32[256,128]{1,0:T(8,128)S(1)}, f32[256,128]{1,0:T(8,128)S(1)}, u32[]{:S(2)}, u32[]{:S(2)}) collective-permute-start(f32[256,128]{1,0:T(8,128)S(1)} %shard_map.371.refs_0_), channel_id=1, source_target_pairs={{0,16},{16,32},{32,48},{48,0},{1,17},{17,33},{33,49},{49,1},{2,18}... | collective-permute-start | bytes 393224 | tf_op jit(solution)/shard_map/ppermute | solution.py:461
  55.8 0.9 copy-start.12
  56.0 0.7 copy-start.13
  56.7 0.6 copy-start.14
  61.7 4.3 %collective-permute-start.3 = (f32[32,256]{1,0:T(8,128)S(1)}, f32[32,256]{1,0:T(8,128)S(1)}, u32[]{:S(2)}, u32[]{:S(2)}) collective-permute-start(f32[32,256]{1,0:T(8,128)S(1)} %get-tuple-element.31), channel_id=1, source_target_pairs={{0,16},{16,32},{32,48},{48,0},{1,17},{17,33},{33,49},{49,1},{2,18}... | collective-permute-start | bytes 98312 | tf_op jit(solution)/shard_map/ppermute | solution.py:461
  64.3 3.9 %collective-permute-start.4 = (f32[32,256]{1,0:T(8,128)S(1)}, f32[32,256]{1,0:T(8,128)S(1)}, u32[]{:S(2)}, u32[]{:S(2)}) collective-permute-start(f32[32,256]{1,0:T(8,128)S(1)} %get-tuple-element.32), channel_id=1, source_target_pairs={{0,32},{16,48},{32,0},{48,16},{1,33},{17,49},{33,1},{49,17},{2,34}... | collective-permute-start | bytes 98312 | tf_op jit(solution)/shard_map/ppermute | solution.py:461
  66.0 3.7 %collective-permute-start.5 = (f32[32,256]{1,0:T(8,128)S(1)}, f32[32,256]{1,0:T(8,128)S(1)}, u32[]{:S(2)}, u32[]{:S(2)}) collective-permute-start(f32[32,256]{1,0:T(8,128)S(1)} %get-tuple-element.33), channel_id=1, source_target_pairs={{0,48},{16,0},{32,16},{48,32},{1,49},{17,1},{33,17},{49,33},{2,50}... | collective-permute-start | bytes 98312 | tf_op jit(solution)/shard_map/ppermute | solution.py:461
  69.8 5.1 %collective-permute-start.6 = (f32[32,256]{1,0:T(8,128)S(1)}, f32[32,256]{1,0:T(8,128)S(1)}, u32[]{:S(2)}, u32[]{:S(2)}) collective-permute-start(f32[32,256]{1,0:T(8,128)S(1)} %add_add_fusion.rows_ref), channel_id=1, source_target_pairs={{0,64},{64,0},{1,65},{65,1},{2,66},{66,2},{3,67},{67,3},{4,68},{68... | collective-permute-start | bytes 98312 | tf_op jit(solution)/shard_map/ppermute | solution.py:552
  77.7 5.9 %collective-permute-start.7 = (f32[32,256]{1,0:T(8,128)S(1)}, f32[32,256]{1,0:T(8,128)S(1)}, u32[]{:S(2)}, u32[]{:S(2)}) collective-permute-start(f32[32,256]{1,0:T(8,128)S(1)} %get-tuple-element.37), channel_id=1, source_target_pairs={{0,64},{64,0},{1,65},{65,1},{2,66},{66,2},{3,67},{67,3},{4,68},{68... | collective-permute-start | bytes 98312 | tf_op jit(solution)/shard_map/ppermute | solution.py:584
  83.6 5.8 %copy-start.11 = (f32[32,256]{1,0:T(8,128)}, f32[32,256]{1,0:T(8,128)S(1)}, u32[]{:S(2)}) copy-start(f32[32,256]{1,0:T(8,128)S(1)} %add.15.refs_0_) | copy-start | bytes 98308
  83.6 4.8 %collective-permute-start.10 = (f32[32,256]{1,0:T(8,128)S(1)}, f32[32,256]{1,0:T(8,128)S(1)}, u32[]{:S(2)}, u32[]{:S(2)}) collective-permute-start(f32[32,256]{1,0:T(8,128)S(1)} %add.15.refs_0_), channel_id=1, source_target_pairs={{0,48},{16,0},{32,16},{48,32},{1,49},{17,1},{33,17},{49,33},{2,50}... | collective-permute-start | bytes 98312 | tf_op jit(solution)/shard_map/ppermute | solution.py:461
  86.6 2.8 %collective-permute-start.9 = (f32[32,256]{1,0:T(8,128)S(1)}, f32[32,256]{1,0:T(8,128)S(1)}, u32[]{:S(2)}, u32[]{:S(2)}) collective-permute-start(f32[32,256]{1,0:T(8,128)S(1)} %add.15.refs_0_), channel_id=1, source_target_pairs={{0,32},{16,48},{32,0},{48,16},{1,33},{17,49},{33,1},{49,17},{2,34}... | collective-permute-start | bytes 98312 | tf_op jit(solution)/shard_map/ppermute | solution.py:461
  86.9 2.5 %collective-permute-start.8 = (f32[32,256]{1,0:T(8,128)S(1)}, f32[32,256]{1,0:T(8,128)S(1)}, u32[]{:S(2)}, u32[]{:S(2)}) collective-permute-start(f32[32,256]{1,0:T(8,128)S(1)} %add.15.refs_0_), channel_id=1, source_target_pairs={{0,16},{16,32},{32,48},{48,0},{1,17},{17,33},{33,49},{49,1},{2,18}... | collective-permute-start | bytes 98312 | tf_op jit(solution)/shard_map/ppermute | solution.py:461
  88.4 1.0 copy-start.15
  89.4 0.6 copy-start.16
  89.4 0.6 copy-start.17
  90.0 21.9 %copy-start.3 = (bf16[128,2048]{1,0:T(8,128)(2,1)S(1)}, bf16[128,2048]{1,0:T(8,128)(2,1)}, u32[]{:S(2)}) copy-start(bf16[128,2048]{1,0:T(8,128)(2,1)} %constant.113.clone.wl_ref) | copy-start | bytes 1572868
  90.0 21.9 %copy-start.4 = (bf16[128,2048]{1,0:T(8,128)(2,1)S(1)}, bf16[128,2048]{1,0:T(8,128)(2,1)}, u32[]{:S(2)}) copy-start(bf16[128,2048]{1,0:T(8,128)(2,1)} %constant.112.clone.wh_ref) | copy-start | bytes 1572868
  90.0 21.9 %copy-start.7 = (f32[1,2048]{1,0:T(1,128)S(1)}, f32[1,2048]{1,0:T(1,128)}, u32[]{:S(2)}) copy-start(f32[1,2048]{1,0:T(1,128)} %constant.84.clone.last_ref) | copy-start | bytes 24580
  90.0 21.9 %copy-start.8 = (f32[32,128]{1,0:T(8,128)S(1)}, f32[32,128]{1,0:T(8,128)}, u32[]{:S(2)}) copy-start(f32[32,128]{1,0:T(8,128)} %constant.111.clone.basis_ref) | copy-start | bytes 49156
  90.0 22.0 %copy-start.9 = (f32[32,16]{1,0:T(8,128)S(1)}, f32[32,16]{1,0:T(8,128)}, u32[]{:S(2)}) copy-start(f32[32,16]{1,0:T(8,128)} %constant.110.clone.back_ref) | copy-start | bytes 6148

commit v5 on v4

--- a/solution.py
+++ b/solution.py
@@ -181,6 +181,16 @@
 PARTS = 4
 
 
+def fetches(sources, targets, sems):
+    copies = [
+        pltpu.make_async_copy(source, target, sems.at[index])
+        for index, (source, target) in enumerate(zip(sources, targets))
+    ]
+    for copy in copies:
+        copy.start()
+    return copies
+
+
 def front_body(mask_ref, basis_ref, lh_ref, ll_ref, last_ref, noise_ref, first_ref, second_ref, *scratch):
     mask, basis, lh, ll, last, first, second, sems = scratch
     tables = [
@@ -283,7 +293,7 @@
     copies[9].wait()
     total_ref[...] = dot3(split(blur[...]), split(total))
     for shift, piece_ref in enumerate(piece_refs):
-        group = lax.rem(place_ref[0] + shift, KERN)
+        group = jnp.bitwise_xor(place_ref[0], shift)
         piece_ref[...] = total_ref[pl.ds(pl.multiple_of(group * ROWS, ROWS), ROWS)]
     for store in stores:
         store.wait()
@@ -323,23 +333,70 @@
     return (1.0 / 16.0) * (sum_q * inner + 1.25 * sum_qu)
 
 
-def dose_edge_body(
-    _, acid_ref, other_ref, target_ref, first_ref, second_ref, ch_ref, cl_ref, th_ref, tl_ref, grad_ref, send_ref
-):
-    halo = dot3(split(other_ref[...]), (ch_ref[0], cl_ref[0]))
-    for place in places(EDGE):
-        acid = acid_ref[(0,) + place] + halo[place]
-        zero = jnp.zeros(acid.shape, F32)
-        sums = sample_sums(first_ref, place, acid, (zero, zero, zero))
-        sums = sample_sums(second_ref, place, acid, sums)
-        grad_ref[place] = acid_grad(sums, target_ref[place])
-    part = dot3(split(grad_ref[...]), (th_ref[0], tl_ref[0]))
-    send_ref[...] = jnp.where(pl.program_id(0) == 0, 0.0, send_ref[...]) + part
-
-
-def dose_body(sums_ref, edge_ref, target_ref, noise_ref, oh_ref, ol_ref, out_ref):
+def dose_edge_body(place_ref, sums_ref, other_ref, *refs):
+    ins, (grad_ref, send_ref), (held, target, cross, cross_t, sems) = refs[:7], refs[7:9], refs[9:]
+    target_ref, first_ref, second_ref, ch_ref, cl_ref, th_ref, tl_ref = ins
+    tile = place_ref[2]
+    sides = [pl.ds(0, EDGE), pl.ds(PERIOD - EDGE, EDGE)]
+    copies = fetches(
+        [ch_ref.at[tile], cl_ref.at[tile]]
+        + [ref.at[:, :, side] for side in sides for ref in (first_ref, second_ref)]
+        + [target_ref.at[:, side] for side in sides]
+        + [th_ref.at[tile], tl_ref.at[tile]],
+        [cross.at[0], cross.at[1]]
+        + [held.at[index] for index in range(4)]
+        + [target.at[index] for index in range(2)]
+        + [cross_t.at[0], cross_t.at[1]],
+        sems,
+    )
+    for copy in copies[:2]:
+        copy.wait()
+    halo = dot3(split(other_ref[...]), (cross[0], cross[1]))
+    for copy in copies[2:8]:
+        copy.wait()
+    grads = []
+    for side in range(2):
+        columns = []
+        for row, lanes in places(EDGE):
+            place = (row, lanes)
+            there = slice(side * (PERIOD - EDGE), side * (PERIOD - EDGE) + EDGE)
+            acid = sums_ref[0, row, there] + halo[row, side * EDGE : (side + 1) * EDGE]
+            zero = jnp.zeros(acid.shape, F32)
+            sums = sample_sums(held.at[2 * side], place, acid, (zero, zero, zero))
+            sums = sample_sums(held.at[2 * side + 1], place, acid, sums)
+            columns.append(acid_grad(sums, target[(side,) + place]))
+        grads.append(jnp.concatenate(columns, 0))
+    grad = jnp.concatenate(grads, 1)
+    grad_ref[...] = grad
+    for copy in copies[8:]:
+        copy.wait()
+    send_ref[...] = dot3(split(grad), (cross_t[0], cross_t[1]))
+
+
+def dose_body(place_ref, sums_ref, edge_ref, target_ref, noise_ref, oh_ref, ol_ref, *refs):
     step = pl.program_id(0)
     last = pl.num_programs(0) - 1
+    ins, out_ref, outs, sems = refs[:11], refs[11], refs[12:20], refs[20]
+    field_ref, kern_ref, wh_ref, wl_ref, gh_ref, gl_ref, blur_ref, th_ref, tl_ref, fold_ref, coef_ref = ins
+    field, kern, wave, grid, blur, table, fold, coef = outs
+    block = place_ref[1]
+    copies = [
+        pltpu.make_async_copy(source, held, sems.at[index])
+        for index, (source, held) in enumerate(
+            zip(
+                [field_ref, kern_ref, wh_ref.at[block], wl_ref.at[block], gh_ref, gl_ref]
+                + [blur_ref.at[block], th_ref, tl_ref, fold_ref, coef_ref],
+                [field, kern, wave.at[0], wave.at[1], grid.at[0], grid.at[1]]
+                + [blur, table.at[0], table.at[1], fold, coef],
+            )
+        )
+    ]
+
+    @pl.when(step == 0)
+    def _():
+        for copy in copies:
+            copy.start()
+
     total = jnp.where(step == 0, 0.0, out_ref[...])
     for col in range(0, CHUNK, LANES):
         lanes = slice(col, col + LANES)
@@ -357,45 +414,23 @@
         total = total + dot3(split(grad), (oh_ref[lanes], ol_ref[lanes]))
     out_ref[...] = total
 
-
-def fetches(sources, targets, sems):
-    copies = [
-        pltpu.make_async_copy(source, target, sems.at[index])
-        for index, (source, target) in enumerate(zip(sources, targets))
-    ]
-    for copy in copies:
-        copy.start()
-    return copies
+    @pl.when(step == last)
+    def _():
+        for copy in copies:
+            copy.wait()
 
 
 def back_body(place_ref, weight_ref, *refs):
-    piece_refs, ins = refs[:KERN], refs[KERN : KERN + 11]
-    field_ref, kern_ref, wh_ref, wl_ref, gh_ref, gl_ref, blur_ref, th_ref, tl_ref, fold_ref, coef_ref = ins
-    out_ref, rows, blur, grid, field, wave, kern, fold, coef, table, sems = refs[KERN + 11 :]
-    block = place_ref[1]
-    group = [lax.rem(place_ref[0] - shift + KERN, KERN) * ROWS for shift in range(KERN)]
-    size = 2 * KERN * REACH
-    pairs = [pl.ds(pair * size, size) for pair in range(PAIRS)]
-    copies = fetches(
-        list(piece_refs)
-        + [blur_ref.at[block], field_ref.at[pairs[0]], gh_ref, gl_ref, wh_ref.at[block], wl_ref.at[block], kern_ref]
-        + [field_ref.at[pair] for pair in pairs[1:]]
-        + [fold_ref, coef_ref, th_ref, tl_ref],
-        [rows.at[pl.ds(pl.multiple_of(first, ROWS), ROWS)] for first in group]
-        + [blur, field.at[pairs[0]], grid.at[0], grid.at[1], wave.at[0], wave.at[1], kern]
-        + [field.at[pair] for pair in pairs[1:]]
-        + [fold, coef, table.at[0], table.at[1]],
-        sems,
-    )
-    for copy in copies[:5]:
-        copy.wait()
+    piece_refs, (field, kern, wave, grid, blur, table, fold, coef) = refs[:KERN], refs[KERN : KERN + 8]
+    out_ref, rows = refs[KERN + 8 :]
+    for shift, piece_ref in enumerate(piece_refs):
+        first = jnp.bitwise_xor(place_ref[0], shift) * ROWS
+        rows[pl.ds(pl.multiple_of(first, ROWS), ROWS)] = piece_ref[...]
     part = 2.0 * dot3(split(blur[...]), split(rows[...]))
     grad = jnp.concatenate([part, part], 1)
     half = KERN * REACH
     sum_re = sum_im = None
     for pair in range(PAIRS):
-        for copy in copies[5:8] if pair == 0 else copies[10 + pair : 11 + pair]:
-            copy.wait()
         pulled = [
             field[index * half : (index + 1) * half] * (weight_ref[index] * grad)
             for index in (2 * pair, 2 * pair + 1)
@@ -409,9 +444,6 @@
                 left = lefts[first : first + REACH]
                 column += [left[:, :FREQ], left[:, FREQ:]]
             stack.append(jnp.concatenate(column, 0))
-        if pair == 0:
-            for copy in copies[8:11]:
-                copy.wait()
         near = dot3((wave[0], wave[1]), split(jnp.concatenate(stack, 1)))
         for index in range(2):
             near_re = near[:FREQ, index * FREQ : (index + 1) * FREQ]
@@ -425,8 +457,6 @@
     mix = jnp.concatenate(
         [jnp.concatenate([grad_re, -grad_im], 1), jnp.concatenate([-grad_im, -grad_re], 1)], 0
     )
-    for copy in copies[13:]:
-        copy.wait()
     folded = dot_exact(split(mix), fold[...])
     coef_re, coef_im = coef[0], coef[1]
     by_cos, by_sin = grad_im[:, :1], grad_re[:, :1]
@@ -458,7 +488,7 @@
 def shifted(values, shifts):
     count = lax.axis_size("kern")
     return [
-        lax.ppermute(value, "kern", [(source, (source + shift) % count) for source in range(count)])
+        lax.ppermute(value, "kern", [(source, source ^ shift) for source in range(count)])
         for value, shift in zip(values, shifts)
     ]
 
@@ -516,7 +546,7 @@
     spec = call(
         spectrum_body,
         f32(2 * FREQ, FREQ),
-        (got, *to_const(GATHER_OWN), jnp.asarray(UNFOLD, BF), jnp.asarray(COEF, F32)),
+        (got, *near_const(GATHER_OWN), jnp.asarray(UNFOLD, BF), jnp.asarray(COEF, F32)),
         place=place,
         grid=(1,),
         in_specs=[pl.BlockSpec((noise_count, ROWS, FREQ), lambda i, _: (0, 0, PERIOD // FREQ))]
@@ -560,59 +590,59 @@
         in_specs=[fixed(ROWS, COARSE)] + [chunk(COARSE)] * 2 + [got_spec],
         out_specs=sums_spec,
     )
-    far = PERIOD // EDGE - 1
     (target,) = hbm(target)
     (sums,) = vmem(sums)
-    edge_spec = pl.BlockSpec((noise_count, ROWS, EDGE), lambda i, _: (0, 0, i * far))
+    inside = pl.BlockSpec(memory_space=pltpu.VMEM)
+    piece_spec = pl.BlockSpec((ROWS, COARSE), lambda: (0, 0))
     edges, send = call(
         dose_edge_body,
         (f32(ROWS, 2 * EDGE), f32(ROWS, COARSE)),
-        (sums, rows_other, target, got, got_last, *to_const(CROSS), *to_const(cross_t)),
-        place=place,
-        grid=(2,),
-        in_specs=[
-            pl.BlockSpec((1, ROWS, EDGE), lambda i, _: (0, 0, i * far)),
-            fixed(ROWS, COARSE),
-            pl.BlockSpec((ROWS, EDGE), lambda i, _: (0, i * far)),
-            edge_spec,
-            edge_spec,
-        ]
-        + [pl.BlockSpec((1, COARSE, EDGE), lambda i, place: (place[2], 0, i))] * 2
-        + [pl.BlockSpec((1, EDGE, COARSE), lambda i, place: (place[2], i, 0))] * 2,
-        out_specs=(pl.BlockSpec((ROWS, EDGE), lambda i, _: (0, i)), fixed(ROWS, COARSE)),
+        (place, sums, rows_other, target, got, got_last, *to_const(CROSS), *to_const(cross_t)),
+        in_specs=[smem, inside, piece_spec, anywhere]
+        + [pl.BlockSpec(memory_space=pl.ANY)] * 2
+        + [anywhere] * 4,
+        out_specs=(piece_spec, piece_spec),
+        scratch_shapes=[
+            pltpu.VMEM((4, noise_count, ROWS, EDGE), BF),
+            pltpu.VMEM((2, ROWS, EDGE), BF),
+            pltpu.VMEM((2,) + CROSS.shape[1:], BF),
+            pltpu.VMEM((2,) + cross_t.shape[1:], BF),
+            pltpu.SemaphoreType.DMA((10,)),
+        ],
     )
     grad_other = lax.ppermute(send, "tile", swap)
-    grad_own = call(
+    blur_t, fold = jnp.asarray(BLUR.transpose(0, 2, 1), F32), jnp.asarray(UNFOLD.T, BF)
+    ins = (field, kernels, *to_const(waves_t), *to_const(GRID.T), blur_t, *to_const(SPREAD), fold, *coef)
+    held = [
+        (field_shape, F32),
+        (kernels.shape, F32),
+        ((2,) + waves_t.shape[1:], BF),
+        ((2,) + GRID.T.shape, BF),
+        (BLUR.shape[:0:-1], F32),
+        ((2,) + SPREAD.shape, BF),
+        (fold.shape, BF),
+        (COEF.shape, F32),
+    ]
+    grad_own, *staged = call(
         dose_body,
-        f32(ROWS, COARSE),
-        (sums, edges, target, got_last, *to_const(OWN)),
+        (f32(ROWS, COARSE),) + tuple(pltpu.VMEM(shape, dtype) for shape, dtype in held),
+        (place, sums, edges, target, got_last, *to_const(OWN), *hbm(*ins)),
         grid=(columns,),
-        in_specs=[sums_spec, fixed(ROWS, 2 * EDGE), chunk(ROWS), got_spec]
-        + [pl.BlockSpec((CHUNK, COARSE), lambda i: (i, 0))] * 2,
-        out_specs=fixed(ROWS, COARSE),
+        in_specs=[smem, sums_spec, fixed(ROWS, 2 * EDGE), chunk(ROWS), got_spec]
+        + [pl.BlockSpec((CHUNK, COARSE), lambda i: (i, 0))] * 2
+        + [anywhere] * len(ins),
+        out_specs=(fixed(ROWS, COARSE),) + (inside,) * len(held),
+        scratch_shapes=[pltpu.SemaphoreType.DMA((len(ins),))],
     )
     grad = grad_own + grad_other
     grads = [grad] + shifted([grad] * len(shifts), shifts)
-    blur_t, fold = jnp.asarray(BLUR.transpose(0, 2, 1), F32), jnp.asarray(UNFOLD.T, BF)
-    ins = (*grads, field, kernels, *to_const(waves_t), *to_const(GRID.T), blur_t, *to_const(SPREAD), fold, *coef)
     spread = call(
         back_body,
         bf16(BLOCKS, RANK, FREQ),
-        (place, weights, *hbm(*ins)),
-        in_specs=[smem] * 2 + [anywhere] * len(ins),
+        (place, weights, *grads, *vmem(*staged)),
+        in_specs=[smem] * 2 + [piece_spec] * KERN + [inside] * len(held),
         out_specs=pl.BlockSpec((BLOCKS, RANK, FREQ), lambda: (0, 0, 0)),
-        scratch_shapes=[
-            pltpu.VMEM((KERN * ROWS, COARSE), F32),
-            pltpu.VMEM(BLUR.shape[:0:-1], F32),
-            pltpu.VMEM((2,) + GRID.T.shape, BF),
-            pltpu.VMEM(field_shape, F32),
-            pltpu.VMEM((2,) + waves_t.shape[1:], BF),
-            pltpu.VMEM(kernels.shape, F32),
-            pltpu.VMEM(fold.shape, BF),
-            pltpu.VMEM(COEF.shape, F32),
-            pltpu.VMEM((2,) + SPREAD.shape, BF),
-            pltpu.SemaphoreType.DMA((KERN + 13,)),
-        ],
+        scratch_shapes=[pltpu.VMEM((KERN * ROWS, COARSE), F32)],
     )
     back = lax.all_to_all(spread, ("kern", "noise"), 0, 0, tiled=True)
     return call(

time: 113 us -> 112 us (level)
  Pallas kernels: 26.7 us -> 24.5 us
  starting transfers between devices: 21.7 us -> 19.5 us
  waiting for transfers between devices: 9.38 us -> 11.4 us
  local copies, waits for them, and re-layouts: 1.31 us -> 2.56 us
    pallas_call x2 -> x1, Pallas kernels: 4.89 us -> 1.11 us  [call(): pl.pallas_call(body, out_shape=out_shape, compiler_params=params, grid_sp...]
    ppermute x9, starting transfers between devices: 12.9 us -> 10.4 us  [shifted(): lax.ppermute(value, 'kern', [(source, source ^ shift) for source in range...]
    ppermute x9, waiting for transfers between devices: 9.37 us -> 11.4 us  [shifted(): lax.ppermute(value, 'kern', [(source, source ^ shift) for source in range...]
    pallas_call x6 -> x7, Pallas kernels: 21.8 us -> 23.4 us  [call(): pl.pallas_call(body, out_shape=out_shape, compiler_params=params, **kw)]
    unnamed x36 -> x32, local copies, waits for them, and re-layouts: 1.31 us -> 2.56 us
  transfers between devices with their start and end apart: 12 -> 12, of which waited for: 7 -> 6; matrix products, arithmetic and copies ran while one was open for 0% -> 0% of each run, Pallas kernels for 12% -> 12%
where the time goes in v5:
time: 112 us; the launch traced here: 111 us
  blocking collectives  52.9 us (47%)
  Pallas kernels  24.5 us (22%)
  starting transfers between devices  19.5 us (17%)
  waiting for transfers between devices  11.4 us (10%)
  local copies, waits for them, and re-layouts  2.56 us (2%)
    all_to_all x1, blocking collectives, body(): got = lax.all_to_all(moved_first, 'noise', 0, 0, tiled=True)  37.4 us
    pallas_call x7, Pallas kernels, call(): pl.pallas_call(body, out_shape=out_shape, compiler_params=params, **kw)  23.4 us
    all_to_all x1, blocking collectives, body(): back = lax.all_to_all(spread, ('kern', 'noise'), 0, 0, tiled=True)  15.6 us
    ppermute x9, waiting for transfers between devices, shifted(): lax.ppermute(value, 'kern', [(source, source ^ shift) for source in range...  11.4 us
    ppermute x9, starting transfers between devices, shifted(): lax.ppermute(value, 'kern', [(source, source ^ shift) for source in range...  10.4 us
    all_to_all x1, starting transfers between devices, body(): got_last = lax.all_to_all(moved, 'noise', 0, 0, tiled=True)  4.57 us
    ppermute x1, starting transfers between devices, body(): rows_other = lax.ppermute(rows, 'tile', swap)  2.62 us
    unnamed x32, local copies, waits for them, and re-layouts  2.56 us
  transfers between devices with their start and end apart: 12, of which 6 were waited for; matrix products, arithmetic and copies ran while one was open for 0% of the time, Pallas kernels for 12%

profile of v5, /device:TPU:1, one launch (start us, length us, event | category | flops | bytes accessed | tf_op | source)
XLA Modules:
  0.0 111.2 jit_solution(9344724394716354435)
XLA Ops:
  0.0 0.1 pad_add_fusion._.place_ref
  0.1 4.0 %shard_map.370 = (bf16[16,32,2176]{2,1,0:T(8,128)(2,1)}, bf16[16,32,2048]{2,1,0:T(8,128)(2,1)}) custom-call(f32[32,2048]{1,0:T(8,128)} %mask_ref.1, f32[16,32]{1,0:T(8,128)} %constant.83.clone.basis_ref, bf16[2048,128]{1,0:T(8,128)(2,1)} %constant.81.clone.lh_ref, bf16[2048,128]{1,0:T(8,128)(2,1)} %constant.82.clone.ll_ref, ...), custom_call_target="tpu_custom_call" | custom-call | tf_op jit(solution)/shard_map/pallas_call | solution.py:166
  4.0 37.4 %all_to_all.15.got_ref.noise_ref.refs_1_ = bf16[16,32,2176]{2,1,0:T(8,128)(2,1)S(1)} all-to-all(bf16[16,32,2176]{2,1,0:T(8,128)(2,1)} %get-tuple-element.32), channel_id=1, replica_groups=mesh['tile'=2,'kern'=4,'noise'=16] {'noise'}, dimensions={0} | all-to-all | bytes 4456448 | tf_op jit(solution)/shard_map/all_to_all | solution.py:534
  41.4 0.0 copy-start
  41.4 0.0 copy-start.4
  41.4 4.6 %all-to-all-start.1 = ((bf16[16,32,2048]{2,1,0:T(8,128)(2,1)}), bf16[16,32,2048]{2,1,0:T(8,128)(2,1)}, u32[]{:S(2)}, u32[]{:S(2)}) async-start(bf16[16,32,2048]{2,1,0:T(8,128)(2,1)} %get-tuple-element.44), calls=%async_computation.1 | async-start | bytes 4194304 | tf_op jit(solution)/shard_map/all_to_all | solution.py:538
  46.0 0.0 copy-done
  46.0 0.0 copy-done.4
  46.0 0.0 copy-done.8
  46.0 0.0 copy-start.1
  46.0 1.2 %copy-done.1 = bf16[4,512,256]{2,1,0:T(8,128)(2,1)S(1)} copy-done((bf16[4,512,256]{2,1,0:T(8,128)(2,1)S(1)}, bf16[4,512,256]{2,1,0:T(8,128)(2,1)}, u32[]{:S(2)}) %copy-start.1) | copy-done | bytes 1048600
  47.2 0.0 copy-start.12
  47.2 1.1 %shard_map.371.refs_0_ = f32[256,128]{1,0:T(8,128)S(1)} custom-call(s32[3]{0:T(128)S(1)} %pad_add_fusion._.place_ref, bf16[16,32,2176]{2,1,0:T(8,128)(2,1)S(1)} %all_to_all.15.got_ref.noise_ref.refs_1_, bf16[4,512,256]{2,1,0:T(8,128)(2,1)S(1)} %copy-done.1, bf16[4,512,256]{2,1,0:T(8,128)(2,1)S(1)} %copy-done, bf16[128,256]{1,0:T(8,128)(2,1)S(1)} %copy-done.8, ...), custom_call_target="tpu_custom_call" | custom-call | tf_op jit(solution)/shard_map/pallas_call | solution.py:168
  48.4 0.0 copy-start.7
  48.4 0.0 copy-start.2
  48.4 0.0 copy-start.3
  48.4 3.2 %collective-permute-start.2 = (f32[256,128]{1,0:T(8,128)S(1)}, f32[256,128]{1,0:T(8,128)S(1)}, u32[]{:S(2)}, u32[]{:S(2)}) collective-permute-start(f32[256,128]{1,0:T(8,128)S(1)} %shard_map.371.refs_0_), channel_id=1, source_target_pairs={{0,48},{16,32},{32,16},{48,0},{1,49},{17,33},{33,17},{49,1},{2,50}... | collective-permute-start | bytes 393224 | tf_op jit(solution)/shard_map/ppermute | solution.py:491
  51.6 0.3 collective-permute-start.1
  51.9 0.2 collective-permute-start
  52.1 4.0 %collective-permute-done.2.refs_3_ = f32[256,128]{1,0:T(8,128)S(1)} collective-permute-done((f32[256,128]{1,0:T(8,128)S(1)}, f32[256,128]{1,0:T(8,128)S(1)}, u32[]{:S(2)}, u32[]{:S(2)}) %collective-permute-start.2) | collective-permute-done | bytes 131104 | tf_op jit(solution)/shard_map/ppermute | solution.py:491
  56.1 0.0 copy-start.13
  56.1 2.7 %collective-permute-done.1.refs_2_ = f32[256,128]{1,0:T(8,128)S(1)} collective-permute-done((f32[256,128]{1,0:T(8,128)S(1)}, f32[256,128]{1,0:T(8,128)S(1)}, u32[]{:S(2)}, u32[]{:S(2)}) %collective-permute-start.1) | collective-permute-done | bytes 131104 | tf_op jit(solution)/shard_map/ppermute | solution.py:491
  58.8 0.0 copy-start.14
  58.8 0.0 collective-permute-done.refs_1_
  58.8 0.0 copy-done.7
  58.8 0.0 copy-done.13
  58.8 0.6 copy-done.14
  59.5 0.0 copy-start.15
  59.5 0.6 copy-done.15
  60.1 0.0 copy-done.12
  60.1 4.4 %shard_map.372 = (f32[576,512]{1,0:T(8,128)}, f32[32,256]{1,0:T(8,128)S(1)}, f32[32,256]{1,0:T(8,128)S(1)}, f32[32,256]{1,0:T(8,128)S(1)}, f32[32,256]{1,0:T(8,128)S(1)}) custom-call(s32[3]{0:T(128)S(1)} %pad_add_fusion._.place_ref, f32[6]{0:T(128)S(1)} %copy-done.12, f32[256,128]{1,0:T(8,128)} %copy-done.7, f32[256,128]{1,0:T(8,128)} %copy-done.15, ...), custom_call_target="tpu_custom_call" | custom-call | tf_op jit(solution)/shard_map/pallas_call | solution.py:166
  64.5 0.4 collective-permute-start.3
  64.9 0.1 collective-permute-start.4
  65.0 1.7 %collective-permute-start.5 = (f32[32,256]{1,0:T(8,128)S(1)}, f32[32,256]{1,0:T(8,128)S(1)}, u32[]{:S(2)}, u32[]{:S(2)}) collective-permute-start(f32[32,256]{1,0:T(8,128)S(1)} %get-tuple-element.42), channel_id=1, source_target_pairs={{0,48},{16,32},{32,16},{48,0},{1,49},{17,33},{33,17},{49,1},{2,50}... | collective-permute-start | bytes 98312 | tf_op jit(solution)/shard_map/ppermute | solution.py:491
  66.7 0.0 collective-permute-done.3
  66.7 1.4 %collective-permute-done.4 = f32[32,256]{1,0:T(8,128)S(1)} collective-permute-done((f32[32,256]{1,0:T(8,128)S(1)}, f32[32,256]{1,0:T(8,128)S(1)}, u32[]{:S(2)}, u32[]{:S(2)}) %collective-permute-start.4) | collective-permute-done | bytes 32800 | tf_op jit(solution)/shard_map/ppermute | solution.py:491
  68.1 1.3 %collective-permute-done.5 = f32[32,256]{1,0:T(8,128)S(1)} collective-permute-done((f32[32,256]{1,0:T(8,128)S(1)}, f32[32,256]{1,0:T(8,128)S(1)}, u32[]{:S(2)}, u32[]{:S(2)}) %collective-permute-start.5) | collective-permute-done | bytes 32800 | tf_op jit(solution)/shard_map/ppermute | solution.py:491
  69.4 2.6 %collective-permute-start.6 = (f32[32,256]{1,0:T(8,128)S(1)}, f32[32,256]{1,0:T(8,128)S(1)}, u32[]{:S(2)}, u32[]{:S(2)}) collective-permute-start(f32[32,256]{1,0:T(8,128)S(1)} %add_add_fusion.rows_ref), channel_id=1, source_target_pairs={{0,64},{64,0},{1,65},{65,1},{2,66},{66,2},{3,67},{67,3},{4,68},{68... | collective-permute-start | bytes 98312 | tf_op jit(solution)/shard_map/ppermute | solution.py:582
  72.1 0.0 copy-done.2
  72.1 0.0 copy-done.3
  72.1 2.8 %shard_map.373.sums_ref = f32[4,32,2048]{2,1,0:T(8,128)S(1)} custom-call(f32[32,256]{1,0:T(8,128)S(1)} %add_add_fusion.rows_ref, bf16[256,2048]{1,0:T(8,128)(2,1)S(1)} %copy-done.3, bf16[256,2048]{1,0:T(8,128)(2,1)S(1)} %copy-done.2, bf16[16,32,2176]{2,1,0:T(8,128)(2,1)S(1)} %all_to_all.15.got_ref.noise_ref.refs_1_), custom_call_target="tpu_custom_call" | custom-call | tf_op jit(solution)/shard_map/pallas_call | solution.py:166
  74.9 0.0 collective-permute-done.6.other_ref
  74.9 0.0 all-to-all-done.1.refs_2_.noise_ref
  74.9 2.5 %shard_map.374 = (f32[32,256]{1,0:T(8,128)S(1)}, f32[32,256]{1,0:T(8,128)S(1)}) custom-call(s32[3]{0:T(128)S(1)} %pad_add_fusion._.place_ref, f32[4,32,2048]{2,1,0:T(8,128)S(1)} %shard_map.373.sums_ref, f32[32,256]{1,0:T(8,128)S(1)} %collective-permute-done.6.other_ref, bf16[32,2048]{1,0:T(8,128)(2,1)} %target_ref, ...), custom_call_target="tpu_custom_call" | custom-call | tf_op jit(solution)/shard_map/pallas_call | solution.py:166
  77.3 1.9 %collective-permute-start.7 = (f32[32,256]{1,0:T(8,128)S(1)}, f32[32,256]{1,0:T(8,128)S(1)}, u32[]{:S(2)}, u32[]{:S(2)}) collective-permute-start(f32[32,256]{1,0:T(8,128)S(1)} %get-tuple-element.48), channel_id=1, source_target_pairs={{0,64},{64,0},{1,65},{65,1},{2,66},{66,2},{3,67},{67,3},{4,68},{68... | collective-permute-start | bytes 98312 | tf_op jit(solution)/shard_map/ppermute | solution.py:613
  79.3 4.6 %shard_map.375 = (f32[32,256]{1,0:T(8,128)S(1)}, f32[576,512]{1,0:T(8,128)S(1)}, f32[6,2,128,128]{3,2,1,0:T(8,128)S(1)}, bf16[2,256,192]{2,1,0:T(8,128)(2,1)S(1)...) custom-call(s32[3]{0:T(128)S(1)} %pad_add_fusion._.place_ref, ...), custom_call_target="tpu_custom_call" | custom-call | tf_op jit(solution)/shard_map/pallas_call | solution.py:166
  83.9 0.0 collective-permute-done.7
  83.9 3.3 %collective-permute-start.10 = (f32[32,256]{1,0:T(8,128)S(1)}, f32[32,256]{1,0:T(8,128)S(1)}, u32[]{:S(2)}, u32[]{:S(2)}) collective-permute-start(f32[32,256]{1,0:T(8,128)S(1)} %add.15.refs_0_), channel_id=1, source_target_pairs={{0,48},{16,32},{32,16},{48,0},{1,49},{17,33},{33,17},{49,1},{2,50}... | collective-permute-start | bytes 98312 | tf_op jit(solution)/shard_map/ppermute | solution.py:491
  87.2 1.2 %collective-permute-start.9 = (f32[32,256]{1,0:T(8,128)S(1)}, f32[32,256]{1,0:T(8,128)S(1)}, u32[]{:S(2)}, u32[]{:S(2)}) collective-permute-start(f32[32,256]{1,0:T(8,128)S(1)} %add.15.refs_0_), channel_id=1, source_target_pairs={{0,32},{16,48},{32,0},{48,16},{1,33},{17,49},{33,1},{49,17},{2,34}... | collective-permute-start | bytes 98312 | tf_op jit(solution)/shard_map/ppermute | solution.py:491
  88.3 0.0 collective-permute-start.8
  88.3 0.4 collective-permute-done.10.refs_3_
  88.8 1.6 %collective-permute-done.9.refs_2_ = f32[32,256]{1,0:T(8,128)S(1)} collective-permute-done((f32[32,256]{1,0:T(8,128)S(1)}, f32[32,256]{1,0:T(8,128)S(1)}, u32[]{:S(2)}, u32[]{:S(2)}) %collective-permute-start.9) | collective-permute-done | bytes 32800 | tf_op jit(solution)/shard_map/ppermute | solution.py:491
  90.4 0.0 collective-permute-done.8.refs_1_
  90.4 0.0 copy-start.5
  90.4 0.0 copy-start.10
  90.4 0.0 copy-start.11
  90.4 4.0 %shard_map.376 = bf16[64,16,128]{2,1,0:T(8,128)(2,1)S(1)} custom-call(s32[3]{0:T(128)S(1)} %pad_add_fusion._.place_ref, f32[6]{0:T(128)S(1)} %copy-done.12, f32[32,256]{1,0:T(8,128)S(1)} %add.15.refs_0_, f32[32,256]{1,0:T(8,128)S(1)} %collective-permute-done.8.refs_1_, f32[32,256]{1,0:T(8,128)S(1)} %collective-permute-done.9.refs_2_, ...), custom_call_target="tpu_custom_call" | custom-call | tf_op jit(solution)/shard_map/pallas_call | solution.py:166
  94.4 15.6 %all_to_all.16.got_ref = bf16[64,16,128]{2,1,0:T(8,128)(2,1)S(1)} all-to-all(bf16[64,16,128]{2,1,0:T(8,128)(2,1)S(1)} %shard_map.376), channel_id=1, replica_groups=mesh['tile'=2,'kern'=4,'noise'=16] {'kern','noise'}, dimensions={0} | all-to-all | bytes 524288 | tf_op jit(solution)/shard_map/all_to_all | solution.py:647
  110.0 0.0 copy-done.5
  110.0 0.0 copy-done.6
  110.0 0.0 copy-done.9
  110.0 0.0 copy-done.10
  110.0 0.0 copy-done.11
  110.1 1.2 %shard_map.377 = f32[32,2048]{1,0:T(8,128)} custom-call(bf16[64,16,128]{2,1,0:T(8,128)(2,1)S(1)} %all_to_all.16.got_ref, f32[32,16]{1,0:T(8,128)S(1)} %copy-done.11, f32[32,128]{1,0:T(8,128)S(1)} %copy-done.10, bf16[128,2048]{1,0:T(8,128)(2,1)S(1)} %copy-done.6, bf16[128,2048]{1,0:T(8,128)(2,1)S(1)} %copy-done.5, f32[1,2048]{1,0:T(1,128)S(1)} %copy-done.9), custom_call_target="tpu_custom_call" | custom-call | tf_op jit(solution)/shard_map/pallas_call | solution.py:166
  (5 shorter events, 0.0 us)
Async XLA Ops:
  41.4 4.6 %copy-start = (bf16[4,512,256]{2,1,0:T(8,128)(2,1)S(1)}, bf16[4,512,256]{2,1,0:T(8,128)(2,1)}, u32[]{:S(2)}) copy-start(bf16[4,512,256]{2,1,0:T(8,128)(2,1)} %constant.87.clone.gl_ref) | copy-start | bytes 3145732
  41.4 4.6 %copy-start.4 = (f32[2,128,128]{2,1,0:T(8,128)S(1)}, f32[2,128,128]{2,1,0:T(8,128)}, u32[]{:S(2)}) copy-start(f32[2,128,128]{2,1,0:T(8,128)} %constant.85.clone.coef_ref.refs_10_) | copy-start | bytes 393220
  41.4 4.6 %copy-start.8 = (bf16[128,256]{1,0:T(8,128)(2,1)S(1)}, bf16[128,256]{1,0:T(8,128)(2,1)}, u32[]{:S(2)}) copy-start(bf16[128,256]{1,0:T(8,128)(2,1)} %constant.88.clone.unfold_ref) | copy-start | bytes 196612
  41.4 33.5 %all-to-all-start.1 = ((bf16[16,32,2048]{2,1,0:T(8,128)(2,1)}), bf16[16,32,2048]{2,1,0:T(8,128)(2,1)}, u32[]{:S(2)}, u32[]{:S(2)}) async-start(bf16[16,32,2048]{2,1,0:T(8,128)(2,1)} %get-tuple-element.44), calls=%async_computation.1 | async-start | bytes 4194304 | tf_op jit(solution)/shard_map/all_to_all | solution.py:538
  46.0 1.2 %copy-start.1 = (bf16[4,512,256]{2,1,0:T(8,128)(2,1)S(1)}, bf16[4,512,256]{2,1,0:T(8,128)(2,1)}, u32[]{:S(2)}) copy-start(bf16[4,512,256]{2,1,0:T(8,128)(2,1)} %constant.86.clone.gh_ref) | copy-start | bytes 3145732
  47.2 12.9 %copy-start.12 = (f32[6]{0:T(128)S(1)}, f32[6]{0:T(128)}, u32[]{:S(2)}) copy-start(f32[6]{0:T(128)} %weight_ref.1) | copy-start | bytes 76
  48.4 10.5 %copy-start.7 = (f32[256,128]{1,0:T(8,128)}, f32[256,128]{1,0:T(8,128)S(1)}, u32[]{:S(2)}) copy-start(f32[256,128]{1,0:T(8,128)S(1)} %shard_map.371.refs_0_) | copy-start | bytes 393220
  48.4 23.7 %copy-start.2 = (bf16[256,2048]{1,0:T(8,128)(2,1)S(1)}, bf16[256,2048]{1,0:T(8,128)(2,1)}, u32[]{:S(2)}) copy-start(bf16[256,2048]{1,0:T(8,128)(2,1)} %constant.95.clone.ol_ref) | copy-start | bytes 3145732
  48.4 23.7 %copy-start.3 = (bf16[256,2048]{1,0:T(8,128)(2,1)S(1)}, bf16[256,2048]{1,0:T(8,128)(2,1)}, u32[]{:S(2)}) copy-start(bf16[256,2048]{1,0:T(8,128)(2,1)} %constant.94.clone.oh_ref) | copy-start | bytes 3145732
  48.4 7.7 %collective-permute-start.2 = (f32[256,128]{1,0:T(8,128)S(1)}, f32[256,128]{1,0:T(8,128)S(1)}, u32[]{:S(2)}, u32[]{:S(2)}) collective-permute-start(f32[256,128]{1,0:T(8,128)S(1)} %shard_map.371.refs_0_), channel_id=1, source_target_pairs={{0,48},{16,32},{32,16},{48,0},{1,49},{17,33},{33,17},{49,1},{2,50}... | collective-permute-start | bytes 393224 | tf_op jit(solution)/shard_map/ppermute | solution.py:491
  51.6 7.2 %collective-permute-start.1 = (f32[256,128]{1,0:T(8,128)S(1)}, f32[256,128]{1,0:T(8,128)S(1)}, u32[]{:S(2)}, u32[]{:S(2)}) collective-permute-start(f32[256,128]{1,0:T(8,128)S(1)} %shard_map.371.refs_0_), channel_id=1, source_target_pairs={{0,32},{16,48},{32,0},{48,16},{1,33},{17,49},{33,1},{49,17},{2,34}... | collective-permute-start | bytes 393224 | tf_op jit(solution)/shard_map/ppermute | solution.py:491
  51.9 6.9 %collective-permute-start = (f32[256,128]{1,0:T(8,128)S(1)}, f32[256,128]{1,0:T(8,128)S(1)}, u32[]{:S(2)}, u32[]{:S(2)}) collective-permute-start(f32[256,128]{1,0:T(8,128)S(1)} %shard_map.371.refs_0_), channel_id=1, source_target_pairs={{0,16},{16,0},{32,48},{48,32},{1,17},{17,1},{33,49},{49,33},{2,18}... | collective-permute-start | bytes 393224 | tf_op jit(solution)/shard_map/ppermute | solution.py:491
  56.1 2.7 %copy-start.13 = (f32[256,128]{1,0:T(8,128)}, f32[256,128]{1,0:T(8,128)S(1)}, u32[]{:S(2)}) copy-start(f32[256,128]{1,0:T(8,128)S(1)} %collective-permute-done.2.refs_3_) | copy-start | bytes 393220
  58.8 0.7 copy-start.14
  59.5 0.6 copy-start.15
  64.5 2.2 %collective-permute-start.3 = (f32[32,256]{1,0:T(8,128)S(1)}, f32[32,256]{1,0:T(8,128)S(1)}, u32[]{:S(2)}, u32[]{:S(2)}) collective-permute-start(f32[32,256]{1,0:T(8,128)S(1)} %get-tuple-element.40), channel_id=1, source_target_pairs={{0,16},{16,0},{32,48},{48,32},{1,17},{17,1},{33,49},{49,33},{2,18}... | collective-permute-start | bytes 98312 | tf_op jit(solution)/shard_map/ppermute | solution.py:491
  64.9 3.2 %collective-permute-start.4 = (f32[32,256]{1,0:T(8,128)S(1)}, f32[32,256]{1,0:T(8,128)S(1)}, u32[]{:S(2)}, u32[]{:S(2)}) collective-permute-start(f32[32,256]{1,0:T(8,128)S(1)} %get-tuple-element.41), channel_id=1, source_target_pairs={{0,32},{16,48},{32,0},{48,16},{1,33},{17,49},{33,1},{49,17},{2,34}... | collective-permute-start | bytes 98312 | tf_op jit(solution)/shard_map/ppermute | solution.py:491
  65.0 4.4 %collective-permute-start.5 = (f32[32,256]{1,0:T(8,128)S(1)}, f32[32,256]{1,0:T(8,128)S(1)}, u32[]{:S(2)}, u32[]{:S(2)}) collective-permute-start(f32[32,256]{1,0:T(8,128)S(1)} %get-tuple-element.42), channel_id=1, source_target_pairs={{0,48},{16,32},{32,16},{48,0},{1,49},{17,33},{33,17},{49,1},{2,50}... | collective-permute-start | bytes 98312 | tf_op jit(solution)/shard_map/ppermute | solution.py:491
  69.4 5.4 %collective-permute-start.6 = (f32[32,256]{1,0:T(8,128)S(1)}, f32[32,256]{1,0:T(8,128)S(1)}, u32[]{:S(2)}, u32[]{:S(2)}) collective-permute-start(f32[32,256]{1,0:T(8,128)S(1)} %add_add_fusion.rows_ref), channel_id=1, source_target_pairs={{0,64},{64,0},{1,65},{65,1},{2,66},{66,2},{3,67},{67,3},{4,68},{68... | collective-permute-start | bytes 98312 | tf_op jit(solution)/shard_map/ppermute | solution.py:582
  77.3 6.6 %collective-permute-start.7 = (f32[32,256]{1,0:T(8,128)S(1)}, f32[32,256]{1,0:T(8,128)S(1)}, u32[]{:S(2)}, u32[]{:S(2)}) collective-permute-start(f32[32,256]{1,0:T(8,128)S(1)} %get-tuple-element.48), channel_id=1, source_target_pairs={{0,64},{64,0},{1,65},{65,1},{2,66},{66,2},{3,67},{67,3},{4,68},{68... | collective-permute-start | bytes 98312 | tf_op jit(solution)/shard_map/ppermute | solution.py:613
  83.9 4.9 %collective-permute-start.10 = (f32[32,256]{1,0:T(8,128)S(1)}, f32[32,256]{1,0:T(8,128)S(1)}, u32[]{:S(2)}, u32[]{:S(2)}) collective-permute-start(f32[32,256]{1,0:T(8,128)S(1)} %add.15.refs_0_), channel_id=1, source_target_pairs={{0,48},{16,32},{32,16},{48,0},{1,49},{17,33},{33,17},{49,1},{2,50}... | collective-permute-start | bytes 98312 | tf_op jit(solution)/shard_map/ppermute | solution.py:491
  87.2 3.2 %collective-permute-start.9 = (f32[32,256]{1,0:T(8,128)S(1)}, f32[32,256]{1,0:T(8,128)S(1)}, u32[]{:S(2)}, u32[]{:S(2)}) collective-permute-start(f32[32,256]{1,0:T(8,128)S(1)} %add.15.refs_0_), channel_id=1, source_target_pairs={{0,32},{16,48},{32,0},{48,16},{1,33},{17,49},{33,1},{49,17},{2,34}... | collective-permute-start | bytes 98312 | tf_op jit(solution)/shard_map/ppermute | solution.py:491
  88.3 2.0 %collective-permute-start.8 = (f32[32,256]{1,0:T(8,128)S(1)}, f32[32,256]{1,0:T(8,128)S(1)}, u32[]{:S(2)}, u32[]{:S(2)}) collective-permute-start(f32[32,256]{1,0:T(8,128)S(1)} %add.15.refs_0_), channel_id=1, source_target_pairs={{0,16},{16,0},{32,48},{48,32},{1,17},{17,1},{33,49},{49,33},{2,18}... | collective-permute-start | bytes 98312 | tf_op jit(solution)/shard_map/ppermute | solution.py:491
  90.4 19.7 %copy-start.5 = (bf16[128,2048]{1,0:T(8,128)(2,1)S(1)}, bf16[128,2048]{1,0:T(8,128)(2,1)}, u32[]{:S(2)}) copy-start(bf16[128,2048]{1,0:T(8,128)(2,1)} %constant.113.clone.wl_ref) | copy-start | bytes 1572868
  90.4 19.7 %copy-start.6 = (bf16[128,2048]{1,0:T(8,128)(2,1)S(1)}, bf16[128,2048]{1,0:T(8,128)(2,1)}, u32[]{:S(2)}) copy-start(bf16[128,2048]{1,0:T(8,128)(2,1)} %constant.112.clone.wh_ref) | copy-start | bytes 1572868
  90.4 19.7 %copy-start.9 = (f32[1,2048]{1,0:T(1,128)S(1)}, f32[1,2048]{1,0:T(1,128)}, u32[]{:S(2)}) copy-start(f32[1,2048]{1,0:T(1,128)} %constant.84.clone.last_ref) | copy-start | bytes 24580
  90.4 19.7 %copy-start.10 = (f32[32,128]{1,0:T(8,128)S(1)}, f32[32,128]{1,0:T(8,128)}, u32[]{:S(2)}) copy-start(f32[32,128]{1,0:T(8,128)} %constant.111.clone.basis_ref) | copy-start | bytes 49156
  90.4 19.7 %copy-start.11 = (f32[32,16]{1,0:T(8,128)S(1)}, f32[32,16]{1,0:T(8,128)}, u32[]{:S(2)}) copy-start(f32[32,16]{1,0:T(8,128)} %constant.110.clone.back_ref) | copy-start | bytes 6148

commit v6 on v5

--- a/solution.py
+++ b/solution.py
@@ -121,11 +121,14 @@
 WAVE = WAVE.reshape(KERN, GROUP_BLOCKS, 2 * REACH, 2 * FREQ).transpose(1, 0, 2, 3)
 WAVE = WAVE.reshape(GROUP_BLOCKS, KERN * 2 * REACH, 2 * FREQ)
 LOW = 4
-HIGH = RANK - LOW
+HIGH = RANK - LOW - 1
 SPREAD = GATHER.reshape(4 * FREQ, BLOCKS, RANK)
-SPREAD = np.concatenate([SPREAD[:, :, : HIGH - 1], SPREAD[:, :, RANK - 1 :], SPREAD[:, :, :LOW]], 2)
+SPARE = SPREAD[:, :, RANK - 1 :]
+SPREAD = np.concatenate([SPREAD[:, :, : HIGH - 1], SPARE, SPREAD[:, :, :LOW], SPARE], 2)
 SPREAD = SPREAD.reshape(4 * FREQ, BLOCKS * RANK).T
-BASIS_BACK = np.concatenate([BASIS[:, : HIGH - 1], np.zeros((ROWS, 1)), BASIS[:, :LOW]], 1)
+BASIS_BACK = np.zeros((ROWS, RANK))
+BASIS_BACK[:, : HIGH - 1] = BASIS[:, : HIGH - 1]
+BASIS_BACK[:, HIGH : HIGH + LOW] = BASIS[:, :LOW]
 GATHER_OWN = GATHER.reshape(4 * FREQ, KERN, GROUP_BLOCKS * RANK).transpose(1, 0, 2)
 BLUR = np.zeros((GROUP_BLOCKS, KERN, ROWS, KERN, REACH))
 for group in range(KERN):
@@ -176,7 +179,7 @@
     return tuple(pltpu.with_memory_space_constraint(value, pltpu.VMEM) for value in values)
 
 
-CHUNK = 1024
+CHUNK = 512
 LANES = 256
 PARTS = 4
 
@@ -320,7 +323,7 @@
 
 def dose_first_body(rows_ref, oh_ref, ol_ref, noise_ref, sums_ref):
     sums_ref[0] = dot3(split(rows_ref[...]), (oh_ref[...], ol_ref[...]))
-    for place in places(CHUNK):
+    for place in places(PERIOD):
         acid = sums_ref[(0,) + place]
         zero = jnp.zeros(acid.shape, F32)
         for index, value in enumerate(sample_sums(noise_ref, place, acid, (zero, zero, zero))):
@@ -374,50 +377,50 @@
 
 
 def dose_body(place_ref, sums_ref, edge_ref, target_ref, noise_ref, oh_ref, ol_ref, *refs):
-    step = pl.program_id(0)
-    last = pl.num_programs(0) - 1
-    ins, out_ref, outs, sems = refs[:11], refs[11], refs[12:20], refs[20]
+    ins, out_ref, outs, (target, noise, own, sems) = refs[:11], refs[11], refs[12:20], refs[20:]
     field_ref, kern_ref, wh_ref, wl_ref, gh_ref, gl_ref, blur_ref, th_ref, tl_ref, fold_ref, coef_ref = ins
     field, kern, wave, grid, blur, table, fold, coef = outs
     block = place_ref[1]
-    copies = [
-        pltpu.make_async_copy(source, held, sems.at[index])
-        for index, (source, held) in enumerate(
-            zip(
-                [field_ref, kern_ref, wh_ref.at[block], wl_ref.at[block], gh_ref, gl_ref]
-                + [blur_ref.at[block], th_ref, tl_ref, fold_ref, coef_ref],
-                [field, kern, wave.at[0], wave.at[1], grid.at[0], grid.at[1]]
-                + [blur, table.at[0], table.at[1], fold, coef],
-            )
-        )
-    ]
-
-    @pl.when(step == 0)
-    def _():
-        for copy in copies:
-            copy.start()
-
-    total = jnp.where(step == 0, 0.0, out_ref[...])
-    for col in range(0, CHUNK, LANES):
-        lanes = slice(col, col + LANES)
-        grads = []
-        for row in range(0, ROWS, 16):
-            place = (slice(row, row + 16), lanes)
-            acid, *sums = [sums_ref[(index,) + place] for index in range(4)]
-            grads.append(acid_grad(sample_sums(noise_ref, place, acid, sums), target_ref[place]))
-        grad = jnp.concatenate(grads, 0)
-        if col == 0:
-            grad = jnp.concatenate([jnp.where(step == 0, edge_ref[:, :EDGE], grad[:, :EDGE]), grad[:, EDGE:]], 1)
-        if col == CHUNK - LANES:
-            here = jnp.where(step == last, edge_ref[:, EDGE:], grad[:, LANES - EDGE :])
-            grad = jnp.concatenate([grad[:, : LANES - EDGE], here], 1)
-        total = total + dot3(split(grad), (oh_ref[lanes], ol_ref[lanes]))
+    chunks = [pl.ds(first, CHUNK) for first in range(0, PERIOD, CHUNK)]
+    copies = fetches(
+        [target_ref]
+        + [ref for part in chunks for ref in (noise_ref.at[:, :, part], oh_ref.at[part], ol_ref.at[part])]
+        + [field_ref, kern_ref, wh_ref.at[block], wl_ref.at[block], gh_ref, gl_ref]
+        + [blur_ref.at[block], th_ref, tl_ref, fold_ref, coef_ref],
+        [target]
+        + [
+            ref
+            for index, part in enumerate(chunks)
+            for ref in (noise.at[index], own.at[0, part], own.at[1, part])
+        ]
+        + [field, kern, wave.at[0], wave.at[1], grid.at[0], grid.at[1]]
+        + [blur, table.at[0], table.at[1], fold, coef],
+        sems,
+    )
+    copies[0].wait()
+    total = None
+    for index in range(len(chunks)):
+        for copy in copies[1 + 3 * index : 4 + 3 * index]:
+            copy.wait()
+        for col in range(0, CHUNK, LANES):
+            first = index * CHUNK + col
+            grads = []
+            for row in range(0, ROWS, 16):
+                place = (slice(row, row + 16), slice(first, first + LANES))
+                acid, *sums = [sums_ref[(which,) + place] for which in range(4)]
+                here = (slice(row, row + 16), slice(col, col + LANES))
+                grads.append(acid_grad(sample_sums(noise.at[index], here, acid, sums), target[place]))
+            grad = jnp.concatenate(grads, 0)
+            if first == 0:
+                grad = jnp.concatenate([edge_ref[:, :EDGE], grad[:, EDGE:]], 1)
+            if first == PERIOD - LANES:
+                grad = jnp.concatenate([grad[:, : LANES - EDGE], edge_ref[:, EDGE:]], 1)
+            lines = slice(first, first + LANES)
+            part = dot3(split(grad), (own[0, lines], own[1, lines]))
+            total = part if total is None else total + part
     out_ref[...] = total
-
-    @pl.when(step == last)
-    def _():
-        for copy in copies:
-            copy.wait()
+    for copy in copies[1 + 3 * len(chunks) :]:
+        copy.wait()
 
 
 def back_body(place_ref, weight_ref, *refs):
@@ -473,7 +476,7 @@
     for index in range(1, got_ref.shape[0]):
         total = total + got_ref[index].astype(F32)
     rows = dot3(split(back_ref[...]), split(total))
-    spare = jnp.sum(basis_ref[...] * total[HIGH - 1 : HIGH], 1, keepdims=True)
+    spare = jnp.sum(basis_ref[...] * (total[HIGH - 1 : HIGH] + total[RANK - 1 :]), 1, keepdims=True)
     out_ref[...] = dot3(split(rows), (wh_ref[...], wl_ref[...])) + spare * last_ref[...]
 
 
@@ -580,15 +583,13 @@
     rows = (pieces[0] + pieces[1]) + (pieces[2] + pieces[3])
     swap = [(0, 1), (1, 0)]
     rows_other = lax.ppermute(rows, "tile", swap)
-    got_spec = pl.BlockSpec((noise_count, ROWS, CHUNK), lambda i: (0, 0, i))
-    sums_spec = pl.BlockSpec((4, ROWS, CHUNK), lambda i: (0, 0, i))
     sums = call(
         dose_first_body,
         f32(4, ROWS, PERIOD),
         (rows, *near_const(OWN.T), got),
-        grid=(columns,),
-        in_specs=[fixed(ROWS, COARSE)] + [chunk(COARSE)] * 2 + [got_spec],
-        out_specs=sums_spec,
+        grid=(1,),
+        in_specs=[fixed(ROWS, COARSE)] + [fixed(COARSE, PERIOD)] * 2 + [fixed(noise_count, ROWS, PERIOD)],
+        out_specs=pl.BlockSpec((4, ROWS, PERIOD), lambda i: (0, 0, 0)),
     )
     (target,) = hbm(target)
     (sums,) = vmem(sums)
@@ -627,12 +628,15 @@
         dose_body,
         (f32(ROWS, COARSE),) + tuple(pltpu.VMEM(shape, dtype) for shape, dtype in held),
         (place, sums, edges, target, got_last, *to_const(OWN), *hbm(*ins)),
-        grid=(columns,),
-        in_specs=[smem, sums_spec, fixed(ROWS, 2 * EDGE), chunk(ROWS), got_spec]
-        + [pl.BlockSpec((CHUNK, COARSE), lambda i: (i, 0))] * 2
-        + [anywhere] * len(ins),
-        out_specs=(fixed(ROWS, COARSE),) + (inside,) * len(held),
-        scratch_shapes=[pltpu.SemaphoreType.DMA((len(ins),))],
+        in_specs=[smem, inside, piece_spec, anywhere, pl.BlockSpec(memory_space=pl.ANY)]
+        + [anywhere] * (2 + len(ins)),
+        out_specs=(piece_spec,) + (inside,) * len(held),
+        scratch_shapes=[
+            pltpu.VMEM((ROWS, PERIOD), BF),
+            pltpu.VMEM((columns, noise_count, ROWS, CHUNK), BF),
+            pltpu.VMEM((2,) + OWN.shape, BF),
+            pltpu.SemaphoreType.DMA((1 + 3 * columns + len(ins),)),
+        ],
     )
     grad = grad_own + grad_other
     grads = [grad] + shifted([grad] * len(shifts), shifts)

time: 112 us -> 111 us (level)
  transfers between devices with their start and end apart: 12 -> 12, of which waited for: 6 -> 6; matrix products, arithmetic and copies ran while one was open for 0% -> 0% of each run, Pallas kernels for 12% -> 11%
where the time goes in v6:
time: 111 us
  blocking collectives  52.9 us (48%)
  Pallas kernels  23.7 us (21%)
  starting transfers between devices  20.1 us (18%)
  waiting for transfers between devices  11.4 us (10%)
  local copies, waits for them, and re-layouts  2.56 us (2%)
    all_to_all x1, blocking collectives, body(): got = lax.all_to_all(moved_first, 'noise', 0, 0, tiled=True)  37.4 us
    pallas_call x7, Pallas kernels, call(): pl.pallas_call(body, out_shape=out_shape, compiler_params=params, **kw)  22.6 us
    all_to_all x1, blocking collectives, body(): back = lax.all_to_all(spread, ('kern', 'noise'), 0, 0, tiled=True)  15.6 us
    ppermute x9, waiting for transfers between devices, shifted(): lax.ppermute(value, 'kern', [(source, source ^ shift) for source in range...  11.4 us
    ppermute x9, starting transfers between devices, shifted(): lax.ppermute(value, 'kern', [(source, source ^ shift) for source in range...  10.4 us
    all_to_all x1, starting transfers between devices, body(): got_last = lax.all_to_all(moved, 'noise', 0, 0, tiled=True)  4.57 us
    ppermute x1, starting transfers between devices, body(): rows_other = lax.ppermute(rows, 'tile', swap)  2.62 us
    ppermute x1, starting transfers between devices, body(): grad_other = lax.ppermute(send, 'tile', swap)  2.57 us
  transfers between devices with their start and end apart: 12, of which 6 were waited for; matrix products, arithmetic and copies ran while one was open for 0% of the time, Pallas kernels for 11%

profile of v6, /device:TPU:1, one launch (start us, length us, event | category | flops | bytes accessed | tf_op | source)
XLA Modules:
  0.0 111.1 jit_solution(11025921081589699765)
XLA Ops:
  0.0 0.1 pad_add_fusion._.place_ref
  0.1 4.0 %shard_map.370 = (bf16[16,32,2176]{2,1,0:T(8,128)(2,1)}, bf16[16,32,2048]{2,1,0:T(8,128)(2,1)}) custom-call(f32[32,2048]{1,0:T(8,128)} %mask_ref.1, f32[16,32]{1,0:T(8,128)} %constant.83.clone.basis_ref, bf16[2048,128]{1,0:T(8,128)(2,1)} %constant.81.clone.lh_ref, bf16[2048,128]{1,0:T(8,128)(2,1)} %constant.82.clone.ll_ref, ...), custom_call_target="tpu_custom_call" | custom-call | tf_op jit(solution)/shard_map/pallas_call | solution.py:169
  4.0 37.4 %all_to_all.15.got_ref.noise_ref.refs_1_ = bf16[16,32,2176]{2,1,0:T(8,128)(2,1)S(1)} all-to-all(bf16[16,32,2176]{2,1,0:T(8,128)(2,1)} %get-tuple-element.32), channel_id=1, replica_groups=mesh['tile'=2,'kern'=4,'noise'=16] {'noise'}, dimensions={0} | all-to-all | bytes 4456448 | tf_op jit(solution)/shard_map/all_to_all | solution.py:537
  41.4 0.0 copy-start
  41.4 0.0 copy-start.4
  41.4 0.0 copy-start.8
  41.4 4.6 %all-to-all-start.1 = ((bf16[16,32,2048]{2,1,0:T(8,128)(2,1)}), bf16[16,32,2048]{2,1,0:T(8,128)(2,1)}, u32[]{:S(2)}, u32[]{:S(2)}) async-start(bf16[16,32,2048]{2,1,0:T(8,128)(2,1)} %get-tuple-element.44), calls=%async_computation.1 | async-start | bytes 4194304 | tf_op jit(solution)/shard_map/all_to_all | solution.py:541
  46.0 0.0 copy-done
  46.0 0.0 copy-done.4
  46.0 0.0 copy-done.8
  46.0 0.0 copy-start.1
  46.0 1.2 %copy-done.1 = bf16[4,512,256]{2,1,0:T(8,128)(2,1)S(1)} copy-done((bf16[4,512,256]{2,1,0:T(8,128)(2,1)S(1)}, bf16[4,512,256]{2,1,0:T(8,128)(2,1)}, u32[]{:S(2)}) %copy-start.1) | copy-done | bytes 1048600
  47.2 0.0 copy-start.12
  47.2 1.1 %shard_map.371.refs_0_ = f32[256,128]{1,0:T(8,128)S(1)} custom-call(s32[3]{0:T(128)S(1)} %pad_add_fusion._.place_ref, bf16[16,32,2176]{2,1,0:T(8,128)(2,1)S(1)} %all_to_all.15.got_ref.noise_ref.refs_1_, bf16[4,512,256]{2,1,0:T(8,128)(2,1)S(1)} %copy-done.1, bf16[4,512,256]{2,1,0:T(8,128)(2,1)S(1)} %copy-done, bf16[128,256]{1,0:T(8,128)(2,1)S(1)} %copy-done.8, ...), custom_call_target="tpu_custom_call" | custom-call | tf_op jit(solution)/shard_map/pallas_call | solution.py:171
  48.4 0.0 copy-start.7
  48.4 0.0 copy-start.2
  48.4 0.0 copy-start.3
  48.4 3.3 %collective-permute-start.2 = (f32[256,128]{1,0:T(8,128)S(1)}, f32[256,128]{1,0:T(8,128)S(1)}, u32[]{:S(2)}, u32[]{:S(2)}) collective-permute-start(f32[256,128]{1,0:T(8,128)S(1)} %shard_map.371.refs_0_), channel_id=1, source_target_pairs={{0,48},{16,32},{32,16},{48,0},{1,49},{17,33},{33,17},{49,1},{2,50}... | collective-permute-start | bytes 393224 | tf_op jit(solution)/shard_map/ppermute | solution.py:494
  51.7 0.3 collective-permute-start.1
  51.9 0.2 collective-permute-start
  52.1 4.0 %collective-permute-done.2.refs_3_ = f32[256,128]{1,0:T(8,128)S(1)} collective-permute-done((f32[256,128]{1,0:T(8,128)S(1)}, f32[256,128]{1,0:T(8,128)S(1)}, u32[]{:S(2)}, u32[]{:S(2)}) %collective-permute-start.2) | collective-permute-done | bytes 131104 | tf_op jit(solution)/shard_map/ppermute | solution.py:494
  56.1 0.0 copy-start.13
  56.1 2.7 %collective-permute-done.1.refs_2_ = f32[256,128]{1,0:T(8,128)S(1)} collective-permute-done((f32[256,128]{1,0:T(8,128)S(1)}, f32[256,128]{1,0:T(8,128)S(1)}, u32[]{:S(2)}, u32[]{:S(2)}) %collective-permute-start.1) | collective-permute-done | bytes 131104 | tf_op jit(solution)/shard_map/ppermute | solution.py:494
  58.8 0.0 copy-start.14
  58.8 0.0 collective-permute-done.refs_1_
  58.8 0.0 copy-done.7
  58.8 0.0 copy-done.13
  58.8 0.6 copy-done.14
  59.5 0.0 copy-start.15
  59.5 0.6 copy-done.15
  60.1 0.0 copy-done.12
  60.1 4.4 %shard_map.372 = (f32[576,512]{1,0:T(8,128)}, f32[32,256]{1,0:T(8,128)S(1)}, f32[32,256]{1,0:T(8,128)S(1)}, f32[32,256]{1,0:T(8,128)S(1)}, f32[32,256]{1,0:T(8,128)S(1)}) custom-call(s32[3]{0:T(128)S(1)} %pad_add_fusion._.place_ref, f32[6]{0:T(128)S(1)} %copy-done.12, f32[256,128]{1,0:T(8,128)} %copy-done.7, f32[256,128]{1,0:T(8,128)} %copy-done.15, ...), custom_call_target="tpu_custom_call" | custom-call | tf_op jit(solution)/shard_map/pallas_call | solution.py:169
  64.5 0.4 collective-permute-start.3
  64.9 0.1 collective-permute-start.4
  65.0 1.7 %collective-permute-start.5 = (f32[32,256]{1,0:T(8,128)S(1)}, f32[32,256]{1,0:T(8,128)S(1)}, u32[]{:S(2)}, u32[]{:S(2)}) collective-permute-start(f32[32,256]{1,0:T(8,128)S(1)} %get-tuple-element.42), channel_id=1, source_target_pairs={{0,48},{16,32},{32,16},{48,0},{1,49},{17,33},{33,17},{49,1},{2,50}... | collective-permute-start | bytes 98312 | tf_op jit(solution)/shard_map/ppermute | solution.py:494
  66.7 0.0 collective-permute-done.3
  66.7 1.4 %collective-permute-done.4 = f32[32,256]{1,0:T(8,128)S(1)} collective-permute-done((f32[32,256]{1,0:T(8,128)S(1)}, f32[32,256]{1,0:T(8,128)S(1)}, u32[]{:S(2)}, u32[]{:S(2)}) %collective-permute-start.4) | collective-permute-done | bytes 32800 | tf_op jit(solution)/shard_map/ppermute | solution.py:494
  68.1 1.3 %collective-permute-done.5 = f32[32,256]{1,0:T(8,128)S(1)} collective-permute-done((f32[32,256]{1,0:T(8,128)S(1)}, f32[32,256]{1,0:T(8,128)S(1)}, u32[]{:S(2)}, u32[]{:S(2)}) %collective-permute-start.5) | collective-permute-done | bytes 32800 | tf_op jit(solution)/shard_map/ppermute | solution.py:494
  69.4 2.6 %collective-permute-start.6 = (f32[32,256]{1,0:T(8,128)S(1)}, f32[32,256]{1,0:T(8,128)S(1)}, u32[]{:S(2)}, u32[]{:S(2)}) collective-permute-start(f32[32,256]{1,0:T(8,128)S(1)} %add_add_fusion.rows_ref), channel_id=1, source_target_pairs={{0,64},{64,0},{1,65},{65,1},{2,66},{66,2},{3,67},{67,3},{4,68},{68... | collective-permute-start | bytes 98312 | tf_op jit(solution)/shard_map/ppermute | solution.py:585
  72.1 0.0 copy-done.2
  72.1 0.0 copy-done.3
  72.1 2.1 %shard_map.373.sums_ref = f32[4,32,2048]{2,1,0:T(8,128)S(1)} custom-call(f32[32,256]{1,0:T(8,128)S(1)} %add_add_fusion.rows_ref, bf16[256,2048]{1,0:T(8,128)(2,1)S(1)} %copy-done.3, bf16[256,2048]{1,0:T(8,128)(2,1)S(1)} %copy-done.2, bf16[16,32,2176]{2,1,0:T(8,128)(2,1)S(1)} %all_to_all.15.got_ref.noise_ref.refs_1_), custom_call_target="tpu_custom_call" | custom-call | tf_op jit(solution)/shard_map/pallas_call | solution.py:169
  74.2 0.0 collective-permute-done.6.other_ref
  74.2 0.0 all-to-all-done.1.refs_2_.noise_ref
  74.2 2.5 %shard_map.374 = (f32[32,256]{1,0:T(8,128)S(1)}, f32[32,256]{1,0:T(8,128)S(1)}) custom-call(s32[3]{0:T(128)S(1)} %pad_add_fusion._.place_ref, f32[4,32,2048]{2,1,0:T(8,128)S(1)} %shard_map.373.sums_ref, f32[32,256]{1,0:T(8,128)S(1)} %collective-permute-done.6.other_ref, bf16[32,2048]{1,0:T(8,128)(2,1)} %target_ref, ...), custom_call_target="tpu_custom_call" | custom-call | tf_op jit(solution)/shard_map/pallas_call | solution.py:169
  76.7 2.6 %collective-permute-start.7 = (f32[32,256]{1,0:T(8,128)S(1)}, f32[32,256]{1,0:T(8,128)S(1)}, u32[]{:S(2)}, u32[]{:S(2)}) collective-permute-start(f32[32,256]{1,0:T(8,128)S(1)} %get-tuple-element.48), channel_id=1, source_target_pairs={{0,64},{64,0},{1,65},{65,1},{2,66},{66,2},{3,67},{67,3},{4,68},{68... | collective-permute-start | bytes 98312 | tf_op jit(solution)/shard_map/ppermute | solution.py:614
  79.3 4.4 %shard_map.375 = (f32[32,256]{1,0:T(8,128)S(1)}, f32[576,512]{1,0:T(8,128)S(1)}, f32[6,2,128,128]{3,2,1,0:T(8,128)S(1)}, bf16[2,256,192]{2,1,0:T(8,128)(2,1)S(1)...) custom-call(s32[3]{0:T(128)S(1)} %pad_add_fusion._.place_ref, ...), custom_call_target="tpu_custom_call" | custom-call | tf_op jit(solution)/shard_map/pallas_call | solution.py:169
  83.7 0.0 collective-permute-done.7
  83.7 3.3 %collective-permute-start.10 = (f32[32,256]{1,0:T(8,128)S(1)}, f32[32,256]{1,0:T(8,128)S(1)}, u32[]{:S(2)}, u32[]{:S(2)}) collective-permute-start(f32[32,256]{1,0:T(8,128)S(1)} %add.15.refs_0_), channel_id=1, source_target_pairs={{0,48},{16,32},{32,16},{48,0},{1,49},{17,33},{33,17},{49,1},{2,50}... | collective-permute-start | bytes 98312 | tf_op jit(solution)/shard_map/ppermute | solution.py:494
  87.0 1.2 %collective-permute-start.9 = (f32[32,256]{1,0:T(8,128)S(1)}, f32[32,256]{1,0:T(8,128)S(1)}, u32[]{:S(2)}, u32[]{:S(2)}) collective-permute-start(f32[32,256]{1,0:T(8,128)S(1)} %add.15.refs_0_), channel_id=1, source_target_pairs={{0,32},{16,48},{32,0},{48,16},{1,33},{17,49},{33,1},{49,17},{2,34}... | collective-permute-start | bytes 98312 | tf_op jit(solution)/shard_map/ppermute | solution.py:494
  88.2 0.0 collective-permute-start.8
  88.2 0.4 collective-permute-done.10.refs_3_
  88.6 1.6 %collective-permute-done.9.refs_2_ = f32[32,256]{1,0:T(8,128)S(1)} collective-permute-done((f32[32,256]{1,0:T(8,128)S(1)}, f32[32,256]{1,0:T(8,128)S(1)}, u32[]{:S(2)}, u32[]{:S(2)}) %collective-permute-start.9) | collective-permute-done | bytes 32800 | tf_op jit(solution)/shard_map/ppermute | solution.py:494
  90.2 0.0 collective-permute-done.8.refs_1_
  90.2 0.0 copy-start.10
  90.2 0.0 copy-start.11
  90.2 4.0 %shard_map.376 = bf16[64,16,128]{2,1,0:T(8,128)(2,1)S(1)} custom-call(s32[3]{0:T(128)S(1)} %pad_add_fusion._.place_ref, f32[6]{0:T(128)S(1)} %copy-done.12, f32[32,256]{1,0:T(8,128)S(1)} %add.15.refs_0_, f32[32,256]{1,0:T(8,128)S(1)} %collective-permute-done.8.refs_1_, f32[32,256]{1,0:T(8,128)S(1)} %collective-permute-done.9.refs_2_, ...), custom_call_target="tpu_custom_call" | custom-call | tf_op jit(solution)/shard_map/pallas_call | solution.py:169
  94.3 15.6 %all_to_all.16.got_ref = bf16[64,16,128]{2,1,0:T(8,128)(2,1)S(1)} all-to-all(bf16[64,16,128]{2,1,0:T(8,128)(2,1)S(1)} %shard_map.376), channel_id=1, replica_groups=mesh['tile'=2,'kern'=4,'noise'=16] {'kern','noise'}, dimensions={0} | all-to-all | bytes 524288 | tf_op jit(solution)/shard_map/all_to_all | solution.py:651
  109.9 0.0 copy-done.5
  109.9 0.0 copy-done.6
  109.9 0.0 copy-done.9
  109.9 0.0 copy-done.10
  109.9 0.0 copy-done.11
  109.9 1.2 %shard_map.377 = f32[32,2048]{1,0:T(8,128)} custom-call(bf16[64,16,128]{2,1,0:T(8,128)(2,1)S(1)} %all_to_all.16.got_ref, f32[32,16]{1,0:T(8,128)S(1)} %copy-done.11, f32[32,128]{1,0:T(8,128)S(1)} %copy-done.10, bf16[128,2048]{1,0:T(8,128)(2,1)S(1)} %copy-done.6, bf16[128,2048]{1,0:T(8,128)(2,1)S(1)} %copy-done.5, f32[1,2048]{1,0:T(1,128)S(1)} %copy-done.9), custom_call_target="tpu_custom_call" | custom-call | tf_op jit(solution)/shard_map/pallas_call | solution.py:169
  (5 shorter events, 0.0 us)
Async XLA Ops:
  41.4 4.6 %copy-start = (bf16[4,512,256]{2,1,0:T(8,128)(2,1)S(1)}, bf16[4,512,256]{2,1,0:T(8,128)(2,1)}, u32[]{:S(2)}) copy-start(bf16[4,512,256]{2,1,0:T(8,128)(2,1)} %constant.87.clone.gl_ref) | copy-start | bytes 3145732
  41.4 4.6 %copy-start.4 = (f32[2,128,128]{2,1,0:T(8,128)S(1)}, f32[2,128,128]{2,1,0:T(8,128)}, u32[]{:S(2)}) copy-start(f32[2,128,128]{2,1,0:T(8,128)} %constant.85.clone.coef_ref.refs_10_) | copy-start | bytes 393220
  41.4 4.6 %copy-start.8 = (bf16[128,256]{1,0:T(8,128)(2,1)S(1)}, bf16[128,256]{1,0:T(8,128)(2,1)}, u32[]{:S(2)}) copy-start(bf16[128,256]{1,0:T(8,128)(2,1)} %constant.88.clone.unfold_ref) | copy-start | bytes 196612
  41.4 32.8 %all-to-all-start.1 = ((bf16[16,32,2048]{2,1,0:T(8,128)(2,1)}), bf16[16,32,2048]{2,1,0:T(8,128)(2,1)}, u32[]{:S(2)}, u32[]{:S(2)}) async-start(bf16[16,32,2048]{2,1,0:T(8,128)(2,1)} %get-tuple-element.44), calls=%async_computation.1 | async-start | bytes 4194304 | tf_op jit(solution)/shard_map/all_to_all | solution.py:541
  46.0 1.2 %copy-start.1 = (bf16[4,512,256]{2,1,0:T(8,128)(2,1)S(1)}, bf16[4,512,256]{2,1,0:T(8,128)(2,1)}, u32[]{:S(2)}) copy-start(bf16[4,512,256]{2,1,0:T(8,128)(2,1)} %constant.86.clone.gh_ref) | copy-start | bytes 3145732
  47.2 12.9 %copy-start.12 = (f32[6]{0:T(128)S(1)}, f32[6]{0:T(128)}, u32[]{:S(2)}) copy-start(f32[6]{0:T(128)} %weight_ref.1) | copy-start | bytes 76
  48.4 10.5 %copy-start.7 = (f32[256,128]{1,0:T(8,128)}, f32[256,128]{1,0:T(8,128)S(1)}, u32[]{:S(2)}) copy-start(f32[256,128]{1,0:T(8,128)S(1)} %shard_map.371.refs_0_) | copy-start | bytes 393220
  48.4 23.7 %copy-start.2 = (bf16[256,2048]{1,0:T(8,128)(2,1)S(1)}, bf16[256,2048]{1,0:T(8,128)(2,1)}, u32[]{:S(2)}) copy-start(bf16[256,2048]{1,0:T(8,128)(2,1)} %constant.95.clone.ol_ref) | copy-start | bytes 3145732
  48.4 23.7 %copy-start.3 = (bf16[256,2048]{1,0:T(8,128)(2,1)S(1)}, bf16[256,2048]{1,0:T(8,128)(2,1)}, u32[]{:S(2)}) copy-start(bf16[256,2048]{1,0:T(8,128)(2,1)} %constant.94.clone.oh_ref) | copy-start | bytes 3145732
  48.4 7.7 %collective-permute-start.2 = (f32[256,128]{1,0:T(8,128)S(1)}, f32[256,128]{1,0:T(8,128)S(1)}, u32[]{:S(2)}, u32[]{:S(2)}) collective-permute-start(f32[256,128]{1,0:T(8,128)S(1)} %shard_map.371.refs_0_), channel_id=1, source_target_pairs={{0,48},{16,32},{32,16},{48,0},{1,49},{17,33},{33,17},{49,1},{2,50}... | collective-permute-start | bytes 393224 | tf_op jit(solution)/shard_map/ppermute | solution.py:494
  51.7 7.2 %collective-permute-start.1 = (f32[256,128]{1,0:T(8,128)S(1)}, f32[256,128]{1,0:T(8,128)S(1)}, u32[]{:S(2)}, u32[]{:S(2)}) collective-permute-start(f32[256,128]{1,0:T(8,128)S(1)} %shard_map.371.refs_0_), channel_id=1, source_target_pairs={{0,32},{16,48},{32,0},{48,16},{1,33},{17,49},{33,1},{49,17},{2,34}... | collective-permute-start | bytes 393224 | tf_op jit(solution)/shard_map/ppermute | solution.py:494
  51.9 6.9 %collective-permute-start = (f32[256,128]{1,0:T(8,128)S(1)}, f32[256,128]{1,0:T(8,128)S(1)}, u32[]{:S(2)}, u32[]{:S(2)}) collective-permute-start(f32[256,128]{1,0:T(8,128)S(1)} %shard_map.371.refs_0_), channel_id=1, source_target_pairs={{0,16},{16,0},{32,48},{48,32},{1,17},{17,1},{33,49},{49,33},{2,18}... | collective-permute-start | bytes 393224 | tf_op jit(solution)/shard_map/ppermute | solution.py:494
  56.1 2.7 %copy-start.13 = (f32[256,128]{1,0:T(8,128)}, f32[256,128]{1,0:T(8,128)S(1)}, u32[]{:S(2)}) copy-start(f32[256,128]{1,0:T(8,128)S(1)} %collective-permute-done.2.refs_3_) | copy-start | bytes 393220
  58.8 0.7 copy-start.14
  59.5 0.6 copy-start.15
  64.5 2.2 %collective-permute-start.3 = (f32[32,256]{1,0:T(8,128)S(1)}, f32[32,256]{1,0:T(8,128)S(1)}, u32[]{:S(2)}, u32[]{:S(2)}) collective-permute-start(f32[32,256]{1,0:T(8,128)S(1)} %get-tuple-element.40), channel_id=1, source_target_pairs={{0,16},{16,0},{32,48},{48,32},{1,17},{17,1},{33,49},{49,33},{2,18}... | collective-permute-start | bytes 98312 | tf_op jit(solution)/shard_map/ppermute | solution.py:494
  64.9 3.2 %collective-permute-start.4 = (f32[32,256]{1,0:T(8,128)S(1)}, f32[32,256]{1,0:T(8,128)S(1)}, u32[]{:S(2)}, u32[]{:S(2)}) collective-permute-start(f32[32,256]{1,0:T(8,128)S(1)} %get-tuple-element.41), channel_id=1, source_target_pairs={{0,32},{16,48},{32,0},{48,16},{1,33},{17,49},{33,1},{49,17},{2,34}... | collective-permute-start | bytes 98312 | tf_op jit(solution)/shard_map/ppermute | solution.py:494
  65.0 4.4 %collective-permute-start.5 = (f32[32,256]{1,0:T(8,128)S(1)}, f32[32,256]{1,0:T(8,128)S(1)}, u32[]{:S(2)}, u32[]{:S(2)}) collective-permute-start(f32[32,256]{1,0:T(8,128)S(1)} %get-tuple-element.42), channel_id=1, source_target_pairs={{0,48},{16,32},{32,16},{48,0},{1,49},{17,33},{33,17},{49,1},{2,50}... | collective-permute-start | bytes 98312 | tf_op jit(solution)/shard_map/ppermute | solution.py:494
  69.4 4.8 %collective-permute-start.6 = (f32[32,256]{1,0:T(8,128)S(1)}, f32[32,256]{1,0:T(8,128)S(1)}, u32[]{:S(2)}, u32[]{:S(2)}) collective-permute-start(f32[32,256]{1,0:T(8,128)S(1)} %add_add_fusion.rows_ref), channel_id=1, source_target_pairs={{0,64},{64,0},{1,65},{65,1},{2,66},{66,2},{3,67},{67,3},{4,68},{68... | collective-permute-start | bytes 98312 | tf_op jit(solution)/shard_map/ppermute | solution.py:585
  76.7 7.0 %collective-permute-start.7 = (f32[32,256]{1,0:T(8,128)S(1)}, f32[32,256]{1,0:T(8,128)S(1)}, u32[]{:S(2)}, u32[]{:S(2)}) collective-permute-start(f32[32,256]{1,0:T(8,128)S(1)} %get-tuple-element.48), channel_id=1, source_target_pairs={{0,64},{64,0},{1,65},{65,1},{2,66},{66,2},{3,67},{67,3},{4,68},{68... | collective-permute-start | bytes 98312 | tf_op jit(solution)/shard_map/ppermute | solution.py:614
  83.7 4.9 %collective-permute-start.10 = (f32[32,256]{1,0:T(8,128)S(1)}, f32[32,256]{1,0:T(8,128)S(1)}, u32[]{:S(2)}, u32[]{:S(2)}) collective-permute-start(f32[32,256]{1,0:T(8,128)S(1)} %add.15.refs_0_), channel_id=1, source_target_pairs={{0,48},{16,32},{32,16},{48,0},{1,49},{17,33},{33,17},{49,1},{2,50}... | collective-permute-start | bytes 98312 | tf_op jit(solution)/shard_map/ppermute | solution.py:494
  87.0 3.2 %collective-permute-start.9 = (f32[32,256]{1,0:T(8,128)S(1)}, f32[32,256]{1,0:T(8,128)S(1)}, u32[]{:S(2)}, u32[]{:S(2)}) collective-permute-start(f32[32,256]{1,0:T(8,128)S(1)} %add.15.refs_0_), channel_id=1, source_target_pairs={{0,32},{16,48},{32,0},{48,16},{1,33},{17,49},{33,1},{49,17},{2,34}... | collective-permute-start | bytes 98312 | tf_op jit(solution)/shard_map/ppermute | solution.py:494
  88.2 2.0 %collective-permute-start.8 = (f32[32,256]{1,0:T(8,128)S(1)}, f32[32,256]{1,0:T(8,128)S(1)}, u32[]{:S(2)}, u32[]{:S(2)}) collective-permute-start(f32[32,256]{1,0:T(8,128)S(1)} %add.15.refs_0_), channel_id=1, source_target_pairs={{0,16},{16,0},{32,48},{48,32},{1,17},{17,1},{33,49},{49,33},{2,18}... | collective-permute-start | bytes 98312 | tf_op jit(solution)/shard_map/ppermute | solution.py:494
  90.2 19.7 %copy-start.5 = (bf16[128,2048]{1,0:T(8,128)(2,1)S(1)}, bf16[128,2048]{1,0:T(8,128)(2,1)}, u32[]{:S(2)}) copy-start(bf16[128,2048]{1,0:T(8,128)(2,1)} %constant.113.clone.wl_ref) | copy-start | bytes 1572868
  90.2 19.7 %copy-start.6 = (bf16[128,2048]{1,0:T(8,128)(2,1)S(1)}, bf16[128,2048]{1,0:T(8,128)(2,1)}, u32[]{:S(2)}) copy-start(bf16[128,2048]{1,0:T(8,128)(2,1)} %constant.112.clone.wh_ref) | copy-start | bytes 1572868
  90.2 19.7 %copy-start.9 = (f32[1,2048]{1,0:T(1,128)S(1)}, f32[1,2048]{1,0:T(1,128)}, u32[]{:S(2)}) copy-start(f32[1,2048]{1,0:T(1,128)} %constant.84.clone.last_ref) | copy-start | bytes 24580
  90.2 19.7 %copy-start.10 = (f32[32,128]{1,0:T(8,128)S(1)}, f32[32,128]{1,0:T(8,128)}, u32[]{:S(2)}) copy-start(f32[32,128]{1,0:T(8,128)} %constant.111.clone.basis_ref) | copy-start | bytes 49156
  90.2 19.7 %copy-start.11 = (f32[32,16]{1,0:T(8,128)S(1)}, f32[32,16]{1,0:T(8,128)}, u32[]{:S(2)}) copy-start(f32[32,16]{1,0:T(8,128)} %constant.110.clone.back_ref) | copy-start | bytes 6148

commit v7 on v6

--- a/solution.py
+++ b/solution.py
@@ -194,8 +194,8 @@
     return copies
 
 
-def front_body(mask_ref, basis_ref, lh_ref, ll_ref, last_ref, noise_ref, first_ref, second_ref, *scratch):
-    mask, basis, lh, ll, last, first, second, sems = scratch
+def front_body(mask_ref, basis_ref, lh_ref, ll_ref, last_ref, noise_ref, first, second_ref, *scratch):
+    mask, basis, lh, ll, last, second, sems = scratch
     tables = [
         pltpu.make_async_copy(source, target, sems.at[index])
         for index, (source, target) in enumerate(
@@ -206,10 +206,10 @@
     loads, stores = [], []
     for index in range(2 * PARTS):
         which, rows = index // PARTS, pl.ds(index % PARTS * part, part)
-        held, out_ref = (first, first_ref) if which == 0 else (second, second_ref)
-        there = held.at[rows, :, pl.ds(0, PERIOD)] if which == 0 else held.at[rows]
+        there = first.at[rows, :, pl.ds(0, PERIOD)] if which == 0 else second.at[rows]
         loads.append(pltpu.make_async_copy(noise_ref.at[which, rows], there, sems.at[5 + index]))
-        stores.append(pltpu.make_async_copy(held.at[rows], out_ref.at[rows], sems.at[5 + 2 * PARTS + index]))
+        if which == 1:
+            stores.append(pltpu.make_async_copy(there, second_ref.at[rows], sems.at[5 + PARTS + index]))
     for copy in tables + loads:
         copy.start()
     for copy in tables:
@@ -224,9 +224,11 @@
     packed = jnp.concatenate(split(jnp.where(row == RANK - 1, apart, line)), 0)
     for index in range(first.shape[0]):
         first[index, :, PERIOD:] = packed
-    for load, store in zip(loads, stores):
+    for load, store in zip(loads[PARTS:], stores):
         load.wait()
         store.start()
+    for load in loads[:PARTS]:
+        load.wait()
     for store in stores:
         store.wait()
 
@@ -521,15 +523,14 @@
     held = (mask_values, basis, *lines, last)
     moved_first, moved = call(
         front_body,
-        (pltpu.HBM((noise_count, ROWS, PERIOD + FREQ), BF), pltpu.HBM((noise_count, ROWS, PERIOD), BF)),
+        (pltpu.VMEM((noise_count, ROWS, PERIOD + FREQ), BF), pltpu.HBM((noise_count, ROWS, PERIOD), BF)),
         hbm(*held, far_noise),
         in_specs=[anywhere] * 6,
-        out_specs=(anywhere, anywhere),
+        out_specs=(pl.BlockSpec(memory_space=pltpu.VMEM), anywhere),
         scratch_shapes=[pltpu.VMEM(value.shape, value.dtype) for value in held]
         + [
-            pltpu.VMEM((noise_count, ROWS, PERIOD + FREQ), BF),
             pltpu.VMEM((noise_count, ROWS, PERIOD), BF),
-            pltpu.SemaphoreType.DMA((5 + 4 * PARTS,)),
+            pltpu.SemaphoreType.DMA((5 + 3 * PARTS,)),
         ],
     )
     place = jnp.stack([lax.axis_index(axis).astype(jnp.int32) for axis in ("kern", "noise", "tile")])

time: 111 us -> 111 us (level)
  no operation moved by 1% of the time
where the time goes in v7:
time: 111 us
  blocking collectives  52.8 us (48%)
  Pallas kernels  23.3 us (21%)
  starting transfers between devices  20.1 us (18%)
  waiting for transfers between devices  11.4 us (10%)
  local copies, waits for them, and re-layouts  2.57 us (2%)
    all_to_all x1, blocking collectives, body(): got = lax.all_to_all(moved_first, 'noise', 0, 0, tiled=True)  37.2 us
    pallas_call x7, Pallas kernels, call(): pl.pallas_call(body, out_shape=out_shape, compiler_params=params, **kw)  22.2 us
    all_to_all x1, blocking collectives, body(): back = lax.all_to_all(spread, ('kern', 'noise'), 0, 0, tiled=True)  15.6 us
    ppermute x9, waiting for transfers between devices, shifted(): lax.ppermute(value, 'kern', [(source, source ^ shift) for source in range...  11.4 us
    ppermute x9, starting transfers between devices, shifted(): lax.ppermute(value, 'kern', [(source, source ^ shift) for source in range...  10.3 us
    all_to_all x1, starting transfers between devices, body(): got_last = lax.all_to_all(moved, 'noise', 0, 0, tiled=True)  4.57 us
    ppermute x1, starting transfers between devices, body(): rows_other = lax.ppermute(rows, 'tile', swap)  2.63 us
    ppermute x1, starting transfers between devices, body(): grad_other = lax.ppermute(send, 'tile', swap)  2.57 us
  transfers between devices with their start and end apart: 12, of which 6 were waited for; matrix products, arithmetic and copies ran while one was open for 0% of the time, Pallas kernels for 11%

profile of v7, /device:TPU:1, one launch (start us, length us, event | category | flops | bytes accessed | tf_op | source)
XLA Modules:
  0.0 110.5 jit_solution(391397414773492229)
XLA Ops:
  0.0 0.1 pad_add_fusion._.place_ref
  0.1 3.6 %shard_map.370 = (bf16[16,32,2176]{2,1,0:T(8,128)(2,1)S(1)}, bf16[16,32,2048]{2,1,0:T(8,128)(2,1)}) custom-call(f32[32,2048]{1,0:T(8,128)} %mask_ref.1, f32[16,32]{1,0:T(8,128)} %constant.83.clone.basis_ref, bf16[2048,128]{1,0:T(8,128)(2,1)} %constant.81.clone.lh_ref, bf16[2048,128]{1,0:T(8,128)(2,1)} %constant.82.clone.ll_ref, ...), custom_call_target="tpu_custom_call" | custom-call | tf_op jit(solution)/shard_map/pallas_call | solution.py:169
  3.7 37.2 %all_to_all.15.got_ref.noise_ref.refs_1_ = bf16[16,32,2176]{2,1,0:T(8,128)(2,1)S(1)} all-to-all(bf16[16,32,2176]{2,1,0:T(8,128)(2,1)S(1)} %get-tuple-element.32), channel_id=1, replica_groups=mesh['tile'=2,'kern'=4,'noise'=16] {'noise'}, dimensions={0} | all-to-all | bytes 4456448 | tf_op jit(solution)/shard_map/all_to_all | solution.py:538
  40.8 0.0 copy-start
  40.8 0.0 copy-start.4
  40.8 0.0 copy-start.8
  40.8 4.6 %all-to-all-start.1 = ((bf16[16,32,2048]{2,1,0:T(8,128)(2,1)}), bf16[16,32,2048]{2,1,0:T(8,128)(2,1)}, u32[]{:S(2)}, u32[]{:S(2)}) async-start(bf16[16,32,2048]{2,1,0:T(8,128)(2,1)} %get-tuple-element.44), calls=%async_computation.1 | async-start | bytes 4194304 | tf_op jit(solution)/shard_map/all_to_all | solution.py:542
  45.4 0.0 copy-done
  45.4 0.0 copy-done.4
  45.4 0.0 copy-done.8
  45.4 0.0 copy-start.1
  45.4 1.2 %copy-done.1 = bf16[4,512,256]{2,1,0:T(8,128)(2,1)S(1)} copy-done((bf16[4,512,256]{2,1,0:T(8,128)(2,1)S(1)}, bf16[4,512,256]{2,1,0:T(8,128)(2,1)}, u32[]{:S(2)}) %copy-start.1) | copy-done | bytes 1048600
  46.7 0.0 copy-start.12
  46.7 1.1 %shard_map.371.refs_0_ = f32[256,128]{1,0:T(8,128)S(1)} custom-call(s32[3]{0:T(128)S(1)} %pad_add_fusion._.place_ref, bf16[16,32,2176]{2,1,0:T(8,128)(2,1)S(1)} %all_to_all.15.got_ref.noise_ref.refs_1_, bf16[4,512,256]{2,1,0:T(8,128)(2,1)S(1)} %copy-done.1, bf16[4,512,256]{2,1,0:T(8,128)(2,1)S(1)} %copy-done, bf16[128,256]{1,0:T(8,128)(2,1)S(1)} %copy-done.8, ...), custom_call_target="tpu_custom_call" | custom-call | tf_op jit(solution)/shard_map/pallas_call | solution.py:171
  47.8 0.0 copy-start.7
  47.8 0.0 copy-start.2
  47.8 0.0 copy-start.3
  47.8 3.2 %collective-permute-start.2 = (f32[256,128]{1,0:T(8,128)S(1)}, f32[256,128]{1,0:T(8,128)S(1)}, u32[]{:S(2)}, u32[]{:S(2)}) collective-permute-start(f32[256,128]{1,0:T(8,128)S(1)} %shard_map.371.refs_0_), channel_id=1, source_target_pairs={{0,48},{16,32},{32,16},{48,0},{1,49},{17,33},{33,17},{49,1},{2,50}... | collective-permute-start | bytes 393224 | tf_op jit(solution)/shard_map/ppermute | solution.py:496
  51.1 0.3 collective-permute-start.1
  51.3 0.2 collective-permute-start
  51.6 4.0 %collective-permute-done.2.refs_3_ = f32[256,128]{1,0:T(8,128)S(1)} collective-permute-done((f32[256,128]{1,0:T(8,128)S(1)}, f32[256,128]{1,0:T(8,128)S(1)}, u32[]{:S(2)}, u32[]{:S(2)}) %collective-permute-start.2) | collective-permute-done | bytes 131104 | tf_op jit(solution)/shard_map/ppermute | solution.py:496
  55.5 0.0 copy-start.13
  55.5 2.7 %collective-permute-done.1.refs_2_ = f32[256,128]{1,0:T(8,128)S(1)} collective-permute-done((f32[256,128]{1,0:T(8,128)S(1)}, f32[256,128]{1,0:T(8,128)S(1)}, u32[]{:S(2)}, u32[]{:S(2)}) %collective-permute-start.1) | collective-permute-done | bytes 131104 | tf_op jit(solution)/shard_map/ppermute | solution.py:496
  58.2 0.0 copy-start.14
  58.2 0.0 collective-permute-done.refs_1_
  58.2 0.0 copy-done.7
  58.2 0.0 copy-done.13
  58.3 0.6 copy-done.14
  58.9 0.0 copy-start.15
  58.9 0.7 copy-done.15
  59.5 0.0 copy-done.12
  59.5 4.4 %shard_map.372 = (f32[576,512]{1,0:T(8,128)}, f32[32,256]{1,0:T(8,128)S(1)}, f32[32,256]{1,0:T(8,128)S(1)}, f32[32,256]{1,0:T(8,128)S(1)}, f32[32,256]{1,0:T(8,128)S(1)}) custom-call(s32[3]{0:T(128)S(1)} %pad_add_fusion._.place_ref, f32[6]{0:T(128)S(1)} %copy-done.12, f32[256,128]{1,0:T(8,128)} %copy-done.7, f32[256,128]{1,0:T(8,128)} %copy-done.15, ...), custom_call_target="tpu_custom_call" | custom-call | tf_op jit(solution)/shard_map/pallas_call | solution.py:169
  64.0 0.4 collective-permute-start.3
  64.4 0.1 collective-permute-start.4
  64.5 1.7 %collective-permute-start.5 = (f32[32,256]{1,0:T(8,128)S(1)}, f32[32,256]{1,0:T(8,128)S(1)}, u32[]{:S(2)}, u32[]{:S(2)}) collective-permute-start(f32[32,256]{1,0:T(8,128)S(1)} %get-tuple-element.42), channel_id=1, source_target_pairs={{0,48},{16,32},{32,16},{48,0},{1,49},{17,33},{33,17},{49,1},{2,50}... | collective-permute-start | bytes 98312 | tf_op jit(solution)/shard_map/ppermute | solution.py:496
  66.2 0.0 collective-permute-done.3
  66.2 1.4 %collective-permute-done.4 = f32[32,256]{1,0:T(8,128)S(1)} collective-permute-done((f32[32,256]{1,0:T(8,128)S(1)}, f32[32,256]{1,0:T(8,128)S(1)}, u32[]{:S(2)}, u32[]{:S(2)}) %collective-permute-start.4) | collective-permute-done | bytes 32800 | tf_op jit(solution)/shard_map/ppermute | solution.py:496
  67.5 1.3 %collective-permute-done.5 = f32[32,256]{1,0:T(8,128)S(1)} collective-permute-done((f32[32,256]{1,0:T(8,128)S(1)}, f32[32,256]{1,0:T(8,128)S(1)}, u32[]{:S(2)}, u32[]{:S(2)}) %collective-permute-start.5) | collective-permute-done | bytes 32800 | tf_op jit(solution)/shard_map/ppermute | solution.py:496
  68.9 2.6 %collective-permute-start.6 = (f32[32,256]{1,0:T(8,128)S(1)}, f32[32,256]{1,0:T(8,128)S(1)}, u32[]{:S(2)}, u32[]{:S(2)}) collective-permute-start(f32[32,256]{1,0:T(8,128)S(1)} %add_add_fusion.rows_ref), channel_id=1, source_target_pairs={{0,64},{64,0},{1,65},{65,1},{2,66},{66,2},{3,67},{67,3},{4,68},{68... | collective-permute-start | bytes 98312 | tf_op jit(solution)/shard_map/ppermute | solution.py:586
  71.5 0.0 copy-done.2
  71.5 0.0 copy-done.3
  71.5 2.1 %shard_map.373.sums_ref = f32[4,32,2048]{2,1,0:T(8,128)S(1)} custom-call(f32[32,256]{1,0:T(8,128)S(1)} %add_add_fusion.rows_ref, bf16[256,2048]{1,0:T(8,128)(2,1)S(1)} %copy-done.3, bf16[256,2048]{1,0:T(8,128)(2,1)S(1)} %copy-done.2, bf16[16,32,2176]{2,1,0:T(8,128)(2,1)S(1)} %all_to_all.15.got_ref.noise_ref.refs_1_), custom_call_target="tpu_custom_call" | custom-call | tf_op jit(solution)/shard_map/pallas_call | solution.py:169
  73.7 0.0 collective-permute-done.6.other_ref
  73.7 0.0 all-to-all-done.1.refs_2_.noise_ref
  73.7 2.5 %shard_map.374 = (f32[32,256]{1,0:T(8,128)S(1)}, f32[32,256]{1,0:T(8,128)S(1)}) custom-call(s32[3]{0:T(128)S(1)} %pad_add_fusion._.place_ref, f32[4,32,2048]{2,1,0:T(8,128)S(1)} %shard_map.373.sums_ref, f32[32,256]{1,0:T(8,128)S(1)} %collective-permute-done.6.other_ref, bf16[32,2048]{1,0:T(8,128)(2,1)} %target_ref, ...), custom_call_target="tpu_custom_call" | custom-call | tf_op jit(solution)/shard_map/pallas_call | solution.py:169
  76.2 2.6 %collective-permute-start.7 = (f32[32,256]{1,0:T(8,128)S(1)}, f32[32,256]{1,0:T(8,128)S(1)}, u32[]{:S(2)}, u32[]{:S(2)}) collective-permute-start(f32[32,256]{1,0:T(8,128)S(1)} %get-tuple-element.48), channel_id=1, source_target_pairs={{0,64},{64,0},{1,65},{65,1},{2,66},{66,2},{3,67},{67,3},{4,68},{68... | collective-permute-start | bytes 98312 | tf_op jit(solution)/shard_map/ppermute | solution.py:615
  78.7 4.4 %shard_map.375 = (f32[32,256]{1,0:T(8,128)S(1)}, f32[576,512]{1,0:T(8,128)S(1)}, f32[6,2,128,128]{3,2,1,0:T(8,128)S(1)}, bf16[2,256,192]{2,1,0:T(8,128)(2,1)S(1)...) custom-call(s32[3]{0:T(128)S(1)} %pad_add_fusion._.place_ref, ...), custom_call_target="tpu_custom_call" | custom-call | tf_op jit(solution)/shard_map/pallas_call | solution.py:169
  83.2 0.0 collective-permute-done.7
  83.2 3.2 %collective-permute-start.10 = (f32[32,256]{1,0:T(8,128)S(1)}, f32[32,256]{1,0:T(8,128)S(1)}, u32[]{:S(2)}, u32[]{:S(2)}) collective-permute-start(f32[32,256]{1,0:T(8,128)S(1)} %add.15.refs_0_), channel_id=1, source_target_pairs={{0,48},{16,32},{32,16},{48,0},{1,49},{17,33},{33,17},{49,1},{2,50}... | collective-permute-start | bytes 98312 | tf_op jit(solution)/shard_map/ppermute | solution.py:496
  86.4 1.2 %collective-permute-start.9 = (f32[32,256]{1,0:T(8,128)S(1)}, f32[32,256]{1,0:T(8,128)S(1)}, u32[]{:S(2)}, u32[]{:S(2)}) collective-permute-start(f32[32,256]{1,0:T(8,128)S(1)} %add.15.refs_0_), channel_id=1, source_target_pairs={{0,32},{16,48},{32,0},{48,16},{1,33},{17,49},{33,1},{49,17},{2,34}... | collective-permute-start | bytes 98312 | tf_op jit(solution)/shard_map/ppermute | solution.py:496
  87.6 0.0 collective-permute-start.8
  87.6 0.4 collective-permute-done.10.refs_3_
  88.0 1.6 %collective-permute-done.9.refs_2_ = f32[32,256]{1,0:T(8,128)S(1)} collective-permute-done((f32[32,256]{1,0:T(8,128)S(1)}, f32[32,256]{1,0:T(8,128)S(1)}, u32[]{:S(2)}, u32[]{:S(2)}) %collective-permute-start.9) | collective-permute-done | bytes 32800 | tf_op jit(solution)/shard_map/ppermute | solution.py:496
  89.6 0.0 collective-permute-done.8.refs_1_
  89.6 0.0 copy-start.10
  89.6 0.0 copy-start.11
  89.6 4.0 %shard_map.376 = bf16[64,16,128]{2,1,0:T(8,128)(2,1)S(1)} custom-call(s32[3]{0:T(128)S(1)} %pad_add_fusion._.place_ref, f32[6]{0:T(128)S(1)} %copy-done.12, f32[32,256]{1,0:T(8,128)S(1)} %add.15.refs_0_, f32[32,256]{1,0:T(8,128)S(1)} %collective-permute-done.8.refs_1_, f32[32,256]{1,0:T(8,128)S(1)} %collective-permute-done.9.refs_2_, ...), custom_call_target="tpu_custom_call" | custom-call | tf_op jit(solution)/shard_map/pallas_call | solution.py:169
  93.7 15.6 %all_to_all.16.got_ref = bf16[64,16,128]{2,1,0:T(8,128)(2,1)S(1)} all-to-all(bf16[64,16,128]{2,1,0:T(8,128)(2,1)S(1)} %shard_map.376), channel_id=1, replica_groups=mesh['tile'=2,'kern'=4,'noise'=16] {'kern','noise'}, dimensions={0} | all-to-all | bytes 524288 | tf_op jit(solution)/shard_map/all_to_all | solution.py:652
  109.3 0.0 copy-done.5
  109.3 0.0 copy-done.6
  109.3 0.0 copy-done.9
  109.3 0.0 copy-done.10
  109.3 0.0 copy-done.11
  109.3 1.2 %shard_map.377 = f32[32,2048]{1,0:T(8,128)} custom-call(bf16[64,16,128]{2,1,0:T(8,128)(2,1)S(1)} %all_to_all.16.got_ref, f32[32,16]{1,0:T(8,128)S(1)} %copy-done.11, f32[32,128]{1,0:T(8,128)S(1)} %copy-done.10, bf16[128,2048]{1,0:T(8,128)(2,1)S(1)} %copy-done.6, bf16[128,2048]{1,0:T(8,128)(2,1)S(1)} %copy-done.5, f32[1,2048]{1,0:T(1,128)S(1)} %copy-done.9), custom_call_target="tpu_custom_call" | custom-call | tf_op jit(solution)/shard_map/pallas_call | solution.py:169
  (5 shorter events, 0.0 us)
Async XLA Ops:
  40.8 4.6 %copy-start = (bf16[4,512,256]{2,1,0:T(8,128)(2,1)S(1)}, bf16[4,512,256]{2,1,0:T(8,128)(2,1)}, u32[]{:S(2)}) copy-start(bf16[4,512,256]{2,1,0:T(8,128)(2,1)} %constant.87.clone.gl_ref) | copy-start | bytes 3145732
  40.8 4.6 %copy-start.4 = (f32[2,128,128]{2,1,0:T(8,128)S(1)}, f32[2,128,128]{2,1,0:T(8,128)}, u32[]{:S(2)}) copy-start(f32[2,128,128]{2,1,0:T(8,128)} %constant.85.clone.coef_ref.refs_10_) | copy-start | bytes 393220
  40.8 4.6 %copy-start.8 = (bf16[128,256]{1,0:T(8,128)(2,1)S(1)}, bf16[128,256]{1,0:T(8,128)(2,1)}, u32[]{:S(2)}) copy-start(bf16[128,256]{1,0:T(8,128)(2,1)} %constant.88.clone.unfold_ref) | copy-start | bytes 196612
  40.8 32.9 %all-to-all-start.1 = ((bf16[16,32,2048]{2,1,0:T(8,128)(2,1)}), bf16[16,32,2048]{2,1,0:T(8,128)(2,1)}, u32[]{:S(2)}, u32[]{:S(2)}) async-start(bf16[16,32,2048]{2,1,0:T(8,128)(2,1)} %get-tuple-element.44), calls=%async_computation.1 | async-start | bytes 4194304 | tf_op jit(solution)/shard_map/all_to_all | solution.py:542
  45.4 1.2 %copy-start.1 = (bf16[4,512,256]{2,1,0:T(8,128)(2,1)S(1)}, bf16[4,512,256]{2,1,0:T(8,128)(2,1)}, u32[]{:S(2)}) copy-start(bf16[4,512,256]{2,1,0:T(8,128)(2,1)} %constant.86.clone.gh_ref) | copy-start | bytes 3145732
  46.7 12.9 %copy-start.12 = (f32[6]{0:T(128)S(1)}, f32[6]{0:T(128)}, u32[]{:S(2)}) copy-start(f32[6]{0:T(128)} %weight_ref.1) | copy-start | bytes 76
  47.8 10.5 %copy-start.7 = (f32[256,128]{1,0:T(8,128)}, f32[256,128]{1,0:T(8,128)S(1)}, u32[]{:S(2)}) copy-start(f32[256,128]{1,0:T(8,128)S(1)} %shard_map.371.refs_0_) | copy-start | bytes 393220
  47.8 23.7 %copy-start.2 = (bf16[256,2048]{1,0:T(8,128)(2,1)S(1)}, bf16[256,2048]{1,0:T(8,128)(2,1)}, u32[]{:S(2)}) copy-start(bf16[256,2048]{1,0:T(8,128)(2,1)} %constant.95.clone.ol_ref) | copy-start | bytes 3145732
  47.8 23.7 %copy-start.3 = (bf16[256,2048]{1,0:T(8,128)(2,1)S(1)}, bf16[256,2048]{1,0:T(8,128)(2,1)}, u32[]{:S(2)}) copy-start(bf16[256,2048]{1,0:T(8,128)(2,1)} %constant.94.clone.oh_ref) | copy-start | bytes 3145732
  47.8 7.7 %collective-permute-start.2 = (f32[256,128]{1,0:T(8,128)S(1)}, f32[256,128]{1,0:T(8,128)S(1)}, u32[]{:S(2)}, u32[]{:S(2)}) collective-permute-start(f32[256,128]{1,0:T(8,128)S(1)} %shard_map.371.refs_0_), channel_id=1, source_target_pairs={{0,48},{16,32},{32,16},{48,0},{1,49},{17,33},{33,17},{49,1},{2,50}... | collective-permute-start | bytes 393224 | tf_op jit(solution)/shard_map/ppermute | solution.py:496
  51.1 7.2 %collective-permute-start.1 = (f32[256,128]{1,0:T(8,128)S(1)}, f32[256,128]{1,0:T(8,128)S(1)}, u32[]{:S(2)}, u32[]{:S(2)}) collective-permute-start(f32[256,128]{1,0:T(8,128)S(1)} %shard_map.371.refs_0_), channel_id=1, source_target_pairs={{0,32},{16,48},{32,0},{48,16},{1,33},{17,49},{33,1},{49,17},{2,34}... | collective-permute-start | bytes 393224 | tf_op jit(solution)/shard_map/ppermute | solution.py:496
  51.3 6.9 %collective-permute-start = (f32[256,128]{1,0:T(8,128)S(1)}, f32[256,128]{1,0:T(8,128)S(1)}, u32[]{:S(2)}, u32[]{:S(2)}) collective-permute-start(f32[256,128]{1,0:T(8,128)S(1)} %shard_map.371.refs_0_), channel_id=1, source_target_pairs={{0,16},{16,0},{32,48},{48,32},{1,17},{17,1},{33,49},{49,33},{2,18}... | collective-permute-start | bytes 393224 | tf_op jit(solution)/shard_map/ppermute | solution.py:496
  55.5 2.7 %copy-start.13 = (f32[256,128]{1,0:T(8,128)}, f32[256,128]{1,0:T(8,128)S(1)}, u32[]{:S(2)}) copy-start(f32[256,128]{1,0:T(8,128)S(1)} %collective-permute-done.2.refs_3_) | copy-start | bytes 393220
  58.2 0.7 copy-start.14
  58.9 0.7 copy-start.15
  64.0 2.2 %collective-permute-start.3 = (f32[32,256]{1,0:T(8,128)S(1)}, f32[32,256]{1,0:T(8,128)S(1)}, u32[]{:S(2)}, u32[]{:S(2)}) collective-permute-start(f32[32,256]{1,0:T(8,128)S(1)} %get-tuple-element.40), channel_id=1, source_target_pairs={{0,16},{16,0},{32,48},{48,32},{1,17},{17,1},{33,49},{49,33},{2,18}... | collective-permute-start | bytes 98312 | tf_op jit(solution)/shard_map/ppermute | solution.py:496
  64.4 3.2 %collective-permute-start.4 = (f32[32,256]{1,0:T(8,128)S(1)}, f32[32,256]{1,0:T(8,128)S(1)}, u32[]{:S(2)}, u32[]{:S(2)}) collective-permute-start(f32[32,256]{1,0:T(8,128)S(1)} %get-tuple-element.41), channel_id=1, source_target_pairs={{0,32},{16,48},{32,0},{48,16},{1,33},{17,49},{33,1},{49,17},{2,34}... | collective-permute-start | bytes 98312 | tf_op jit(solution)/shard_map/ppermute | solution.py:496
  64.5 4.4 %collective-permute-start.5 = (f32[32,256]{1,0:T(8,128)S(1)}, f32[32,256]{1,0:T(8,128)S(1)}, u32[]{:S(2)}, u32[]{:S(2)}) collective-permute-start(f32[32,256]{1,0:T(8,128)S(1)} %get-tuple-element.42), channel_id=1, source_target_pairs={{0,48},{16,32},{32,16},{48,0},{1,49},{17,33},{33,17},{49,1},{2,50}... | collective-permute-start | bytes 98312 | tf_op jit(solution)/shard_map/ppermute | solution.py:496
  68.9 4.8 %collective-permute-start.6 = (f32[32,256]{1,0:T(8,128)S(1)}, f32[32,256]{1,0:T(8,128)S(1)}, u32[]{:S(2)}, u32[]{:S(2)}) collective-permute-start(f32[32,256]{1,0:T(8,128)S(1)} %add_add_fusion.rows_ref), channel_id=1, source_target_pairs={{0,64},{64,0},{1,65},{65,1},{2,66},{66,2},{3,67},{67,3},{4,68},{68... | collective-permute-start | bytes 98312 | tf_op jit(solution)/shard_map/ppermute | solution.py:586
  76.2 7.0 %collective-permute-start.7 = (f32[32,256]{1,0:T(8,128)S(1)}, f32[32,256]{1,0:T(8,128)S(1)}, u32[]{:S(2)}, u32[]{:S(2)}) collective-permute-start(f32[32,256]{1,0:T(8,128)S(1)} %get-tuple-element.48), channel_id=1, source_target_pairs={{0,64},{64,0},{1,65},{65,1},{2,66},{66,2},{3,67},{67,3},{4,68},{68... | collective-permute-start | bytes 98312 | tf_op jit(solution)/shard_map/ppermute | solution.py:615
  83.2 4.8 %collective-permute-start.10 = (f32[32,256]{1,0:T(8,128)S(1)}, f32[32,256]{1,0:T(8,128)S(1)}, u32[]{:S(2)}, u32[]{:S(2)}) collective-permute-start(f32[32,256]{1,0:T(8,128)S(1)} %add.15.refs_0_), channel_id=1, source_target_pairs={{0,48},{16,32},{32,16},{48,0},{1,49},{17,33},{33,17},{49,1},{2,50}... | collective-permute-start | bytes 98312 | tf_op jit(solution)/shard_map/ppermute | solution.py:496
  86.4 3.2 %collective-permute-start.9 = (f32[32,256]{1,0:T(8,128)S(1)}, f32[32,256]{1,0:T(8,128)S(1)}, u32[]{:S(2)}, u32[]{:S(2)}) collective-permute-start(f32[32,256]{1,0:T(8,128)S(1)} %add.15.refs_0_), channel_id=1, source_target_pairs={{0,32},{16,48},{32,0},{48,16},{1,33},{17,49},{33,1},{49,17},{2,34}... | collective-permute-start | bytes 98312 | tf_op jit(solution)/shard_map/ppermute | solution.py:496
  87.6 2.0 %collective-permute-start.8 = (f32[32,256]{1,0:T(8,128)S(1)}, f32[32,256]{1,0:T(8,128)S(1)}, u32[]{:S(2)}, u32[]{:S(2)}) collective-permute-start(f32[32,256]{1,0:T(8,128)S(1)} %add.15.refs_0_), channel_id=1, source_target_pairs={{0,16},{16,0},{32,48},{48,32},{1,17},{17,1},{33,49},{49,33},{2,18}... | collective-permute-start | bytes 98312 | tf_op jit(solution)/shard_map/ppermute | solution.py:496
  89.6 19.7 %copy-start.5 = (bf16[128,2048]{1,0:T(8,128)(2,1)S(1)}, bf16[128,2048]{1,0:T(8,128)(2,1)}, u32[]{:S(2)}) copy-start(bf16[128,2048]{1,0:T(8,128)(2,1)} %constant.113.clone.wl_ref) | copy-start | bytes 1572868
  89.6 19.7 %copy-start.6 = (bf16[128,2048]{1,0:T(8,128)(2,1)S(1)}, bf16[128,2048]{1,0:T(8,128)(2,1)}, u32[]{:S(2)}) copy-start(bf16[128,2048]{1,0:T(8,128)(2,1)} %constant.112.clone.wh_ref) | copy-start | bytes 1572868
  89.6 19.7 %copy-start.9 = (f32[1,2048]{1,0:T(1,128)S(1)}, f32[1,2048]{1,0:T(1,128)}, u32[]{:S(2)}) copy-start(f32[1,2048]{1,0:T(1,128)} %constant.84.clone.last_ref) | copy-start | bytes 24580
  89.6 19.7 %copy-start.10 = (f32[32,128]{1,0:T(8,128)S(1)}, f32[32,128]{1,0:T(8,128)}, u32[]{:S(2)}) copy-start(f32[32,128]{1,0:T(8,128)} %constant.111.clone.basis_ref) | copy-start | bytes 49156
  89.6 19.7 %copy-start.11 = (f32[32,16]{1,0:T(8,128)S(1)}, f32[32,16]{1,0:T(8,128)}, u32[]{:S(2)}) copy-start(f32[32,16]{1,0:T(8,128)} %constant.110.clone.back_ref) | copy-start | bytes 6148

commit v8 on v7

--- a/solution.py
+++ b/solution.py
@@ -210,7 +210,7 @@
         loads.append(pltpu.make_async_copy(noise_ref.at[which, rows], there, sems.at[5 + index]))
         if which == 1:
             stores.append(pltpu.make_async_copy(there, second_ref.at[rows], sems.at[5 + PARTS + index]))
-    for copy in tables + loads:
+    for copy in tables + loads[PARTS:] + loads[:PARTS]:
         copy.start()
     for copy in tables:
         copy.wait()

time: 111 us -> 110 us (level)
  no operation moved by 1% of the time
where the time goes in v8:
time: 110 us
  blocking collectives  52.8 us (48%)
  Pallas kernels  23 us (21%)
  starting transfers between devices  20.1 us (18%)
  waiting for transfers between devices  11.4 us (10%)
  local copies, waits for them, and re-layouts  2.57 us (2%)
    all_to_all x1, blocking collectives, body(): got = lax.all_to_all(moved_first, 'noise', 0, 0, tiled=True)  37.1 us
    pallas_call x7, Pallas kernels, call(): pl.pallas_call(body, out_shape=out_shape, compiler_params=params, **kw)  21.9 us
    all_to_all x1, blocking collectives, body(): back = lax.all_to_all(spread, ('kern', 'noise'), 0, 0, tiled=True)  15.6 us
    ppermute x9, waiting for transfers between devices, shifted(): lax.ppermute(value, 'kern', [(source, source ^ shift) for source in range...  11.4 us
    ppermute x9, starting transfers between devices, shifted(): lax.ppermute(value, 'kern', [(source, source ^ shift) for source in range...  10.3 us
    all_to_all x1, starting transfers between devices, body(): got_last = lax.all_to_all(moved, 'noise', 0, 0, tiled=True)  4.57 us
    ppermute x1, starting transfers between devices, body(): rows_other = lax.ppermute(rows, 'tile', swap)  2.63 us
    ppermute x1, starting transfers between devices, body(): grad_other = lax.ppermute(send, 'tile', swap)  2.57 us
  transfers between devices with their start and end apart: 12, of which 6 were waited for; matrix products, arithmetic and copies ran while one was open for 0% of the time, Pallas kernels for 11%

profile of v8, /device:TPU:1, one launch (start us, length us, event | category | flops | bytes accessed | tf_op | source)
XLA Modules:
  0.0 110.2 jit_solution(8984771475287486733)
XLA Ops:
  0.0 0.1 pad_add_fusion._.place_ref
  0.1 3.2 %shard_map.370 = (bf16[16,32,2176]{2,1,0:T(8,128)(2,1)S(1)}, bf16[16,32,2048]{2,1,0:T(8,128)(2,1)}) custom-call(f32[32,2048]{1,0:T(8,128)} %mask_ref.1, f32[16,32]{1,0:T(8,128)} %constant.83.clone.basis_ref, bf16[2048,128]{1,0:T(8,128)(2,1)} %constant.81.clone.lh_ref, bf16[2048,128]{1,0:T(8,128)(2,1)} %constant.82.clone.ll_ref, ...), custom_call_target="tpu_custom_call" | custom-call | tf_op jit(solution)/shard_map/pallas_call | solution.py:169
  3.3 37.1 %all_to_all.15.got_ref.noise_ref.refs_1_ = bf16[16,32,2176]{2,1,0:T(8,128)(2,1)S(1)} all-to-all(bf16[16,32,2176]{2,1,0:T(8,128)(2,1)S(1)} %get-tuple-element.32), channel_id=1, replica_groups=mesh['tile'=2,'kern'=4,'noise'=16] {'noise'}, dimensions={0} | all-to-all | bytes 4456448 | tf_op jit(solution)/shard_map/all_to_all | solution.py:538
  40.5 0.0 copy-start
  40.5 0.0 copy-start.4
  40.5 0.0 copy-start.8
  40.5 4.6 %all-to-all-start.1 = ((bf16[16,32,2048]{2,1,0:T(8,128)(2,1)}), bf16[16,32,2048]{2,1,0:T(8,128)(2,1)}, u32[]{:S(2)}, u32[]{:S(2)}) async-start(bf16[16,32,2048]{2,1,0:T(8,128)(2,1)} %get-tuple-element.44), calls=%async_computation.1 | async-start | bytes 4194304 | tf_op jit(solution)/shard_map/all_to_all | solution.py:542
  45.0 0.0 copy-done
  45.0 0.0 copy-done.4
  45.1 0.0 copy-done.8
  45.1 0.0 copy-start.1
  45.1 1.2 %copy-done.1 = bf16[4,512,256]{2,1,0:T(8,128)(2,1)S(1)} copy-done((bf16[4,512,256]{2,1,0:T(8,128)(2,1)S(1)}, bf16[4,512,256]{2,1,0:T(8,128)(2,1)}, u32[]{:S(2)}) %copy-start.1) | copy-done | bytes 1048600
  46.3 0.0 copy-start.12
  46.3 1.1 %shard_map.371.refs_0_ = f32[256,128]{1,0:T(8,128)S(1)} custom-call(s32[3]{0:T(128)S(1)} %pad_add_fusion._.place_ref, bf16[16,32,2176]{2,1,0:T(8,128)(2,1)S(1)} %all_to_all.15.got_ref.noise_ref.refs_1_, bf16[4,512,256]{2,1,0:T(8,128)(2,1)S(1)} %copy-done.1, bf16[4,512,256]{2,1,0:T(8,128)(2,1)S(1)} %copy-done, bf16[128,256]{1,0:T(8,128)(2,1)S(1)} %copy-done.8, ...), custom_call_target="tpu_custom_call" | custom-call | tf_op jit(solution)/shard_map/pallas_call | solution.py:171
  47.4 0.0 copy-start.7
  47.4 0.0 copy-start.2
  47.4 0.0 copy-start.3
  47.5 3.3 %collective-permute-start.2 = (f32[256,128]{1,0:T(8,128)S(1)}, f32[256,128]{1,0:T(8,128)S(1)}, u32[]{:S(2)}, u32[]{:S(2)}) collective-permute-start(f32[256,128]{1,0:T(8,128)S(1)} %shard_map.371.refs_0_), channel_id=1, source_target_pairs={{0,48},{16,32},{32,16},{48,0},{1,49},{17,33},{33,17},{49,1},{2,50}... | collective-permute-start | bytes 393224 | tf_op jit(solution)/shard_map/ppermute | solution.py:496
  50.7 0.3 collective-permute-start.1
  51.0 0.2 collective-permute-start
  51.2 4.0 %collective-permute-done.2.refs_3_ = f32[256,128]{1,0:T(8,128)S(1)} collective-permute-done((f32[256,128]{1,0:T(8,128)S(1)}, f32[256,128]{1,0:T(8,128)S(1)}, u32[]{:S(2)}, u32[]{:S(2)}) %collective-permute-start.2) | collective-permute-done | bytes 131104 | tf_op jit(solution)/shard_map/ppermute | solution.py:496
  55.2 0.0 copy-start.13
  55.2 2.7 %collective-permute-done.1.refs_2_ = f32[256,128]{1,0:T(8,128)S(1)} collective-permute-done((f32[256,128]{1,0:T(8,128)S(1)}, f32[256,128]{1,0:T(8,128)S(1)}, u32[]{:S(2)}, u32[]{:S(2)}) %collective-permute-start.1) | collective-permute-done | bytes 131104 | tf_op jit(solution)/shard_map/ppermute | solution.py:496
  57.9 0.0 copy-start.14
  57.9 0.0 collective-permute-done.refs_1_
  57.9 0.0 copy-done.7
  57.9 0.0 copy-done.13
  57.9 0.6 copy-done.14
  58.5 0.0 copy-start.15
  58.5 0.7 copy-done.15
  59.2 0.0 copy-done.12
  59.2 4.4 %shard_map.372 = (f32[576,512]{1,0:T(8,128)}, f32[32,256]{1,0:T(8,128)S(1)}, f32[32,256]{1,0:T(8,128)S(1)}, f32[32,256]{1,0:T(8,128)S(1)}, f32[32,256]{1,0:T(8,128)S(1)}) custom-call(s32[3]{0:T(128)S(1)} %pad_add_fusion._.place_ref, f32[6]{0:T(128)S(1)} %copy-done.12, f32[256,128]{1,0:T(8,128)} %copy-done.7, f32[256,128]{1,0:T(8,128)} %copy-done.15, ...), custom_call_target="tpu_custom_call" | custom-call | tf_op jit(solution)/shard_map/pallas_call | solution.py:169
  63.6 0.4 collective-permute-start.3
  64.0 0.1 collective-permute-start.4
  64.1 1.7 %collective-permute-start.5 = (f32[32,256]{1,0:T(8,128)S(1)}, f32[32,256]{1,0:T(8,128)S(1)}, u32[]{:S(2)}, u32[]{:S(2)}) collective-permute-start(f32[32,256]{1,0:T(8,128)S(1)} %get-tuple-element.42), channel_id=1, source_target_pairs={{0,48},{16,32},{32,16},{48,0},{1,49},{17,33},{33,17},{49,1},{2,50}... | collective-permute-start | bytes 98312 | tf_op jit(solution)/shard_map/ppermute | solution.py:496
  65.8 0.0 collective-permute-done.3
  65.8 1.4 %collective-permute-done.4 = f32[32,256]{1,0:T(8,128)S(1)} collective-permute-done((f32[32,256]{1,0:T(8,128)S(1)}, f32[32,256]{1,0:T(8,128)S(1)}, u32[]{:S(2)}, u32[]{:S(2)}) %collective-permute-start.4) | collective-permute-done | bytes 32800 | tf_op jit(solution)/shard_map/ppermute | solution.py:496
  67.2 1.3 %collective-permute-done.5 = f32[32,256]{1,0:T(8,128)S(1)} collective-permute-done((f32[32,256]{1,0:T(8,128)S(1)}, f32[32,256]{1,0:T(8,128)S(1)}, u32[]{:S(2)}, u32[]{:S(2)}) %collective-permute-start.5) | collective-permute-done | bytes 32800 | tf_op jit(solution)/shard_map/ppermute | solution.py:496
  68.5 2.6 %collective-permute-start.6 = (f32[32,256]{1,0:T(8,128)S(1)}, f32[32,256]{1,0:T(8,128)S(1)}, u32[]{:S(2)}, u32[]{:S(2)}) collective-permute-start(f32[32,256]{1,0:T(8,128)S(1)} %add_add_fusion.rows_ref), channel_id=1, source_target_pairs={{0,64},{64,0},{1,65},{65,1},{2,66},{66,2},{3,67},{67,3},{4,68},{68... | collective-permute-start | bytes 98312 | tf_op jit(solution)/shard_map/ppermute | solution.py:586
  71.2 0.0 copy-done.2
  71.2 0.0 copy-done.3
  71.2 2.1 %shard_map.373.sums_ref = f32[4,32,2048]{2,1,0:T(8,128)S(1)} custom-call(f32[32,256]{1,0:T(8,128)S(1)} %add_add_fusion.rows_ref, bf16[256,2048]{1,0:T(8,128)(2,1)S(1)} %copy-done.3, bf16[256,2048]{1,0:T(8,128)(2,1)S(1)} %copy-done.2, bf16[16,32,2176]{2,1,0:T(8,128)(2,1)S(1)} %all_to_all.15.got_ref.noise_ref.refs_1_), custom_call_target="tpu_custom_call" | custom-call | tf_op jit(solution)/shard_map/pallas_call | solution.py:169
  73.3 0.0 collective-permute-done.6.other_ref
  73.3 0.0 all-to-all-done.1.refs_2_.noise_ref
  73.3 2.5 %shard_map.374 = (f32[32,256]{1,0:T(8,128)S(1)}, f32[32,256]{1,0:T(8,128)S(1)}) custom-call(s32[3]{0:T(128)S(1)} %pad_add_fusion._.place_ref, f32[4,32,2048]{2,1,0:T(8,128)S(1)} %shard_map.373.sums_ref, f32[32,256]{1,0:T(8,128)S(1)} %collective-permute-done.6.other_ref, bf16[32,2048]{1,0:T(8,128)(2,1)} %target_ref, ...), custom_call_target="tpu_custom_call" | custom-call | tf_op jit(solution)/shard_map/pallas_call | solution.py:169
  75.8 2.6 %collective-permute-start.7 = (f32[32,256]{1,0:T(8,128)S(1)}, f32[32,256]{1,0:T(8,128)S(1)}, u32[]{:S(2)}, u32[]{:S(2)}) collective-permute-start(f32[32,256]{1,0:T(8,128)S(1)} %get-tuple-element.48), channel_id=1, source_target_pairs={{0,64},{64,0},{1,65},{65,1},{2,66},{66,2},{3,67},{67,3},{4,68},{68... | collective-permute-start | bytes 98312 | tf_op jit(solution)/shard_map/ppermute | solution.py:615
  78.4 4.4 %shard_map.375 = (f32[32,256]{1,0:T(8,128)S(1)}, f32[576,512]{1,0:T(8,128)S(1)}, f32[6,2,128,128]{3,2,1,0:T(8,128)S(1)}, bf16[2,256,192]{2,1,0:T(8,128)(2,1)S(1)...) custom-call(s32[3]{0:T(128)S(1)} %pad_add_fusion._.place_ref, ...), custom_call_target="tpu_custom_call" | custom-call | tf_op jit(solution)/shard_map/pallas_call | solution.py:169
  82.8 0.0 collective-permute-done.7
  82.8 3.2 %collective-permute-start.10 = (f32[32,256]{1,0:T(8,128)S(1)}, f32[32,256]{1,0:T(8,128)S(1)}, u32[]{:S(2)}, u32[]{:S(2)}) collective-permute-start(f32[32,256]{1,0:T(8,128)S(1)} %add.15.refs_0_), channel_id=1, source_target_pairs={{0,48},{16,32},{32,16},{48,0},{1,49},{17,33},{33,17},{49,1},{2,50}... | collective-permute-start | bytes 98312 | tf_op jit(solution)/shard_map/ppermute | solution.py:496
  86.1 1.2 %collective-permute-start.9 = (f32[32,256]{1,0:T(8,128)S(1)}, f32[32,256]{1,0:T(8,128)S(1)}, u32[]{:S(2)}, u32[]{:S(2)}) collective-permute-start(f32[32,256]{1,0:T(8,128)S(1)} %add.15.refs_0_), channel_id=1, source_target_pairs={{0,32},{16,48},{32,0},{48,16},{1,33},{17,49},{33,1},{49,17},{2,34}... | collective-permute-start | bytes 98312 | tf_op jit(solution)/shard_map/ppermute | solution.py:496
  87.2 0.0 collective-permute-start.8
  87.2 0.4 collective-permute-done.10.refs_3_
  87.7 1.6 %collective-permute-done.9.refs_2_ = f32[32,256]{1,0:T(8,128)S(1)} collective-permute-done((f32[32,256]{1,0:T(8,128)S(1)}, f32[32,256]{1,0:T(8,128)S(1)}, u32[]{:S(2)}, u32[]{:S(2)}) %collective-permute-start.9) | collective-permute-done | bytes 32800 | tf_op jit(solution)/shard_map/ppermute | solution.py:496
  89.3 0.0 collective-permute-done.8.refs_1_
  89.3 0.0 copy-start.10
  89.3 0.0 copy-start.11
  89.3 4.0 %shard_map.376 = bf16[64,16,128]{2,1,0:T(8,128)(2,1)S(1)} custom-call(s32[3]{0:T(128)S(1)} %pad_add_fusion._.place_ref, f32[6]{0:T(128)S(1)} %copy-done.12, f32[32,256]{1,0:T(8,128)S(1)} %add.15.refs_0_, f32[32,256]{1,0:T(8,128)S(1)} %collective-permute-done.8.refs_1_, f32[32,256]{1,0:T(8,128)S(1)} %collective-permute-done.9.refs_2_, ...), custom_call_target="tpu_custom_call" | custom-call | tf_op jit(solution)/shard_map/pallas_call | solution.py:169
  93.3 15.6 %all_to_all.16.got_ref = bf16[64,16,128]{2,1,0:T(8,128)(2,1)S(1)} all-to-all(bf16[64,16,128]{2,1,0:T(8,128)(2,1)S(1)} %shard_map.376), channel_id=1, replica_groups=mesh['tile'=2,'kern'=4,'noise'=16] {'kern','noise'}, dimensions={0} | all-to-all | bytes 524288 | tf_op jit(solution)/shard_map/all_to_all | solution.py:652
  109.0 0.0 copy-done.5
  109.0 0.0 copy-done.6
  109.0 0.0 copy-done.9
  109.0 0.0 copy-done.10
  109.0 0.0 copy-done.11
  109.0 1.2 %shard_map.377 = f32[32,2048]{1,0:T(8,128)} custom-call(bf16[64,16,128]{2,1,0:T(8,128)(2,1)S(1)} %all_to_all.16.got_ref, f32[32,16]{1,0:T(8,128)S(1)} %copy-done.11, f32[32,128]{1,0:T(8,128)S(1)} %copy-done.10, bf16[128,2048]{1,0:T(8,128)(2,1)S(1)} %copy-done.6, bf16[128,2048]{1,0:T(8,128)(2,1)S(1)} %copy-done.5, f32[1,2048]{1,0:T(1,128)S(1)} %copy-done.9), custom_call_target="tpu_custom_call" | custom-call | tf_op jit(solution)/shard_map/pallas_call | solution.py:169
  (5 shorter events, 0.0 us)
Async XLA Ops:
  40.5 4.6 %copy-start = (bf16[4,512,256]{2,1,0:T(8,128)(2,1)S(1)}, bf16[4,512,256]{2,1,0:T(8,128)(2,1)}, u32[]{:S(2)}) copy-start(bf16[4,512,256]{2,1,0:T(8,128)(2,1)} %constant.87.clone.gl_ref) | copy-start | bytes 3145732
  40.5 4.6 %copy-start.4 = (f32[2,128,128]{2,1,0:T(8,128)S(1)}, f32[2,128,128]{2,1,0:T(8,128)}, u32[]{:S(2)}) copy-start(f32[2,128,128]{2,1,0:T(8,128)} %constant.85.clone.coef_ref.refs_10_) | copy-start | bytes 393220
  40.5 4.6 %copy-start.8 = (bf16[128,256]{1,0:T(8,128)(2,1)S(1)}, bf16[128,256]{1,0:T(8,128)(2,1)}, u32[]{:S(2)}) copy-start(bf16[128,256]{1,0:T(8,128)(2,1)} %constant.88.clone.unfold_ref) | copy-start | bytes 196612
  40.5 32.9 %all-to-all-start.1 = ((bf16[16,32,2048]{2,1,0:T(8,128)(2,1)}), bf16[16,32,2048]{2,1,0:T(8,128)(2,1)}, u32[]{:S(2)}, u32[]{:S(2)}) async-start(bf16[16,32,2048]{2,1,0:T(8,128)(2,1)} %get-tuple-element.44), calls=%async_computation.1 | async-start | bytes 4194304 | tf_op jit(solution)/shard_map/all_to_all | solution.py:542
  45.1 1.2 %copy-start.1 = (bf16[4,512,256]{2,1,0:T(8,128)(2,1)S(1)}, bf16[4,512,256]{2,1,0:T(8,128)(2,1)}, u32[]{:S(2)}) copy-start(bf16[4,512,256]{2,1,0:T(8,128)(2,1)} %constant.86.clone.gh_ref) | copy-start | bytes 3145732
  46.3 12.9 %copy-start.12 = (f32[6]{0:T(128)S(1)}, f32[6]{0:T(128)}, u32[]{:S(2)}) copy-start(f32[6]{0:T(128)} %weight_ref.1) | copy-start | bytes 76
  47.4 10.5 %copy-start.7 = (f32[256,128]{1,0:T(8,128)}, f32[256,128]{1,0:T(8,128)S(1)}, u32[]{:S(2)}) copy-start(f32[256,128]{1,0:T(8,128)S(1)} %shard_map.371.refs_0_) | copy-start | bytes 393220
  47.4 23.7 %copy-start.2 = (bf16[256,2048]{1,0:T(8,128)(2,1)S(1)}, bf16[256,2048]{1,0:T(8,128)(2,1)}, u32[]{:S(2)}) copy-start(bf16[256,2048]{1,0:T(8,128)(2,1)} %constant.95.clone.ol_ref) | copy-start | bytes 3145732
  47.4 23.7 %copy-start.3 = (bf16[256,2048]{1,0:T(8,128)(2,1)S(1)}, bf16[256,2048]{1,0:T(8,128)(2,1)}, u32[]{:S(2)}) copy-start(bf16[256,2048]{1,0:T(8,128)(2,1)} %constant.94.clone.oh_ref) | copy-start | bytes 3145732
  47.5 7.7 %collective-permute-start.2 = (f32[256,128]{1,0:T(8,128)S(1)}, f32[256,128]{1,0:T(8,128)S(1)}, u32[]{:S(2)}, u32[]{:S(2)}) collective-permute-start(f32[256,128]{1,0:T(8,128)S(1)} %shard_map.371.refs_0_), channel_id=1, source_target_pairs={{0,48},{16,32},{32,16},{48,0},{1,49},{17,33},{33,17},{49,1},{2,50}... | collective-permute-start | bytes 393224 | tf_op jit(solution)/shard_map/ppermute | solution.py:496
  50.7 7.2 %collective-permute-start.1 = (f32[256,128]{1,0:T(8,128)S(1)}, f32[256,128]{1,0:T(8,128)S(1)}, u32[]{:S(2)}, u32[]{:S(2)}) collective-permute-start(f32[256,128]{1,0:T(8,128)S(1)} %shard_map.371.refs_0_), channel_id=1, source_target_pairs={{0,32},{16,48},{32,0},{48,16},{1,33},{17,49},{33,1},{49,17},{2,34}... | collective-permute-start | bytes 393224 | tf_op jit(solution)/shard_map/ppermute | solution.py:496
  51.0 6.9 %collective-permute-start = (f32[256,128]{1,0:T(8,128)S(1)}, f32[256,128]{1,0:T(8,128)S(1)}, u32[]{:S(2)}, u32[]{:S(2)}) collective-permute-start(f32[256,128]{1,0:T(8,128)S(1)} %shard_map.371.refs_0_), channel_id=1, source_target_pairs={{0,16},{16,0},{32,48},{48,32},{1,17},{17,1},{33,49},{49,33},{2,18}... | collective-permute-start | bytes 393224 | tf_op jit(solution)/shard_map/ppermute | solution.py:496
  55.2 2.7 %copy-start.13 = (f32[256,128]{1,0:T(8,128)}, f32[256,128]{1,0:T(8,128)S(1)}, u32[]{:S(2)}) copy-start(f32[256,128]{1,0:T(8,128)S(1)} %collective-permute-done.2.refs_3_) | copy-start | bytes 393220
  57.9 0.7 copy-start.14
  58.5 0.7 copy-start.15
  63.6 2.2 %collective-permute-start.3 = (f32[32,256]{1,0:T(8,128)S(1)}, f32[32,256]{1,0:T(8,128)S(1)}, u32[]{:S(2)}, u32[]{:S(2)}) collective-permute-start(f32[32,256]{1,0:T(8,128)S(1)} %get-tuple-element.40), channel_id=1, source_target_pairs={{0,16},{16,0},{32,48},{48,32},{1,17},{17,1},{33,49},{49,33},{2,18}... | collective-permute-start | bytes 98312 | tf_op jit(solution)/shard_map/ppermute | solution.py:496
  64.0 3.2 %collective-permute-start.4 = (f32[32,256]{1,0:T(8,128)S(1)}, f32[32,256]{1,0:T(8,128)S(1)}, u32[]{:S(2)}, u32[]{:S(2)}) collective-permute-start(f32[32,256]{1,0:T(8,128)S(1)} %get-tuple-element.41), channel_id=1, source_target_pairs={{0,32},{16,48},{32,0},{48,16},{1,33},{17,49},{33,1},{49,17},{2,34}... | collective-permute-start | bytes 98312 | tf_op jit(solution)/shard_map/ppermute | solution.py:496
  64.1 4.4 %collective-permute-start.5 = (f32[32,256]{1,0:T(8,128)S(1)}, f32[32,256]{1,0:T(8,128)S(1)}, u32[]{:S(2)}, u32[]{:S(2)}) collective-permute-start(f32[32,256]{1,0:T(8,128)S(1)} %get-tuple-element.42), channel_id=1, source_target_pairs={{0,48},{16,32},{32,16},{48,0},{1,49},{17,33},{33,17},{49,1},{2,50}... | collective-permute-start | bytes 98312 | tf_op jit(solution)/shard_map/ppermute | solution.py:496
  68.5 4.8 %collective-permute-start.6 = (f32[32,256]{1,0:T(8,128)S(1)}, f32[32,256]{1,0:T(8,128)S(1)}, u32[]{:S(2)}, u32[]{:S(2)}) collective-permute-start(f32[32,256]{1,0:T(8,128)S(1)} %add_add_fusion.rows_ref), channel_id=1, source_target_pairs={{0,64},{64,0},{1,65},{65,1},{2,66},{66,2},{3,67},{67,3},{4,68},{68... | collective-permute-start | bytes 98312 | tf_op jit(solution)/shard_map/ppermute | solution.py:586
  75.8 7.0 %collective-permute-start.7 = (f32[32,256]{1,0:T(8,128)S(1)}, f32[32,256]{1,0:T(8,128)S(1)}, u32[]{:S(2)}, u32[]{:S(2)}) collective-permute-start(f32[32,256]{1,0:T(8,128)S(1)} %get-tuple-element.48), channel_id=1, source_target_pairs={{0,64},{64,0},{1,65},{65,1},{2,66},{66,2},{3,67},{67,3},{4,68},{68... | collective-permute-start | bytes 98312 | tf_op jit(solution)/shard_map/ppermute | solution.py:615
  82.8 4.8 %collective-permute-start.10 = (f32[32,256]{1,0:T(8,128)S(1)}, f32[32,256]{1,0:T(8,128)S(1)}, u32[]{:S(2)}, u32[]{:S(2)}) collective-permute-start(f32[32,256]{1,0:T(8,128)S(1)} %add.15.refs_0_), channel_id=1, source_target_pairs={{0,48},{16,32},{32,16},{48,0},{1,49},{17,33},{33,17},{49,1},{2,50}... | collective-permute-start | bytes 98312 | tf_op jit(solution)/shard_map/ppermute | solution.py:496
  86.1 3.2 %collective-permute-start.9 = (f32[32,256]{1,0:T(8,128)S(1)}, f32[32,256]{1,0:T(8,128)S(1)}, u32[]{:S(2)}, u32[]{:S(2)}) collective-permute-start(f32[32,256]{1,0:T(8,128)S(1)} %add.15.refs_0_), channel_id=1, source_target_pairs={{0,32},{16,48},{32,0},{48,16},{1,33},{17,49},{33,1},{49,17},{2,34}... | collective-permute-start | bytes 98312 | tf_op jit(solution)/shard_map/ppermute | solution.py:496
  87.2 2.0 %collective-permute-start.8 = (f32[32,256]{1,0:T(8,128)S(1)}, f32[32,256]{1,0:T(8,128)S(1)}, u32[]{:S(2)}, u32[]{:S(2)}) collective-permute-start(f32[32,256]{1,0:T(8,128)S(1)} %add.15.refs_0_), channel_id=1, source_target_pairs={{0,16},{16,0},{32,48},{48,32},{1,17},{17,1},{33,49},{49,33},{2,18}... | collective-permute-start | bytes 98312 | tf_op jit(solution)/shard_map/ppermute | solution.py:496
  89.3 19.7 %copy-start.5 = (bf16[128,2048]{1,0:T(8,128)(2,1)S(1)}, bf16[128,2048]{1,0:T(8,128)(2,1)}, u32[]{:S(2)}) copy-start(bf16[128,2048]{1,0:T(8,128)(2,1)} %constant.113.clone.wl_ref) | copy-start | bytes 1572868
  89.3 19.7 %copy-start.6 = (bf16[128,2048]{1,0:T(8,128)(2,1)S(1)}, bf16[128,2048]{1,0:T(8,128)(2,1)}, u32[]{:S(2)}) copy-start(bf16[128,2048]{1,0:T(8,128)(2,1)} %constant.112.clone.wh_ref) | copy-start | bytes 1572868
  89.3 19.7 %copy-start.9 = (f32[1,2048]{1,0:T(1,128)S(1)}, f32[1,2048]{1,0:T(1,128)}, u32[]{:S(2)}) copy-start(f32[1,2048]{1,0:T(1,128)} %constant.84.clone.last_ref) | copy-start | bytes 24580
  89.3 19.7 %copy-start.10 = (f32[32,128]{1,0:T(8,128)S(1)}, f32[32,128]{1,0:T(8,128)}, u32[]{:S(2)}) copy-start(f32[32,128]{1,0:T(8,128)} %constant.111.clone.basis_ref) | copy-start | bytes 49156
  89.3 19.7 %copy-start.11 = (f32[32,16]{1,0:T(8,128)S(1)}, f32[32,16]{1,0:T(8,128)}, u32[]{:S(2)}) copy-start(f32[32,16]{1,0:T(8,128)} %constant.110.clone.back_ref) | copy-start | bytes 6148
